TPU v7x, 32 devices: a whole 2x2x4 slice. The times are simulated.
32 devices in a mesh: aper: 8 (over y, x, core), shot: 4 (over z).
Axes of the slice: x: 2, y: 2, z: 4, core: 2. Of those that a mesh axis runs over, the one named last changes fastest.
Arguments:
- wavefield: float32 [4, 9, 32, 128, 128], P('shot', None, 'aper'), may hold values from -6 to 6
- lame_lambda: float32 [32, 128, 128], P('aper', 'shot'), may hold values from 0.5 to 2
- lame_mu: float32 [32, 128, 128], P('aper', 'shot'), may hold values from 0.3 to 1
- buoyancy: float32 [32, 128, 128], P('aper', 'shot'), may hold values from 0.4 to 1
- quality: float32 [32, 128, 128], P('aper', 'shot'), may hold values from 0.05 to 2
- active: int32 [4, 8, 4, 4], replicated, may hold values 0 or 1
Outputs:
- final_field: float32 [4, 9, 32, 128, 128], P('shot', None, 'aper')
All inputs are finite; a program needn't handle non-finite values.
Results may differ from a plain program's by a relative error of at most 0.00002.
Values sent between devices are 32-bit elements; how exact they have to be, the bound alone decides.
No kernel may reach another device: no remote copies, remote signals or barrier semaphores. Data moves between devices by JAX's collectives and lax.ppermute only.
A program may use at most 64 MiB of HBM per device.

v0:
```python
import jax
import jax.numpy as jnp
from jax import lax
from jax.sharding import PartitionSpec as P

BLK = 32
STEPS = 4


COEF_NEAR = 1.125
COEF_FAR = -1.0 / 24.0
TIME_STEP = 0.2


def extended(shard, sides, width):
    for axis, dim in sides:
        devices, length = (lax.axis_size(axis), shard.shape[dim])
        up = [(i, (i + 1) % devices) for i in range(devices - 1)]
        down = [(j, i) for i, j in up]
        last = lax.slice_in_dim(shard, length - width, length, axis=dim)
        initial = lax.slice_in_dim(shard, 0, width, axis=dim)
        before = lax.ppermute(last, axis, up)
        after = lax.ppermute(initial, axis, down)
        shard = jnp.concatenate([before, shard, after], axis=dim)
    return shard


def forward_rows(values, offset, length):
    return COEF_NEAR * (
        values[offset + 1 : offset + 1 + length] - values[offset : offset + length]
    ) + COEF_FAR * (
        values[offset + 2 : offset + 2 + length] - values[offset - 1 : offset - 1 + length]
    )


def backward_rows(values, offset, length):
    return COEF_NEAR * (
        values[offset : offset + length] - values[offset - 1 : offset - 1 + length]
    ) + COEF_FAR * (
        values[offset + 1 : offset + 1 + length] - values[offset - 2 : offset - 2 + length]
    )


def shifted(values, along, amount):
    widths = [(0, 0)] * values.ndim
    widths[along] = (2, 2)
    padded = jnp.pad(values, widths)
    return lax.slice_in_dim(padded, 2 + amount, 2 + amount + values.shape[along], axis=along)


def forward_axis(values, along):
    return COEF_NEAR * (shifted(values, along, 1) - values) + COEF_FAR * (
        shifted(values, along, 2) - shifted(values, along, -1)
    )


def backward_axis(values, along):
    return COEF_NEAR * (values - shifted(values, along, -1)) + COEF_FAR * (
        shifted(values, along, 1) - shifted(values, along, -2)
    )


def velocity_update(previous, stress, offset, length, buoyancy, damping, active_cells):

    def pick_rows(values):
        return values[offset : offset + length]

    grad_first = (
        forward_rows(stress[0], offset, length)
        + backward_axis(pick_rows(stress[3]), 1)
        + backward_axis(pick_rows(stress[4]), 2)
    )
    grad_second = (
        backward_rows(stress[3], offset, length)
        + forward_axis(pick_rows(stress[1]), 1)
        + backward_axis(pick_rows(stress[5]), 2)
    )
    grad_third = (
        backward_rows(stress[4], offset, length)
        + backward_axis(pick_rows(stress[5]), 1)
        + forward_axis(pick_rows(stress[2]), 2)
    )
    forcing = jnp.stack([grad_first, grad_second, grad_third])
    return previous + active_cells * (
        damping * (previous + TIME_STEP * buoyancy * forcing) - previous
    )


def stress_update(previous, velocity, offset, length, lambda_field, shear, damping, active_cells):

    def pick_rows(values):
        return values[offset : offset + length]

    strain_first = backward_rows(velocity[0], offset, length)
    strain_second = backward_axis(pick_rows(velocity[1]), 1)
    strain_third = backward_axis(pick_rows(velocity[2]), 2)
    dilation = strain_first + strain_second + strain_third
    shear_xy = forward_axis(pick_rows(velocity[0]), 1) + forward_rows(velocity[1], offset, length)
    shear_xz = forward_axis(pick_rows(velocity[0]), 2) + forward_rows(velocity[2], offset, length)
    shear_yz = forward_axis(pick_rows(velocity[1]), 2) + forward_axis(pick_rows(velocity[2]), 1)
    rates = jnp.stack(
        [
            lambda_field * dilation + 2.0 * shear * strain_first,
            lambda_field * dilation + 2.0 * shear * strain_second,
            lambda_field * dilation + 2.0 * shear * strain_third,
            shear * shear_xy,
            shear * shear_xz,
            shear * shear_yz,
        ]
    )
    return previous + active_cells * (damping * (previous + TIME_STEP * rates) - previous)


def upsample(blocks):
    return jnp.repeat(jnp.repeat(blocks, BLK, axis=1), BLK, axis=2)


def per_device(wavefield, lame_lambda, lame_mu, buoyancy, quality, active):
    panels = (
        lax.all_gather(lame_lambda, "shot", axis=1, tiled=True),
        lax.all_gather(lame_mu, "shot", axis=1, tiled=True),
        lax.all_gather(buoyancy, "shot", axis=1, tiled=True),
        lax.all_gather(quality, "shot", axis=1, tiled=True),
    )
    model = jnp.stack(panels)
    values = wavefield[0]
    slab_rows = values.shape[1]
    device = lax.axis_index("aper")
    damping = jnp.exp(-TIME_STEP * model[3])
    for moment in range(STEPS):
        blocks = lax.dynamic_index_in_dim(
            active[moment].astype(jnp.float32), device, 0, keepdims=True
        )
        active_cells = upsample(blocks)
        stress_pad = extended(values[3:], (("aper", 1),), 2)
        velocity = velocity_update(
            values[:3], stress_pad, 2, slab_rows, model[2], damping, active_cells
        )
        velocity_pad = extended(velocity, (("aper", 1),), 2)
        stress = stress_update(
            values[3:], velocity_pad, 2, slab_rows, model[0], model[1], damping, active_cells
        )
        values = jnp.concatenate([velocity, stress], axis=0)
    return values[None]


def solution(mesh):
    return jax.shard_map(
        per_device,
        mesh=mesh,
        in_specs=(
            P("shot", None, "aper", None, None),
            P("aper", "shot", None),
            P("aper", "shot", None),
            P("aper", "shot", None),
            P("aper", "shot", None),
            P(),
        ),
        out_specs=P("shot", None, "aper", None, None),
        check_vma=False,
    )
```

profile of v0, /device:TPU:3, one launch (start us, length us, event | category | flops | bytes accessed | tf_op | source)
XLA Modules:
  0.0 212.2 jit_solution(7834022111282499080)
XLA Ops:
  2.8 2.6 %collective-permute-start = (f32[6,2,128,128]{3,2,1,0:T(8,128)}, f32[6,2,128,128]{3,2,1,0:T(8,128)S(1)}, u32[]{:S(2)}, u32[]{:S(2)}) collective-permute-start(f32[6,2,128,128]{3,2,1,0:T(8,128)} %get-tuple-element.47), channel_id=1, source_target_pairs={{4,0},{8,4},{12,8},{16,12},{20,16},{24,20},{28,24},{5,1},{9,5},{13... | collective-permute-start | bytes 2359304 | tf_op jit(solution)/shard_map/ppermute | solution.py:23
  5.4 3.9 %collective-permute-start.1 = (f32[6,2,128,128]{3,2,1,0:T(8,128)}, f32[6,2,128,128]{3,2,1,0:T(8,128)}, u32[]{:S(2)}, u32[]{:S(2)}) collective-permute-start(f32[6,2,128,128]{3,2,1,0:T(8,128)} %get-tuple-element.48), channel_id=1, source_target_pairs={{0,4},{4,8},{8,12},{12,16},{16,20},{20,24},{24,28},{1,5},{5,9},{9,... | collective-permute-start | bytes 2359304 | tf_op jit(solution)/shard_map/ppermute | solution.py:22
  9.9 12.1 %all_gather.12 = f32[4,128,128]{2,1,0:T(8,128)S(1)} all-gather(f32[4,32,128]{2,1,0:T(8,128)S(1)} %copy-done.41), channel_id=1, replica_groups=mesh['aper'=8,'shot'=4] {'shot'}, dimensions={1}, use_global_device_ids=true | all-gather | bytes 327680 | tf_op jit(solution)/shard_map/all_gather | solution.py:123
  22.0 12.4 %all_gather.13 = f32[4,128,128]{2,1,0:T(8,128)S(1)} all-gather(f32[4,32,128]{2,1,0:T(8,128)S(1)} %copy-done.42), channel_id=1, replica_groups=mesh['aper'=8,'shot'=4] {'shot'}, dimensions={1}, use_global_device_ids=true | all-gather | bytes 327680 | tf_op jit(solution)/shard_map/all_gather | solution.py:122
  34.9 1.6 slice_bitcast_fusion.32
  41.7 5.8 %collective-permute-start.2 = (f32[3,2,128,128]{3,2,1,0:T(8,128)S(1)}, f32[3,2,128,128]{3,2,1,0:T(8,128)S(1)}, u32[]{:S(2)}, u32[]{:S(2)}) collective-permute-start(f32[3,2,128,128]{3,2,1,0:T(8,128)S(1)} %get-tuple-element.67), channel_id=1, source_target_pairs={{0,4},{4,8},{8,12},{12,16},{16,20},{20,24},{24,28},{1,5},{5,9},{9,... | collective-permute-start | bytes 1179656 | tf_op jit(solution)/shard_map/ppermute | solution.py:22
  47.5 1.9 collective-permute-start.3
  49.4 12.0 %all_gather.15 = f32[4,128,128]{2,1,0:T(8,128)S(1)} all-gather(f32[4,32,128]{2,1,0:T(8,128)S(1)} %copy-done.43), channel_id=1, replica_groups=mesh['aper'=8,'shot'=4] {'shot'}, dimensions={1}, use_global_device_ids=true | all-gather | bytes 327680 | tf_op jit(solution)/shard_map/all_gather | solution.py:121
  61.4 10.9 %all_gather.14 = f32[4,128,128]{2,1,0:T(8,128)S(1)} all-gather(f32[4,32,128]{2,1,0:T(8,128)S(1)} %copy-done.44), channel_id=1, replica_groups=mesh['aper'=8,'shot'=4] {'shot'}, dimensions={1}, use_global_device_ids=true | all-gather | bytes 327680 | tf_op jit(solution)/shard_map/all_gather | solution.py:120
  75.5 8.4 %collective-permute-start.4 = (f32[6,2,128,128]{3,2,1,0:T(8,128)}, f32[6,2,128,128]{3,2,1,0:T(8,128)S(1)}, u32[]{:S(2)}, u32[]{:S(2)}) collective-permute-start(f32[6,2,128,128]{3,2,1,0:T(8,128)} %get-tuple-element.45), channel_id=1, source_target_pairs={{4,0},{8,4},{12,8},{16,12},{20,16},{24,20},{28,24},{5,1},{9,5},{13... | collective-permute-start | bytes 2359304 | tf_op jit(solution)/shard_map/ppermute | solution.py:23
  84.0 3.2 %collective-permute-start.5 = (f32[6,2,128,128]{3,2,1,0:T(8,128)}, f32[6,2,128,128]{3,2,1,0:T(8,128)}, u32[]{:S(2)}, u32[]{:S(2)}) collective-permute-start(f32[6,2,128,128]{3,2,1,0:T(8,128)} %get-tuple-element.46), channel_id=1, source_target_pairs={{0,4},{4,8},{8,12},{12,16},{16,20},{20,24},{24,28},{1,5},{5,9},{9,... | collective-permute-start | bytes 2359304 | tf_op jit(solution)/shard_map/ppermute | solution.py:22
  89.1 12.6 %collective-permute-done.4 = f32[6,2,128,128]{3,2,1,0:T(8,128)S(1)} collective-permute-done((f32[6,2,128,128]{3,2,1,0:T(8,128)}, f32[6,2,128,128]{3,2,1,0:T(8,128)S(1)}, u32[]{:S(2)}, u32[]{:S(2)}) %collective-permute-start.4) | collective-permute-done | bytes 786464 | tf_op jit(solution)/shard_map/ppermute | solution.py:23
  107.4 5.3 %collective-permute-start.6 = (f32[3,2,128,128]{3,2,1,0:T(8,128)S(1)}, f32[3,2,128,128]{3,2,1,0:T(8,128)S(1)}, u32[]{:S(2)}, u32[]{:S(2)}) collective-permute-start(f32[3,2,128,128]{3,2,1,0:T(8,128)S(1)} %get-tuple-element.62), channel_id=1, source_target_pairs={{0,4},{4,8},{8,12},{12,16},{16,20},{20,24},{24,28},{1,5},{5,9},{9,... | collective-permute-start | bytes 1179656 | tf_op jit(solution)/shard_map/ppermute | solution.py:22
  112.7 1.9 collective-permute-start.7
  114.7 6.2 %collective-permute-done.6 = f32[3,2,128,128]{3,2,1,0:T(8,128)S(1)} collective-permute-done((f32[3,2,128,128]{3,2,1,0:T(8,128)S(1)}, f32[3,2,128,128]{3,2,1,0:T(8,128)S(1)}, u32[]{:S(2)}, u32[]{:S(2)}) %collective-permute-start.6) | collective-permute-done | bytes 393248 | tf_op jit(solution)/shard_map/ppermute | solution.py:22
  120.9 1.8 collective-permute-done.7
  125.9 1.9 collective-permute-start.8
  127.8 4.5 %collective-permute-start.9 = (f32[6,2,128,128]{3,2,1,0:T(8,128)}, f32[6,2,128,128]{3,2,1,0:T(8,128)S(1)}, u32[]{:S(2)}, u32[]{:S(2)}) collective-permute-start(f32[6,2,128,128]{3,2,1,0:T(8,128)} %get-tuple-element.39), channel_id=1, source_target_pairs={{0,4},{4,8},{8,12},{12,16},{16,20},{20,24},{24,28},{1,5},{5,9},{9,... | collective-permute-start | bytes 2359304 | tf_op jit(solution)/shard_map/ppermute | solution.py:22
  137.5 10.6 %collective-permute-done.8 = f32[6,2,128,128]{3,2,1,0:T(8,128)S(1)} collective-permute-done((f32[6,2,128,128]{3,2,1,0:T(8,128)}, f32[6,2,128,128]{3,2,1,0:T(8,128)S(1)}, u32[]{:S(2)}, u32[]{:S(2)}) %collective-permute-start.8) | collective-permute-done | bytes 786464 | tf_op jit(solution)/shard_map/ppermute | solution.py:23
  150.3 1.7 fusion.14
  152.1 2.4 %collective-permute-start.10 = (f32[3,2,128,128]{3,2,1,0:T(8,128)S(1)}, f32[3,2,128,128]{3,2,1,0:T(8,128)S(1)}, u32[]{:S(2)}, u32[]{:S(2)}) collective-permute-start(f32[3,2,128,128]{3,2,1,0:T(8,128)S(1)} %get-tuple-element.57), channel_id=1, source_target_pairs={{0,4},{4,8},{8,12},{12,16},{16,20},{20,24},{24,28},{1,5},{5,9},{9,... | collective-permute-start | bytes 1179656 | tf_op jit(solution)/shard_map/ppermute | solution.py:22
  154.5 1.9 collective-permute-start.11
  156.5 4.7 %collective-permute-done.10 = f32[3,2,128,128]{3,2,1,0:T(8,128)S(1)} collective-permute-done((f32[3,2,128,128]{3,2,1,0:T(8,128)S(1)}, f32[3,2,128,128]{3,2,1,0:T(8,128)S(1)}, u32[]{:S(2)}, u32[]{:S(2)}) %collective-permute-start.10) | collective-permute-done | bytes 393248 | tf_op jit(solution)/shard_map/ppermute | solution.py:22
  161.2 4.8 %collective-permute-done.11 = f32[3,2,128,128]{3,2,1,0:T(8,128)S(1)} collective-permute-done((f32[3,2,128,128]{3,2,1,0:T(8,128)S(1)}, f32[3,2,128,128]{3,2,1,0:T(8,128)S(1)}, u32[]{:S(2)}, u32[]{:S(2)}) %collective-permute-start.11) | collective-permute-done | bytes 393248 | tf_op jit(solution)/shard_map/ppermute | solution.py:23
  168.8 1.9 collective-permute-start.12
  170.7 4.7 %collective-permute-start.13 = (f32[6,2,128,128]{3,2,1,0:T(8,128)}, f32[6,2,128,128]{3,2,1,0:T(8,128)S(1)}, u32[]{:S(2)}, u32[]{:S(2)}) collective-permute-start(f32[6,2,128,128]{3,2,1,0:T(8,128)} %get-tuple-element.32), channel_id=1, source_target_pairs={{0,4},{4,8},{8,12},{12,16},{16,20},{20,24},{24,28},{1,5},{5,9},{9,... | collective-permute-start | bytes 2359304 | tf_op jit(solution)/shard_map/ppermute | solution.py:22
  179.2 12.0 %collective-permute-done.12 = f32[6,2,128,128]{3,2,1,0:T(8,128)S(1)} collective-permute-done((f32[6,2,128,128]{3,2,1,0:T(8,128)}, f32[6,2,128,128]{3,2,1,0:T(8,128)S(1)}, u32[]{:S(2)}, u32[]{:S(2)}) %collective-permute-start.12) | collective-permute-done | bytes 786464 | tf_op jit(solution)/shard_map/ppermute | solution.py:23
  193.6 1.8 fusion.19
  195.4 2.2 %collective-permute-start.14 = (f32[3,2,128,128]{3,2,1,0:T(8,128)S(1)}, f32[3,2,128,128]{3,2,1,0:T(8,128)S(1)}, u32[]{:S(2)}, u32[]{:S(2)}) collective-permute-start(f32[3,2,128,128]{3,2,1,0:T(8,128)S(1)} %get-tuple-element.52), channel_id=1, source_target_pairs={{0,4},{4,8},{8,12},{12,16},{16,20},{20,24},{24,28},{1,5},{5,9},{9,... | collective-permute-start | bytes 1179656 | tf_op jit(solution)/shard_map/ppermute | solution.py:22
  197.6 2.1 collective-permute-start.15
  199.8 4.3 %collective-permute-done.14 = f32[3,2,128,128]{3,2,1,0:T(8,128)S(1)} collective-permute-done((f32[3,2,128,128]{3,2,1,0:T(8,128)S(1)}, f32[3,2,128,128]{3,2,1,0:T(8,128)S(1)}, u32[]{:S(2)}, u32[]{:S(2)}) %collective-permute-start.14) | collective-permute-done | bytes 393248 | tf_op jit(solution)/shard_map/ppermute | solution.py:22
  204.1 5.0 %collective-permute-done.15 = f32[3,2,128,128]{3,2,1,0:T(8,128)S(1)} collective-permute-done((f32[3,2,128,128]{3,2,1,0:T(8,128)S(1)}, f32[3,2,128,128]{3,2,1,0:T(8,128)S(1)}, u32[]{:S(2)}, u32[]{:S(2)}) %collective-permute-start.15) | collective-permute-done | bytes 393248 | tf_op jit(solution)/shard_map/ppermute | solution.py:23
  (187 shorter events, 42.0 us)
Async XLA Ops:
  1.5 7.8 %copy-start.45 = (s32[4,8,4,4]{1,3,2,0:T(4,128)S(1)}, s32[4,8,4,4]{1,3,2,0:T(4,128)}, u32[]{:S(2)}) copy-start(s32[4,8,4,4]{1,3,2,0:T(4,128)} %param.11) | copy-start | bytes 6148
  1.5 8.4 %copy-start.41 = (f32[4,32,128]{2,1,0:T(8,128)S(1)}, f32[4,32,128]{2,1,0:T(8,128)}, u32[]{:S(2)}) copy-start(f32[4,32,128]{2,1,0:T(8,128)} %param.10) | copy-start | bytes 196612
  1.5 20.5 %copy-start.42 = (f32[4,32,128]{2,1,0:T(8,128)S(1)}, f32[4,32,128]{2,1,0:T(8,128)}, u32[]{:S(2)}) copy-start(f32[4,32,128]{2,1,0:T(8,128)} %param.9) | copy-start | bytes 196612
  2.8 33.7 %collective-permute-start = (f32[6,2,128,128]{3,2,1,0:T(8,128)}, f32[6,2,128,128]{3,2,1,0:T(8,128)S(1)}, u32[]{:S(2)}, u32[]{:S(2)}) collective-permute-start(f32[6,2,128,128]{3,2,1,0:T(8,128)} %get-tuple-element.47), channel_id=1, source_target_pairs={{4,0},{8,4},{12,8},{16,12},{20,16},{24,20},{28,24},{5,1},{9,5},{13... | collective-permute-start | bytes 2359304 | tf_op jit(solution)/shard_map/ppermute | solution.py:23
  5.4 31.2 %collective-permute-start.1 = (f32[6,2,128,128]{3,2,1,0:T(8,128)}, f32[6,2,128,128]{3,2,1,0:T(8,128)}, u32[]{:S(2)}, u32[]{:S(2)}) collective-permute-start(f32[6,2,128,128]{3,2,1,0:T(8,128)} %get-tuple-element.48), channel_id=1, source_target_pairs={{0,4},{4,8},{8,12},{12,16},{16,20},{20,24},{24,28},{1,5},{5,9},{9,... | collective-permute-start | bytes 2359304 | tf_op jit(solution)/shard_map/ppermute | solution.py:22
  34.9 70.8 %copy-start.1 = (f32[4,128,128]{2,1,0:T(8,128)}, f32[4,128,128]{2,1,0:T(8,128)S(1)}, u32[]{:S(2)}) copy-start(f32[4,128,128]{2,1,0:T(8,128)S(1)} %multiply_exponential_fusion) | copy-start | bytes 786436
  34.9 2.2 %copy-start = (f32[1,9,4,128,128]{4,3,2,1,0:T(8,128)S(1)}, f32[1,9,4,128,128]{4,3,2,1,0:T(8,128)}, u32[]{:S(2)}) copy-start(f32[1,9,4,128,128]{4,3,2,1,0:T(8,128)} %param.6) | copy-start | bytes 7077892
  34.9 70.8 %copy-start.5 = (f32[4,128,128]{2,1,0:T(8,128)}, f32[4,128,128]{2,1,0:T(8,128)S(1)}, u32[]{:S(2)}) copy-start(f32[4,128,128]{2,1,0:T(8,128)S(1)} %broadcast_multiply_fusion.1) | copy-start | bytes 786436
  38.4 67.3 %copy-start.8 = (f32[1,4,128,128]{3,2,1,0:T(8,128)}, f32[1,4,128,128]{3,2,1,0:T(8,128)S(1)}, u32[]{:S(2)}) copy-start(f32[1,4,128,128]{3,2,1,0:T(8,128)S(1)} %fusion.31) | copy-start | bytes 786436
  41.0 8.5 %copy-start.43 = (f32[4,32,128]{2,1,0:T(8,128)S(1)}, f32[4,32,128]{2,1,0:T(8,128)}, u32[]{:S(2)}) copy-start(f32[4,32,128]{2,1,0:T(8,128)} %param.8) | copy-start | bytes 196612
  41.2 20.3 %copy-start.44 = (f32[4,32,128]{2,1,0:T(8,128)S(1)}, f32[4,32,128]{2,1,0:T(8,128)}, u32[]{:S(2)}) copy-start(f32[4,32,128]{2,1,0:T(8,128)} %param.7) | copy-start | bytes 196612
  41.7 30.8 %collective-permute-start.2 = (f32[3,2,128,128]{3,2,1,0:T(8,128)S(1)}, f32[3,2,128,128]{3,2,1,0:T(8,128)S(1)}, u32[]{:S(2)}, u32[]{:S(2)}) collective-permute-start(f32[3,2,128,128]{3,2,1,0:T(8,128)S(1)} %get-tuple-element.67), channel_id=1, source_target_pairs={{0,4},{4,8},{8,12},{12,16},{16,20},{20,24},{24,28},{1,5},{5,9},{9,... | collective-permute-start | bytes 1179656 | tf_op jit(solution)/shard_map/ppermute | solution.py:22
  47.5 24.9 %collective-permute-start.3 = (f32[3,2,128,128]{3,2,1,0:T(8,128)S(1)}, f32[3,2,128,128]{3,2,1,0:T(8,128)S(1)}, u32[]{:S(2)}, u32[]{:S(2)}) collective-permute-start(f32[3,2,128,128]{3,2,1,0:T(8,128)S(1)} %get-tuple-element.68), channel_id=1, source_target_pairs={{4,0},{8,4},{12,8},{16,12},{20,16},{24,20},{28,24},{5,1},{9,5},{13... | collective-permute-start | bytes 1179656 | tf_op jit(solution)/shard_map/ppermute | solution.py:23
  75.5 26.2 %collective-permute-start.4 = (f32[6,2,128,128]{3,2,1,0:T(8,128)}, f32[6,2,128,128]{3,2,1,0:T(8,128)S(1)}, u32[]{:S(2)}, u32[]{:S(2)}) collective-permute-start(f32[6,2,128,128]{3,2,1,0:T(8,128)} %get-tuple-element.45), channel_id=1, source_target_pairs={{4,0},{8,4},{12,8},{16,12},{20,16},{24,20},{28,24},{5,1},{9,5},{13... | collective-permute-start | bytes 2359304 | tf_op jit(solution)/shard_map/ppermute | solution.py:23
  84.0 17.8 %collective-permute-start.5 = (f32[6,2,128,128]{3,2,1,0:T(8,128)}, f32[6,2,128,128]{3,2,1,0:T(8,128)}, u32[]{:S(2)}, u32[]{:S(2)}) collective-permute-start(f32[6,2,128,128]{3,2,1,0:T(8,128)} %get-tuple-element.46), channel_id=1, source_target_pairs={{0,4},{4,8},{8,12},{12,16},{16,20},{20,24},{24,28},{1,5},{5,9},{9,... | collective-permute-start | bytes 2359304 | tf_op jit(solution)/shard_map/ppermute | solution.py:22
  103.1 2.6 %copy-start.23 = (f32[1,4,128,128]{3,2,1,0:T(8,128)}, f32[1,4,128,128]{3,2,1,0:T(8,128)S(1)}, u32[]{:S(2)}) copy-start(f32[1,4,128,128]{3,2,1,0:T(8,128)S(1)} %fusion.75) | copy-start | bytes 786436
  107.3 15.4 %copy-start.20 = (f32[4,128,128]{2,1,0:T(8,128)S(1)}, f32[4,128,128]{2,1,0:T(8,128)}, u32[]{:S(2)}) copy-start(f32[4,128,128]{2,1,0:T(8,128)} %copy-done.19) | copy-start | bytes 786436
  107.4 13.4 %collective-permute-start.6 = (f32[3,2,128,128]{3,2,1,0:T(8,128)S(1)}, f32[3,2,128,128]{3,2,1,0:T(8,128)S(1)}, u32[]{:S(2)}, u32[]{:S(2)}) collective-permute-start(f32[3,2,128,128]{3,2,1,0:T(8,128)S(1)} %get-tuple-element.62), channel_id=1, source_target_pairs={{0,4},{4,8},{8,12},{12,16},{16,20},{20,24},{24,28},{1,5},{5,9},{9,... | collective-permute-start | bytes 1179656 | tf_op jit(solution)/shard_map/ppermute | solution.py:22
  112.7 10.0 %collective-permute-start.7 = (f32[3,2,128,128]{3,2,1,0:T(8,128)S(1)}, f32[3,2,128,128]{3,2,1,0:T(8,128)S(1)}, u32[]{:S(2)}, u32[]{:S(2)}) collective-permute-start(f32[3,2,128,128]{3,2,1,0:T(8,128)S(1)} %get-tuple-element.63), channel_id=1, source_target_pairs={{4,0},{8,4},{12,8},{16,12},{20,16},{24,20},{28,24},{5,1},{9,5},{13... | collective-permute-start | bytes 1179656 | tf_op jit(solution)/shard_map/ppermute | solution.py:23
  124.6 7.8 %copy-start.46 = (s32[1,8,4,4]{1,3,2,0:T(4,128)S(1)}, s32[1,8,4,4]{1,3,2,0:T(4,128)}, u32[]{:S(2)}) copy-start(s32[1,8,4,4]{1,3,2,0:T(4,128)} %get-tuple-element.69) | copy-start | bytes 1540
  124.6 7.8 %copy-start.47 = (s32[1,8,4,4]{1,3,2,0:T(4,128)S(1)}, s32[1,8,4,4]{1,3,2,0:T(4,128)}, u32[]{:S(2)}) copy-start(s32[1,8,4,4]{1,3,2,0:T(4,128)} %get-tuple-element.72) | copy-start | bytes 1540
  125.9 22.2 %collective-permute-start.8 = (f32[6,2,128,128]{3,2,1,0:T(8,128)}, f32[6,2,128,128]{3,2,1,0:T(8,128)S(1)}, u32[]{:S(2)}, u32[]{:S(2)}) collective-permute-start(f32[6,2,128,128]{3,2,1,0:T(8,128)} %get-tuple-element.38), channel_id=1, source_target_pairs={{4,0},{8,4},{12,8},{16,12},{20,16},{24,20},{28,24},{5,1},{9,5},{13... | collective-permute-start | bytes 2359304 | tf_op jit(solution)/shard_map/ppermute | solution.py:23
  127.8 20.3 %collective-permute-start.9 = (f32[6,2,128,128]{3,2,1,0:T(8,128)}, f32[6,2,128,128]{3,2,1,0:T(8,128)S(1)}, u32[]{:S(2)}, u32[]{:S(2)}) collective-permute-start(f32[6,2,128,128]{3,2,1,0:T(8,128)} %get-tuple-element.39), channel_id=1, source_target_pairs={{0,4},{4,8},{8,12},{12,16},{16,20},{20,24},{24,28},{1,5},{5,9},{9,... | collective-permute-start | bytes 2359304 | tf_op jit(solution)/shard_map/ppermute | solution.py:22
  150.3 1.7 copy-start.36
  152.0 14.0 %copy-start.21 = (f32[4,128,128]{2,1,0:T(8,128)S(1)}, f32[4,128,128]{2,1,0:T(8,128)}, u32[]{:S(2)}) copy-start(f32[4,128,128]{2,1,0:T(8,128)} %copy-done.19) | copy-start | bytes 786436
  152.1 9.1 %collective-permute-start.10 = (f32[3,2,128,128]{3,2,1,0:T(8,128)S(1)}, f32[3,2,128,128]{3,2,1,0:T(8,128)S(1)}, u32[]{:S(2)}, u32[]{:S(2)}) collective-permute-start(f32[3,2,128,128]{3,2,1,0:T(8,128)S(1)} %get-tuple-element.57), channel_id=1, source_target_pairs={{0,4},{4,8},{8,12},{12,16},{16,20},{20,24},{24,28},{1,5},{5,9},{9,... | collective-permute-start | bytes 1179656 | tf_op jit(solution)/shard_map/ppermute | solution.py:22
  154.5 11.5 %collective-permute-start.11 = (f32[3,2,128,128]{3,2,1,0:T(8,128)S(1)}, f32[3,2,128,128]{3,2,1,0:T(8,128)S(1)}, u32[]{:S(2)}, u32[]{:S(2)}) collective-permute-start(f32[3,2,128,128]{3,2,1,0:T(8,128)S(1)} %get-tuple-element.58), channel_id=1, source_target_pairs={{4,0},{8,4},{12,8},{16,12},{20,16},{24,20},{28,24},{5,1},{9,5},{13... | collective-permute-start | bytes 1179656 | tf_op jit(solution)/shard_map/ppermute | solution.py:23
  168.8 22.4 %collective-permute-start.12 = (f32[6,2,128,128]{3,2,1,0:T(8,128)}, f32[6,2,128,128]{3,2,1,0:T(8,128)S(1)}, u32[]{:S(2)}, u32[]{:S(2)}) collective-permute-start(f32[6,2,128,128]{3,2,1,0:T(8,128)} %get-tuple-element.31), channel_id=1, source_target_pairs={{4,0},{8,4},{12,8},{16,12},{20,16},{24,20},{28,24},{5,1},{9,5},{13... | collective-permute-start | bytes 2359304 | tf_op jit(solution)/shard_map/ppermute | solution.py:23
  170.7 20.5 %collective-permute-start.13 = (f32[6,2,128,128]{3,2,1,0:T(8,128)}, f32[6,2,128,128]{3,2,1,0:T(8,128)S(1)}, u32[]{:S(2)}, u32[]{:S(2)}) collective-permute-start(f32[6,2,128,128]{3,2,1,0:T(8,128)} %get-tuple-element.32), channel_id=1, source_target_pairs={{0,4},{4,8},{8,12},{12,16},{16,20},{20,24},{24,28},{1,5},{5,9},{9,... | collective-permute-start | bytes 2359304 | tf_op jit(solution)/shard_map/ppermute | solution.py:22
  195.3 13.8 %copy-start.22 = (f32[4,128,128]{2,1,0:T(8,128)S(1)}, f32[4,128,128]{2,1,0:T(8,128)}, u32[]{:S(2)}) copy-start(f32[4,128,128]{2,1,0:T(8,128)} %copy-done.19) | copy-start | bytes 786436
  195.4 8.7 %collective-permute-start.14 = (f32[3,2,128,128]{3,2,1,0:T(8,128)S(1)}, f32[3,2,128,128]{3,2,1,0:T(8,128)S(1)}, u32[]{:S(2)}, u32[]{:S(2)}) collective-permute-start(f32[3,2,128,128]{3,2,1,0:T(8,128)S(1)} %get-tuple-element.52), channel_id=1, source_target_pairs={{0,4},{4,8},{8,12},{12,16},{16,20},{20,24},{24,28},{1,5},{5,9},{9,... | collective-permute-start | bytes 1179656 | tf_op jit(solution)/shard_map/ppermute | solution.py:22
  197.6 11.5 %collective-permute-start.15 = (f32[3,2,128,128]{3,2,1,0:T(8,128)S(1)}, f32[3,2,128,128]{3,2,1,0:T(8,128)S(1)}, u32[]{:S(2)}, u32[]{:S(2)}) collective-permute-start(f32[3,2,128,128]{3,2,1,0:T(8,128)S(1)} %get-tuple-element.53), channel_id=1, source_target_pairs={{4,0},{8,4},{12,8},{16,12},{20,16},{24,20},{28,24},{5,1},{9,5},{13... | collective-permute-start | bytes 1179656 | tf_op jit(solution)/shard_map/ppermute | solution.py:23
  (32 other events, 40.0 us)
where the time goes:
time: 214 us; the launch traced here: 212 us
  waiting for transfers between devices  62.1 us (29%)
  starting transfers between devices  54.8 us (26%)
  blocking collectives  47.4 us (22%)
  local copies, waits for them, and re-layouts  24.8 us (12%)
  other arithmetic  22.2 us (10%)
    ppermute x8, waiting for transfers between devices, extended(): after = lax.ppermute(initial, axis, down)  46.8 us
    ppermute x8, starting transfers between devices, extended(): before = lax.ppermute(last, axis, up)  32.1 us
    ppermute x8, starting transfers between devices, extended(): after = lax.ppermute(initial, axis, down)  22.7 us
    ppermute x8, waiting for transfers between devices, extended(): before = lax.ppermute(last, axis, up)  15.3 us
    all_gather x1, blocking collectives, per_device(): lax.all_gather(buoyancy, 'shot', axis=1, tiled=True)  12.4 us
    all_gather x1, blocking collectives, per_device(): lax.all_gather(quality, 'shot', axis=1, tiled=True)  12.1 us
    all_gather x1, blocking collectives, per_device(): lax.all_gather(lame_mu, 'shot', axis=1, tiled=True)  12 us
    all_gather x1, blocking collectives, per_device(): lax.all_gather(lame_lambda, 'shot', axis=1, tiled=True)  10.9 us
  transfers between devices with their start and end apart: 16, of which 10 were waited for; matrix products, arithmetic and copies ran while one was open for 6% of the time, Pallas kernels for 0%

commit v1 on v0

v1 whole, which is shorter than its diff:
```python
import functools

import jax
import jax.numpy as jnp
from jax import lax
from jax.experimental import pallas as pl
from jax.experimental.pallas import tpu as pltpu
from jax.sharding import PartitionSpec as P

NEAR = 1.125
FAR = -1.0 / 24.0
DT = 0.2
ROWS = 8
PAD = 8
REACH = 3
VMEM = pl.BlockSpec(memory_space=pltpu.VMEM)
ANY = pl.BlockSpec(memory_space=pl.ANY)
F32 = jnp.float32


def call(body, ins, outs, alias=(), scratch=(), anywhere=(), flops=1_000_000):
    in_names, out_names = list(ins), list(outs)

    def kernel(*refs):
        names = {}
        for name, ref in zip(in_names, refs):
            if name not in alias:
                names[name] = ref
        for name, ref in zip(out_names, refs[len(in_names):]):
            names[name] = ref
        body(names, *refs[len(in_names) + len(out_names):])

    size = sum(4 * a.size for a in ins.values())
    ins = {name: pltpu.with_memory_space_constraint(a, pltpu.HBM) if name in anywhere
           else pltpu.with_memory_space_constraint(a, pltpu.VMEM) if name in alias
           else a for name, a in ins.items()}
    results = pl.pallas_call(
        kernel,
        out_shape=[pltpu.HBM(shape, F32) if name in anywhere else pltpu.VMEM(shape, F32)
                   for name, shape in outs.items()],
        in_specs=[ANY if name in anywhere else VMEM for name in in_names],
        out_specs=[ANY if name in anywhere else VMEM for name in out_names],
        scratch_shapes=list(scratch),
        input_output_aliases={in_names.index(n): out_names.index(n) for n in alias},
        compiler_params=pltpu.CompilerParams(vmem_limit_bytes=24 * 2**20),
        cost_estimate=pl.CostEstimate(flops=flops, bytes_accessed=size, transcendentals=0),
    )(*ins.values())
    return dict(zip(out_names, results))


def odd_slab():
    return lax.rem(lax.axis_index("aper"), 2) == 1


def pick(flag, yes, no):
    return jnp.where(flag, jnp.int32(yes), jnp.int32(no))


class Shifts:
    def __init__(self, lanes):
        lane = lax.broadcasted_iota(jnp.int32, (ROWS, lanes), 1)
        self.lanes = lanes
        self.f_up1 = jnp.where(lane < lanes - 1, F32(NEAR), F32(0))
        self.f_up2 = jnp.where(lane < lanes - 2, F32(FAR), F32(0))
        self.f_dn1 = jnp.where(lane >= 1, F32(-FAR), F32(0))
        self.b_dn1 = jnp.where(lane >= 1, F32(-NEAR), F32(0))
        self.b_dn2 = jnp.where(lane >= 2, F32(-FAR), F32(0))
        self.b_up1 = jnp.where(lane < lanes - 1, F32(FAR), F32(0))

    def fz(self, f):
        n = self.lanes
        return (self.f_up1 * pltpu.roll(f, n - 1, 1) - NEAR * f) + (
            self.f_up2 * pltpu.roll(f, n - 2, 1) + self.f_dn1 * pltpu.roll(f, 1, 1)
        )

    def bz(self, f):
        n = self.lanes
        return (self.b_dn1 * pltpu.roll(f, 1, 1) + NEAR * f) + (
            self.b_up1 * pltpu.roll(f, n - 1, 1) + self.b_dn2 * pltpu.roll(f, 2, 1)
        )


def fwd(at):
    return NEAR * (at(1) - at(0)) + FAR * (at(2) - at(-1))


def bwd(at):
    return NEAR * (at(0) - at(-1)) + FAR * (at(1) - at(-2))


def tile_reader(ref, field, start):
    seen = {}

    def read(layer, dy=0):
        if (layer, dy) not in seen:
            seen[layer, dy] = ref[field, layer, pl.ds(start + PAD + dy, ROWS), :]
        return seen[layer, dy]

    return read


def factors(active_cells, damp):
    return jnp.where(active_cells, damp, F32(1)), jnp.where(active_cells, DT * damp, F32(0))


def mask_rows(refs, moment, slab, start, blocks, block_rows):
    row = (moment * 3 + slab) * blocks + start // block_rows
    return jnp.broadcast_to(refs["mask"][pl.ds(row, 1), :], (ROWS, refs["mask"].shape[1])) > 0


def zero_pads(ref, rows):
    zeros = jnp.zeros((ref.shape[0], ref.shape[1], PAD, ref.shape[3]), F32)
    ref[:, :, :PAD, :] = zeros
    ref[:, :, PAD + rows:, :] = zeros


class Plan:
    def __init__(self, cx, rows, lanes, blocks, steps, cuts):
        self.cx, self.rows, self.lanes = cx, rows, lanes
        self.blocks, self.steps, self.cuts = blocks, steps, cuts
        self.block_rows = rows // blocks
        self.tiles = rows // ROWS

    def chunk(self, step, which):
        cut = self.cuts[step]
        return (0, cut) if which == 0 else (cut, self.tiles)

    def slots(self, step):
        n = self.cx
        if step < self.steps - 1:
            return [
                ((f, n + j), (f, REACH + j), (f, j), (f, n + REACH + j))
                for f in range(3) for j in range(REACH)
            ]
        top = [(0, n + 1), (0, n + 2), (1, n + 2), (2, n + 2), (2, n + 2)]
        bottom = [(0, 3), (1, 4), (1, 3), (2, 3), (2, 4)]
        below = [(0, 1), (0, 2), (1, 2), (2, 2), (2, 2)]
        above = [(0, n + 3), (1, n + 4), (1, n + 3), (2, n + 3), (2, n + 4)]
        return list(zip(top, bottom, below, above))

    def velocity(self, refs, moment, which, sh, so, previous):
        first, last = self.chunk(moment, which)
        z = Shifts(self.lanes)

        def tile(k, carry):
            start = pl.multiple_of(k * ROWS, ROWS)
            here = mask_rows(refs, moment, 1, start, self.blocks, self.block_rows)
            xx = tile_reader(sh, 0, start)
            xy = tile_reader(sh, 1, start)
            xz = tile_reader(sh, 2, start)
            yy = tile_reader(so, 0, start)
            zz = tile_reader(so, 1, start)
            yz = tile_reader(so, 2, start)
            for i in range(self.cx):
                keep, gain = factors(here, refs["damp"][i, pl.ds(start, ROWS), :])
                gain = gain * refs["buoy"][i, pl.ds(start, ROWS), :]
                gx = fwd(lambda d: xx(i + 1 + d)) + bwd(lambda d: xy(i + 2, d)) + z.bz(xz(i + 2))
                gy = bwd(lambda d: xy(i + 2 + d)) + fwd(lambda d: yy(i, d)) + z.bz(yz(i))
                gz = bwd(lambda d: xz(i + 2 + d)) + bwd(lambda d: yz(i, d)) + z.fz(zz(i))
                for f, g in enumerate((gx, gy, gz)):
                    refs["vel_next"][f, REACH + i, pl.ds(start + PAD, ROWS), :] = (
                        keep * previous(f, i, start) + gain * g
                    )
            return carry

        lax.fori_loop(first, last, tile, 0)
        odd = odd_slab()
        rows = pl.ds(PAD + first * ROWS, (last - first) * ROWS)
        for slot, (top, bottom, _, _) in enumerate(self.slots(moment)):
            field, layer = pick(odd, top[0], bottom[0]), pick(odd, top[1], bottom[1])
            refs["send_far"][slot] = refs["vel_next"][field, layer, rows, :]
            field, layer = pick(odd, bottom[0], top[0]), pick(odd, bottom[1], top[1])
            refs["send_near"][slot] = refs["vel_next"][field, layer, rows, :]

    def arrivals(self, refs, moment, which):
        first, last = self.chunk(moment, which)
        odd = odd_slab()
        rows = pl.ds(PAD + first * ROWS, (last - first) * ROWS)
        for slot, (_, _, below, above) in enumerate(self.slots(moment)):
            field, layer = pick(odd, above[0], below[0]), pick(odd, above[1], below[1])
            refs["vel"][field, layer, rows, :] = refs["from_far"][slot]
            field, layer = pick(odd, below[0], above[0]), pick(odd, below[1], above[1])
            refs["vel"][field, layer, rows, :] = refs["from_near"][slot]

    def stress_tiles(self, moment, which):
        first, last = self.chunk(moment, which)
        if which == 1:
            return first - 1, last
        return first, last - 1 if moment == self.steps - 1 else last

    def stress(self, refs, moment, which, final, part=None):
        first, last = part or self.stress_tiles(moment, which)
        base = self.stress_tiles(moment, which)[0]
        n = self.cx
        z = Shifts(self.lanes)
        old_h, old_o = refs["sh"], refs["so"]

        def tile(k, carry):
            start = pl.multiple_of(k * ROWS, ROWS)
            masks = [mask_rows(refs, moment, slab, start, self.blocks, self.block_rows) for slab in range(3)]
            vx = tile_reader(refs["vel"], 0, start)
            vy = tile_reader(refs["vel"], 1, start)
            vz = tile_reader(refs["vel"], 2, start)
            rows = pl.ds(start, ROWS)
            padded = pl.ds(start + PAD, ROWS)

            def put_h(field, i, value):
                if final:
                    refs["done"][(0, 3, 4)[field], i, pl.ds(start - base * ROWS, ROWS), :] = value
                else:
                    refs["sh_next"][field, i + (1, 2, 2)[field], padded, :] = value

            def put_o(field, i, value):
                if final:
                    refs["done"][(1, 2, 5)[field], i, pl.ds(start - base * ROWS, ROWS), :] = value
                else:
                    refs["so_next"][field, i, padded, :] = value

            for i in range(0, n) if final else range(-2, n + 2):
                own = 0 <= i < n
                if own:
                    damp = refs["damp"][i, rows, :]
                else:
                    damp = refs["damp_edge"][i + 2 if i < 0 else i - n + 2, rows, :]
                keep, gain = factors(masks[0 if i < 0 else 1 if own else 2], damp)
                at = i + REACH
                mu = gain * refs["mu"][i + 2, rows, :]
                if i >= -1:
                    ex = bwd(lambda d: vx(at + d))
                    ey = bwd(lambda d: vy(at, d))
                    ez = z.bz(vz(at))
                    spread = gain * refs["lam"][i + 1, rows, :] * (ex + ey + ez)
                    mu2 = mu + mu
                    put_h(0, i, keep * old_h[0, i + 1, padded, :] + (spread + mu2 * ex))
                if own:
                    put_o(0, i, keep * old_o[0, i, padded, :] + (spread + mu2 * ey))
                    put_o(1, i, keep * old_o[1, i, padded, :] + (spread + mu2 * ez))
                    yz = z.fz(vy(at)) + fwd(lambda d: vz(at, d))
                    put_o(2, i, keep * old_o[2, i, padded, :] + mu * yz)
                if i <= n:
                    xy = fwd(lambda d: vx(at, d)) + fwd(lambda d: vy(at + d))
                    put_h(1, i, keep * old_h[1, i + 2, padded, :] + mu * xy)
                    xz = z.fz(vx(at)) + fwd(lambda d: vz(at + d))
                    put_h(2, i, keep * old_h[2, i + 2, padded, :] + mu * xz)
            return carry

        lax.fori_loop(first, last, tile, 0)

    def finish(self, refs, moment, which, done, sems):
        refs = dict(refs, done=done)
        first, last = self.stress_tiles(moment, which)
        copies = []

        def move(src, dst):
            copy = pltpu.make_async_copy(src, dst, sems.at[len(copies)])
            copy.start()
            copies.append(copy)

        for f in range(3):
            span = (last - first) * ROWS
            move(refs["vel"].at[f, pl.ds(REACH, self.cx), pl.ds(PAD + first * ROWS, span)],
                 refs["out"].at[0, f, :, pl.ds(first * ROWS, span)])
        for a, b in self.parts(first, last):
            self.stress(refs, moment, which, True, (a, b))
            span = (b - a) * ROWS
            for f in range(6):
                move(done.at[f, :, pl.ds((a - first) * ROWS, span)],
                     refs["out"].at[0, 3 + f, :, pl.ds(a * ROWS, span)])
        for copy in copies:
            copy.wait()

    @staticmethod
    def parts(first, last):
        middle = (first + last + 1) // 2
        return [(a, b) for a, b in ((first, middle), (middle, last)) if b > a]


STRESS_SLOTS = 5
MODEL_SLOTS = 6


def pack(cx, panel_rows, rows, refs, sems):
    odd = odd_slab()
    copies = []

    def move(src, dst):
        copy = pltpu.make_async_copy(src, dst, sems.at[len(copies)])
        copy.start()
        copies.append(copy)

    top = [(3, cx - 1), (6, cx - 2), (6, cx - 1), (7, cx - 2), (7, cx - 1)]
    bottom = [(3, 0), (3, 1), (6, 0), (7, 0), (7, 0)]
    for name, flag in (("far", odd), ("near", jnp.logical_not(odd))):
        for slot in range(STRESS_SLOTS):
            field = pick(flag, top[slot][0], bottom[slot][0])
            layer = pick(flag, top[slot][1], bottom[slot][1])
            move(refs["wave"].at[0, field, layer], refs[name].at[pl.ds(slot * rows, rows)])
        base = STRESS_SLOTS * rows
        for slot in range(MODEL_SLOTS):
            array = refs[("lam", "lam", "mu", "mu", "q", "q")[slot]]
            layer = pick(flag, cx - 2 + slot % 2, slot % 2)
            move(array.at[layer], refs[name].at[pl.ds(base + slot * panel_rows, panel_rows)])
    for i, name in enumerate(("buoy", "q")):
        move(refs[name], refs["first"].at[pl.ds(i * cx, cx)])
    for i, name in enumerate(("lam", "mu")):
        move(refs[name], refs["second"].at[pl.ds(i * cx, cx)])
    for copy in copies:
        copy.wait()


def prepare(cx, rows, refs):
    zero_pads(refs["sh"], rows)
    zero_pads(refs["so"], rows)
    inner = pl.ds(PAD, rows)
    for field, (source, shift) in enumerate(((3, 1), (6, 2), (7, 2))):
        for i in range(cx):
            refs["sh"][field, i + shift, inner, :] = refs["wave"][0, source, i]
    for field, source in enumerate((4, 5, 8)):
        for i in range(cx):
            refs["so"][field, i, inner, :] = refs["wave"][0, source, i]
    for field in range(3):
        for i in range(cx):
            refs["old"][field, i] = refs["wave"][0, field, i]


def panel_place(k, shots, panel_rows):
    return pl.ds(pl.multiple_of(partner(lax.axis_index("shot"), k, shots) * panel_rows, panel_rows), panel_rows)


def partner(index, k, shots):
    if shots & (shots - 1) == 0:
        return index ^ k
    return lax.rem(index + shots - k, shots)


def panel_pairs(k, shots):
    if shots & (shots - 1) == 0:
        return [(i, i ^ k) for i in range(shots)]
    return [(i, (i + k) % shots) for i in range(shots)]


def per_device(cuts_of, shots, slabs, wave, lam, mu, buoy, q, active):
    cx, panel_rows, lanes = lam.shape
    rows = wave.shape[3]
    steps, _, blocks, lane_blocks = active.shape
    plan = Plan(cx, rows, lanes, blocks, steps, cuts_of(steps, rows // ROWS))
    padded = rows + 2 * PAD
    far = [(i, i + 1) for i in range(1, slabs - 1, 2)]
    near = [(i, i + 1) for i in range(0, slabs - 1, 2)]
    far = far + [(j, i) for i, j in far]
    near = near + [(j, i) for i, j in near]

    def exchange(to_far, to_near):
        return lax.ppermute(to_far, "aper", far), lax.ppermute(to_near, "aper", near)

    def gather(mine):
        return [mine] + [lax.ppermute(mine, "shot", panel_pairs(k, shots)) for k in range(1, shots)]

    halo_rows = STRESS_SLOTS * rows + MODEL_SLOTS * panel_rows
    sent = call(
        functools.partial(pack, cx, panel_rows, rows),
        dict(wave=wave, lam=lam, mu=mu, buoy=buoy, q=q),
        dict(far=(halo_rows, lanes), near=(halo_rows, lanes),
             first=(2 * cx, panel_rows, lanes), second=(2 * cx, panel_rows, lanes)),
        scratch=[pltpu.SemaphoreType.DMA((2 * (STRESS_SLOTS + MODEL_SLOTS) + 4,))],
        anywhere=("wave", "lam", "mu", "buoy", "q"),
    )
    halo_far, halo_near = exchange(sent["far"], sent["near"])
    firsts = gather(sent["first"])
    seconds = gather(sent["second"])
    edge = jnp.concatenate([halo_far[STRESS_SLOTS * rows:], halo_near[STRESS_SLOTS * rows:]])
    edges = gather(edge)

    device = lax.axis_index("aper")
    around = lax.dynamic_slice_in_dim(jnp.pad(active, ((0, 0), (1, 1), (0, 0), (0, 0))), device, 3, 1)
    mask = jnp.repeat(around.astype(F32).reshape(steps * 3 * blocks, lane_blocks), lanes // lane_blocks, axis=1)

    sh_shape, so_shape = (3, cx + 3, padded, lanes), (3, cx, padded, lanes)
    vel_shape, slab_shape = (3, cx + 2 * REACH, padded, lanes), (cx, rows, lanes)
    state = call(functools.partial(prepare, cx, rows), dict(wave=wave),
                 dict(sh=sh_shape, so=so_shape, old=(3,) + slab_shape))

    def sends(step, which):
        first, last = plan.chunk(step, which)
        shape = (len(plan.slots(step)), (last - first) * ROWS, lanes)
        return dict(send_far=shape, send_near=shape)

    def start_first(refs):
        odd = odd_slab()
        inner = pl.ds(PAD, rows)
        below = [(0, 0), (1, 0), (1, 1), (2, 0), (2, 1)]
        above = [(0, cx + 1), (0, cx + 2), (1, cx + 2), (2, cx + 2), (2, cx + 2)]
        for slot in range(STRESS_SLOTS):
            part = pl.ds(slot * rows, rows)
            field = pick(odd, above[slot][0], below[slot][0])
            layer = pick(odd, above[slot][1], below[slot][1])
            refs["sh"][field, layer, inner, :] = refs["halo_far"][part, :]
            field = pick(odd, below[slot][0], above[slot][0])
            layer = pick(odd, below[slot][1], above[slot][1])
            refs["sh"][field, layer, inner, :] = refs["halo_near"][part, :]
        for k in range(shots):
            place = panel_place(k, shots, panel_rows)
            for i in range(cx):
                refs["buoy"][i, place, :] = refs["first%d" % k][i]
                refs["damp"][i, place, :] = jnp.exp(-DT * refs["first%d" % k][cx + i])
        zero_pads(refs["vel_next"], rows)
        start_chunk(refs, 0)

    def start_chunk(refs, which):
        plan.velocity(refs, 0, which, refs["sh"], refs["so"],
                      lambda f, i, start: refs["old"][f, i, pl.ds(start, ROWS), :])

    ins = dict(sh=state["sh"], so=state["so"], old=state["old"], mask=mask,
               halo_far=halo_far, halo_near=halo_near)
    ins.update({"first%d" % k: a for k, a in enumerate(firsts)})
    got = call(start_first, ins,
               dict(sh=sh_shape, buoy=slab_shape, damp=slab_shape, vel_next=vel_shape, **sends(0, 0)),
               alias=("sh",))
    sh, so = got["sh"], state["so"]
    model = dict(mask=mask, buoy=got["buoy"], damp=got["damp"])
    arrived = [exchange(got["send_far"], got["send_near"])]
    got = call(lambda refs: start_chunk(refs, 1),
               dict(sh=sh, so=so, old=state["old"], vel_next=got["vel_next"], **model),
               dict(vel_next=vel_shape, **sends(0, 1)), alias=("vel_next",))
    vel = got["vel_next"]
    arrived.append(exchange(got["send_far"], got["send_near"]))

    def assemble(refs):
        odd = odd_slab()
        for k in range(shots):
            place = panel_place(k, shots, panel_rows)
            for i in range(cx):
                refs["lam"][i + 1, place, :] = refs["second%d" % k][i]
                refs["mu"][i + 2, place, :] = refs["second%d" % k][cx + i]
            for half, flag in ((0, odd), (1, jnp.logical_not(odd))):
                def part(slot):
                    return refs["edge%d" % k][pl.ds((half * MODEL_SLOTS + slot) * panel_rows, panel_rows), :]
                for j in range(2):
                    layer = pick(flag, cx + 1 + j, 0)
                    if j == 1:
                        refs["lam"][layer, place, :] = part(1)
                    else:
                        refs["lam"][layer, place, :] = part(0)
                    refs["mu"][pick(flag, cx + 2 + j, j), place, :] = part(2 + j)
                    refs["damp_edge"][pick(flag, 2 + j, j), place, :] = jnp.exp(-DT * part(4 + j))

    ins = {"second%d" % k: a for k, a in enumerate(seconds)}
    ins.update({"edge%d" % k: a for k, a in enumerate(edges)})
    model.update(call(assemble, ins, dict(lam=(cx + 3, rows, lanes), mu=(cx + 4, rows, lanes),
                                          damp_edge=(4, rows, lanes))))

    out_shape = wave.shape
    for step in range(steps):
        final = step == steps - 1

        def advance(refs, *scratch, which, step=step, final=final):
            plan.arrivals(refs, step, which)
            if final:
                plan.finish(refs, step, which, *scratch)
                return
            if which == 0:
                zero_pads(refs["sh_next"], rows)
                zero_pads(refs["so_next"], rows)
                zero_pads(refs["vel_next"], rows)
            plan.stress(refs, step, which, False)
            plan.velocity(
                refs, step + 1, which, refs["sh_next"], refs["so_next"],
                lambda f, i, start: refs["vel"][f, REACH + i, pl.ds(start + PAD, ROWS), :])

        nexts = dict(out=out_shape) if final else dict(
            sh_next=sh_shape, so_next=so_shape, vel_next=vel_shape)
        following = []
        carried = {}
        for which in range(2):
            ins = dict(vel=vel, sh=sh, so=so, from_far=arrived[which][0], from_near=arrived[which][1],
                       **model, **carried)
            outs = dict(vel=vel_shape, **nexts)
            scratch = []
            if final:
                first, last = plan.stress_tiles(step, which)
                scratch = [pltpu.VMEM((6, cx, (last - first) * ROWS, lanes), F32),
                           pltpu.SemaphoreType.DMA((3 + 6 * len(plan.parts(first, last)),))]
            else:
                outs.update(sends(step + 1, which))
            got = call(functools.partial(advance, which=which), ins, outs, alias=("vel",) + tuple(carried),
                       scratch=scratch, anywhere=("out",))
            vel = got["vel"]
            carried = {name: got[name] for name in nexts}
            if not final:
                following.append(exchange(got["send_far"], got["send_near"]))
        if final:
            return carried["out"]
        vel, sh, so, arrived = carried["vel_next"], carried["sh_next"], carried["so_next"], following


def cuts_of(steps, tiles):
    middle = tiles // 2 + steps // 2
    return [max(1, middle - step) for step in range(steps)]


def solution(mesh):
    body = functools.partial(per_device, cuts_of, mesh.shape["shot"], mesh.shape["aper"])
    return jax.shard_map(
        body,
        mesh=mesh,
        in_specs=(
            P("shot", None, "aper", None, None),
            P("aper", "shot", None),
            P("aper", "shot", None),
            P("aper", "shot", None),
            P("aper", "shot", None),
            P(),
        ),
        out_specs=P("shot", None, "aper", None, None),
        check_vma=False,
    )
```

time: 214 us -> 109 us (0.51)
  blocking collectives: 47.4 us -> 0 us
  waiting for transfers between devices: 62.1 us -> 31.1 us
  Pallas kernels: 0 us -> 22.7 us
  local copies, waits for them, and re-layouts: 24.8 us -> 3.06 us
  other arithmetic: 22.2 us -> 0.76 us
  starting transfers between devices: 54.8 us -> 49.3 us
    all_gather x4 -> x0, blocking collectives: 47.4 us -> none  [the longest x1 12.4 us: per_device(): lax.all_gather(buoyancy, 'shot', axis=1, tiled=True)]
    ppermute x16 -> x27, waiting for transfers between devices: 62.1 us -> 31.1 us  [the longest x9 17.6 us: gather(): lax.ppermute(mine, 'shot', panel_pairs(k, shots))]
    pallas_call x0 -> x13, Pallas kernels: none -> 22.7 us  [call(): pl.pallas_call(kernel, out_shape=[pltpu.HBM(shape, F32) if name in anywhe...]
    another operation x16 -> x0, other arithmetic: 10.5 us -> none  [the longest x12 9.36 us: velocity_update(): forcing = jnp.stack([grad_first, grad_second, grad_third])]
    slice x18 -> x2, local copies, waits for them, and re-layouts: 9.44 us -> 0.02 us  [the longest x1 0.01 us: per_device(): halo_far[STRESS_SLOTS * rows:]]
    broadcast_in_dim x16 -> x1, local copies, waits for them, and re-layouts: 9.27 us -> 0.64 us  [per_device(): jnp.repeat(around.astype(F32).reshape(steps * 3 * blocks, lane_blocks), l...]
    add x8 -> x0, other arithmetic: 6.61 us -> none  [the longest x4 5.23 us: velocity_update(): previous + active_cells * (damping * (previous + TIME_STEP * buoyancy * f...]
    ppermute x16 -> x27, starting transfers between devices: 54.8 us -> 49.3 us  [the longest x9 33.7 us: exchange(): lax.ppermute(to_far, 'aper', far)]
  transfers between devices with their start and end apart: 16 -> 27, of which waited for: 10 -> 9; matrix products, arithmetic and copies ran while one was open for 6% -> 3% of each run, Pallas kernels for 0% -> 15%
where the time goes in v1:
time: 109 us; the launch traced here: 107 us
  starting transfers between devices  49.3 us (45%)
  waiting for transfers between devices  31.1 us (29%)
  Pallas kernels  22.7 us (21%)
  local copies, waits for them, and re-layouts  3.06 us (3%)
    ppermute x9, starting transfers between devices, exchange(): lax.ppermute(to_far, 'aper', far)  33.7 us
    pallas_call x13, Pallas kernels, call(): pl.pallas_call(kernel, out_shape=[pltpu.HBM(shape, F32) if name in anywhe...  22.7 us
    ppermute x9, waiting for transfers between devices, gather(): lax.ppermute(mine, 'shot', panel_pairs(k, shots))  17.6 us
    ppermute x9, waiting for transfers between devices, exchange(): lax.ppermute(to_far, 'aper', far)  13.5 us
    ppermute x9, starting transfers between devices, gather(): lax.ppermute(mine, 'shot', panel_pairs(k, shots))  12.8 us
    ppermute x9, starting transfers between devices, exchange(): lax.ppermute(to_near, 'aper', near)  2.87 us
  transfers between devices with their start and end apart: 27, of which 9 were waited for; matrix products, arithmetic and copies ran while one was open for 3% of the time, Pallas kernels for 15%

profile of v1, /device:TPU:3, one launch (start us, length us, event | category | flops | bytes accessed | tf_op | source)
XLA Modules:
  0.0 107.3 jit_solution(12669634090436891316)
XLA Ops:
  0.0 2.6 %shard_map.65 = (f32[832,128]{1,0:T(8,128)}, f32[832,128]{1,0:T(8,128)}, f32[8,32,128]{2,1,0:T(8,128)}, f32[8,32,128]{2,1,0:T(8,128)S(1)}) custom-call(f32[1,9,4,128,128]{4,3,2,1,0:T(8,128)} %refs_0_.3, f32[4,32,128]{2,1,0:T(8,128)} %refs_1_.1, f32[4,32,128]{2,1,0:T(8,128)} %refs_2_.1, f32[4,32,128]{2,1,0:T(8,128)} %refs_3_.1, f32[4,32,128]{2,1,0:T(8,128)} %refs_4_.1), custom_call_target="tpu_custom_call" | custom-call | flops 1000000 | bytes 2621440 | tf_op jit(solution)/shard_map/pallas_call | solution.py:37
  2.6 3.7 %collective-permute-start = (f32[832,128]{1,0:T(8,128)}, f32[832,128]{1,0:T(8,128)S(1)}, u32[]{:S(2)}, u32[]{:S(2)}) collective-permute-start(f32[832,128]{1,0:T(8,128)} %get-tuple-element.63), channel_id=1, source_target_pairs={{4,8},{12,16},{20,24},{8,4},{16,12},{24,20},{5,9},{13,17},{21,25},... | collective-permute-start | bytes 1277960 | tf_op jit(solution)/shard_map/ppermute | solution.py:354
  6.3 3.4 %collective-permute-start.4 = (f32[8,32,128]{2,1,0:T(8,128)}, f32[8,32,128]{2,1,0:T(8,128)S(1)}, u32[]{:S(2)}, u32[]{:S(2)}) collective-permute-start(f32[8,32,128]{2,1,0:T(8,128)} %get-tuple-element.65.refs_6_), channel_id=1, source_target_pairs={{0,3},{1,2},{2,1},{3,0},{4,7},{5,6},{6,5},{7,4},{8,11},{9,10},{10,... | collective-permute-start | bytes 393224 | tf_op jit(solution)/shard_map/ppermute | solution.py:357
  10.9 2.4 %collective-permute-done.4.refs_9_ = f32[8,32,128]{2,1,0:T(8,128)S(1)} collective-permute-done((f32[8,32,128]{2,1,0:T(8,128)}, f32[8,32,128]{2,1,0:T(8,128)S(1)}, u32[]{:S(2)}, u32[]{:S(2)}) %collective-permute-start.4) | collective-permute-done | bytes 131104 | tf_op jit(solution)/shard_map/ppermute | solution.py:357
  13.9 3.2 %collective-permute-start.9 = (f32[8,32,128]{2,1,0:T(8,128)S(1)}, f32[8,32,128]{2,1,0:T(8,128)S(1)}, u32[]{:S(2)}, u32[]{:S(2)}) collective-permute-start(f32[8,32,128]{2,1,0:T(8,128)S(1)} %get-tuple-element.73.refs_0_), channel_id=1, source_target_pairs={{0,3},{1,2},{2,1},{3,0},{4,7},{5,6},{6,5},{7,4},{8,11},{9,10},{10,... | collective-permute-start | bytes 393224 | tf_op jit(solution)/shard_map/ppermute | solution.py:357
  19.6 4.0 %collective-permute-done.3.refs_8_ = f32[8,32,128]{2,1,0:T(8,128)} collective-permute-done((f32[8,32,128]{2,1,0:T(8,128)}, f32[8,32,128]{2,1,0:T(8,128)}, u32[]{:S(2)}, u32[]{:S(2)}) %collective-permute-start.3) | collective-permute-done | bytes 131104 | tf_op jit(solution)/shard_map/ppermute | solution.py:357
  23.7 2.3 %shard_map.66 = (f32[3,7,144,128]{3,2,1,0:T(8,128)S(1)}, f32[4,128,128]{2,1,0:T(8,128)S(1)}, f32[4,128,128]{2,1,0:T(8,128)S(1)}, f32[3,10,144,128]{3,2,1,0:T(8,1...) custom-call(f32[3,7,144,128]{3,2,1,0:T(8,128)S(1)} %get-tuple-element.60.refs_0_, ...), custom_call_target="tpu_custom_call", output_to_operand_aliasing={{0}: (0, {})} | custom-call | flops 1000000 | bytes 4620288 | tf_op jit(solution)/shard_map/pallas_call | solution.py:37
  26.0 6.5 %collective-permute-start.5 = (f32[9,80,128]{2,1,0:T(8,128)S(1)}, f32[9,80,128]{2,1,0:T(8,128)S(1)}, u32[]{:S(2)}, u32[]{:S(2)}) collective-permute-start(f32[9,80,128]{2,1,0:T(8,128)S(1)} %get-tuple-element.71), channel_id=1, source_target_pairs={{4,8},{12,16},{20,24},{8,4},{16,12},{24,20},{5,9},{13,17},{21,25},... | collective-permute-start | bytes 1105928 | tf_op jit(solution)/shard_map/ppermute | solution.py:354
  33.6 1.9 %collective-permute-start.11 = (f32[384,128]{1,0:T(8,128)S(1)}, f32[384,128]{1,0:T(8,128)S(1)}, u32[]{:S(2)}, u32[]{:S(2)}) collective-permute-start(f32[384,128]{1,0:T(8,128)S(1)} %pad_maximum_fusion.refs_4_), channel_id=1, source_target_pairs={{0,2},{1,3},{2,0},{3,1},{4,6},{5,7},{6,4},{7,5},{8,10},{9,11},{10,... | collective-permute-start | bytes 589832 | tf_op jit(solution)/shard_map/ppermute | solution.py:357
  36.3 8.1 %collective-permute-done.7.refs_1_ = f32[8,32,128]{2,1,0:T(8,128)S(1)} collective-permute-done((f32[8,32,128]{2,1,0:T(8,128)S(1)}, f32[8,32,128]{2,1,0:T(8,128)S(1)}, u32[]{:S(2)}, u32[]{:S(2)}) %collective-permute-start.7) | collective-permute-done | bytes 131104 | tf_op jit(solution)/shard_map/ppermute | solution.py:357
  44.4 2.2 %collective-permute-start.10 = (f32[384,128]{1,0:T(8,128)S(1)}, f32[384,128]{1,0:T(8,128)S(1)}, u32[]{:S(2)}, u32[]{:S(2)}) collective-permute-start(f32[384,128]{1,0:T(8,128)S(1)} %pad_maximum_fusion.refs_4_), channel_id=1, source_target_pairs={{0,1},{1,0},{2,3},{3,2},{4,5},{5,4},{6,7},{7,6},{8,9},{9,8},{10,11... | collective-permute-start | bytes 589832 | tf_op jit(solution)/shard_map/ppermute | solution.py:357
  47.4 3.5 %collective-permute-start.13 = (f32[9,48,128]{2,1,0:T(8,128)S(1)}, f32[9,48,128]{2,1,0:T(8,128)S(1)}, u32[]{:S(2)}, u32[]{:S(2)}) collective-permute-start(f32[9,48,128]{2,1,0:T(8,128)S(1)} %get-tuple-element.78), channel_id=1, source_target_pairs={{4,8},{12,16},{20,24},{8,4},{16,12},{24,20},{5,9},{13,17},{21,25},... | collective-permute-start | bytes 663560 | tf_op jit(solution)/shard_map/ppermute | solution.py:354
  50.9 1.9 %collective-permute-done.11.refs_6_ = f32[384,128]{1,0:T(8,128)S(1)} collective-permute-done((f32[384,128]{1,0:T(8,128)S(1)}, f32[384,128]{1,0:T(8,128)S(1)}, u32[]{:S(2)}, u32[]{:S(2)}) %collective-permute-start.11) | collective-permute-done | bytes 196640 | tf_op jit(solution)/shard_map/ppermute | solution.py:357
  52.8 1.2 %collective-permute-start.14 = (f32[9,48,128]{2,1,0:T(8,128)S(1)}, f32[9,48,128]{2,1,0:T(8,128)S(1)}, u32[]{:S(2)}, u32[]{:S(2)}) collective-permute-start(f32[9,48,128]{2,1,0:T(8,128)S(1)} %get-tuple-element.79), channel_id=1, source_target_pairs={{0,4},{8,12},{16,20},{24,28},{4,0},{12,8},{20,16},{28,24},{1,5},{9... | collective-permute-start | bytes 663560 | tf_op jit(solution)/shard_map/ppermute | solution.py:354
  54.0 1.1 %collective-permute-done.10.refs_5_ = f32[384,128]{1,0:T(8,128)S(1)} collective-permute-done((f32[384,128]{1,0:T(8,128)S(1)}, f32[384,128]{1,0:T(8,128)S(1)}, u32[]{:S(2)}, u32[]{:S(2)}) %collective-permute-start.10) | collective-permute-done | bytes 196640 | tf_op jit(solution)/shard_map/ppermute | solution.py:357
  55.3 2.6 %shard_map.69 = (f32[3,10,144,128]{3,2,1,0:T(8,128)S(1)}, f32[3,7,144,128]{3,2,1,0:T(8,128)S(1)}, f32[3,4,144,128]{3,2,1,0:T(8,128)S(1)}, f32[3,10,144,128]{3,2,...) custom-call(f32[3,10,144,128]{3,2,1,0:T(8,128)S(1)} %get-tuple-element.70., ...), custom_call_target="tpu_custom_call", output_to_operand_aliasing={{0}: (0, {})} | custom-call | flops 1000000 | bytes 7176192 | tf_op jit(solution)/shard_map/pallas_call | solution.py:37
  57.8 4.0 %collective-permute-start.15 = (f32[9,72,128]{2,1,0:T(8,128)S(1)}, f32[9,72,128]{2,1,0:T(8,128)S(1)}, u32[]{:S(2)}, u32[]{:S(2)}) collective-permute-start(f32[9,72,128]{2,1,0:T(8,128)S(1)} %get-tuple-element.86), channel_id=1, source_target_pairs={{4,8},{12,16},{20,24},{8,4},{16,12},{24,20},{5,9},{13,17},{21,25},... | collective-permute-start | bytes 995336 | tf_op jit(solution)/shard_map/ppermute | solution.py:354
  61.9 1.8 %shard_map.70 = (f32[3,10,144,128]{3,2,1,0:T(8,128)S(1)}, f32[3,7,144,128]{3,2,1,0:T(8,128)S(1)}, f32[3,4,144,128]{3,2,1,0:T(8,128)S(1)}, f32[3,10,144,128]{3,2,...) custom-call(f32[3,10,144,128]{3,2,1,0:T(8,128)S(1)} %get-tuple-eleme, ...), custom_call_target="tpu_custom_call", output_to_operand_aliasing={{0}: (0, {}), {1}: (11, {}), {2}: (12, {}), {3}: (13, {})} | custom-call | flops 1000000 | bytes 11526144 | tf_op jit(solution)/shard_map/pallas_call | solution.py:37
  63.8 2.5 %collective-permute-start.17 = (f32[9,56,128]{2,1,0:T(8,128)S(1)}, f32[9,56,128]{2,1,0:T(8,128)S(1)}, u32[]{:S(2)}, u32[]{:S(2)}) collective-permute-start(f32[9,56,128]{2,1,0:T(8,128)S(1)} %get-tuple-element.89), channel_id=1, source_target_pairs={{4,8},{12,16},{20,24},{8,4},{16,12},{24,20},{5,9},{13,17},{21,25},... | collective-permute-start | bytes 774152 | tf_op jit(solution)/shard_map/ppermute | solution.py:354
  67.0 3.7 %collective-permute-done.15.refs_3_ = f32[9,72,128]{2,1,0:T(8,128)S(1)} collective-permute-done((f32[9,72,128]{2,1,0:T(8,128)S(1)}, f32[9,72,128]{2,1,0:T(8,128)S(1)}, u32[]{:S(2)}, u32[]{:S(2)}) %collective-permute-start.15) | collective-permute-done | bytes 331808 | tf_op jit(solution)/shard_map/ppermute | solution.py:354
  70.7 2.3 %shard_map.71 = (f32[3,10,144,128]{3,2,1,0:T(8,128)S(1)}, f32[3,7,144,128]{3,2,1,0:T(8,128)S(1)}, f32[3,4,144,128]{3,2,1,0:T(8,128)S(1)}, f32[3,10,144,128]{3,2,...) custom-call(f32[3,10,144,128]{3,2,1,0:T(8,128)S(1)} %get-tuple-element.83., ...), custom_call_target="tpu_custom_call", output_to_operand_aliasing={{0}: (0, {})} | custom-call | flops 1000000 | bytes 7102464 | tf_op jit(solution)/shard_map/pallas_call | solution.py:37
  73.0 4.0 %collective-permute-start.19 = (f32[9,64,128]{2,1,0:T(8,128)S(1)}, f32[9,64,128]{2,1,0:T(8,128)S(1)}, u32[]{:S(2)}, u32[]{:S(2)}) collective-permute-start(f32[9,64,128]{2,1,0:T(8,128)S(1)} %get-tuple-element.97), channel_id=1, source_target_pairs={{4,8},{12,16},{20,24},{8,4},{16,12},{24,20},{5,9},{13,17},{21,25},... | collective-permute-start | bytes 884744 | tf_op jit(solution)/shard_map/ppermute | solution.py:354
  77.1 2.1 %shard_map.72 = (f32[3,10,144,128]{3,2,1,0:T(8,128)S(1)}, f32[3,7,144,128]{3,2,1,0:T(8,128)S(1)}, f32[3,4,144,128]{3,2,1,0:T(8,128)S(1)}, f32[3,10,144,128]{3,2,...) custom-call(f32[3,10,144,128]{3,2,1,0:T(8,128)S(1)} %get-tuple-eleme, ...), custom_call_target="tpu_custom_call", output_to_operand_aliasing={{0}: (0, {}), {1}: (11, {}), {2}: (12, {}), {3}: (13, {})} | custom-call | flops 1000000 | bytes 11599872 | tf_op jit(solution)/shard_map/pallas_call | solution.py:37
  79.2 2.8 %collective-permute-start.21 = (f32[9,64,128]{2,1,0:T(8,128)S(1)}, f32[9,64,128]{2,1,0:T(8,128)S(1)}, u32[]{:S(2)}, u32[]{:S(2)}) collective-permute-start(f32[9,64,128]{2,1,0:T(8,128)S(1)} %get-tuple-element.100), channel_id=1, source_target_pairs={{4,8},{12,16},{20,24},{8,4},{16,12},{24,20},{5,9},{13,17},{21,25},... | collective-permute-start | bytes 884744 | tf_op jit(solution)/shard_map/ppermute | solution.py:354
  82.2 2.0 %shard_map.73 = (f32[3,10,144,128]{3,2,1,0:T(8,128)S(1)}, f32[3,7,144,128]{3,2,1,0:T(8,128)S(1)}, f32[3,4,144,128]{3,2,1,0:T(8,128)S(1)}, f32[3,10,144,128]{3,2,...) custom-call(f32[3,10,144,128]{3,2,1,0:T(8,128)S(1)} %get-tuple-element.94., ...), custom_call_target="tpu_custom_call", output_to_operand_aliasing={{0}: (0, {})} | custom-call | flops 1000000 | bytes 7028736 | tf_op jit(solution)/shard_map/pallas_call | solution.py:37
  84.2 4.8 %collective-permute-done.21.refs_3_ = f32[9,64,128]{2,1,0:T(8,128)S(1)} collective-permute-done((f32[9,64,128]{2,1,0:T(8,128)S(1)}, f32[9,64,128]{2,1,0:T(8,128)S(1)}, u32[]{:S(2)}, u32[]{:S(2)}) %collective-permute-start.21) | collective-permute-done | bytes 294944 | tf_op jit(solution)/shard_map/ppermute | solution.py:354
  89.0 2.3 %shard_map.74 = (f32[3,10,144,128]{3,2,1,0:T(8,128)S(1)}, f32[3,7,144,128]{3,2,1,0:T(8,128)S(1)}, f32[3,4,144,128]{3,2,1,0:T(8,128)S(1)}, f32[3,10,144,128]{3,2,...) custom-call(f32[3,10,144,128]{3,2,1,0:T(8,128)S(1)} %get-tuple-eleme, ...), custom_call_target="tpu_custom_call", output_to_operand_aliasing={{0}: (0, {}), {1}: (11, {}), {2}: (12, {}), {3}: (13, {})} | custom-call | flops 1000000 | bytes 11673600 | tf_op jit(solution)/shard_map/pallas_call | solution.py:37
  91.4 4.8 %collective-permute-start.25 = (f32[5,72,128]{2,1,0:T(8,128)S(1)}, f32[5,72,128]{2,1,0:T(8,128)S(1)}, u32[]{:S(2)}, u32[]{:S(2)}) collective-permute-start(f32[5,72,128]{2,1,0:T(8,128)S(1)} %get-tuple-element.111), channel_id=1, source_target_pairs={{4,8},{12,16},{20,24},{8,4},{16,12},{24,20},{5,9},{13,17},{21,25},... | collective-permute-start | bytes 552968 | tf_op jit(solution)/shard_map/ppermute | solution.py:354
  96.3 1.9 %collective-permute-start.23 = (f32[5,56,128]{2,1,0:T(8,128)S(1)}, f32[5,56,128]{2,1,0:T(8,128)S(1)}, u32[]{:S(2)}, u32[]{:S(2)}) collective-permute-start(f32[5,56,128]{2,1,0:T(8,128)S(1)} %get-tuple-element.108), channel_id=1, source_target_pairs={{4,8},{12,16},{20,24},{8,4},{16,12},{24,20},{5,9},{13,17},{21,25},... | collective-permute-start | bytes 430088 | tf_op jit(solution)/shard_map/ppermute | solution.py:354
  98.8 4.8 %collective-permute-done.23.refs_3_ = f32[5,56,128]{2,1,0:T(8,128)S(1)} collective-permute-done((f32[5,56,128]{2,1,0:T(8,128)S(1)}, f32[5,56,128]{2,1,0:T(8,128)S(1)}, u32[]{:S(2)}, u32[]{:S(2)}) %collective-permute-start.23) | collective-permute-done | bytes 143392 | tf_op jit(solution)/shard_map/ppermute | solution.py:354
  103.6 1.6 %shard_map.75 = (f32[3,10,144,128]{3,2,1,0:T(8,128)S(1)}, f32[1,9,4,128,128]{4,3,2,1,0:T(8,128)}) custom-call(f32[3,10,144,128]{3,2,1,0:T(8,128)S(1)} %get-tuple-element.105.refs_0_, f32[3,7,144,128]{3,2,1,0:T(8,128)S(1)} %get-tuple-element.106.refs_1_, f32[3,4,144,128]{3,2,1,0:T(8,128)S(1)} %get-tuple-element.107.refs_2_, ...), custom_call_target="tpu_custom_call", output_to_operand_aliasing={{0}: (0, {})} | custom-call | flops 1000000 | bytes 6725632 | tf_op jit(solution)/shard_map/pallas_call | solution.py:37
  105.2 2.1 %shard_map.76 = (f32[3,10,144,128]{3,2,1,0:T(8,128)S(1)}, f32[1,9,4,128,128]{4,3,2,1,0:T(8,128)}) custom-call(f32[3,10,144,128]{3,2,1,0:T(8,128)S(1)} %get-tuple-element.110.refs_0_, f32[3,7,144,128]{3,2,1,0:T(8,128)S(1)} %get-tuple-element.106.refs_1_, ...), custom_call_target="tpu_custom_call", output_to_operand_aliasing={{0}: (0, {}), {1}: (11, {})} | custom-call | flops 1000000 | bytes 9166848 | tf_op jit(solution)/shard_map/pallas_call | solution.py:37
  (51 shorter events, 8.8 us)
Async XLA Ops:
  0.0 19.4 %copy-start = (f32[1,9,4,128,128]{4,3,2,1,0:T(8,128)S(1)}, f32[1,9,4,128,128]{4,3,2,1,0:T(8,128)}, u32[]{:S(2)}) copy-start(f32[1,9,4,128,128]{4,3,2,1,0:T(8,128)} %refs_0_.3) | copy-start | bytes 7077892
  0.0 10.1 %copy-start.3 = (s32[4,8,4,4]{1,3,2,0:T(4,128)S(1)}, s32[4,8,4,4]{1,3,2,0:T(4,128)}, u32[]{:S(2)}) copy-start(s32[4,8,4,4]{1,3,2,0:T(4,128)} %param.11) | copy-start | bytes 6148
  2.6 21.1 %collective-permute-start = (f32[832,128]{1,0:T(8,128)}, f32[832,128]{1,0:T(8,128)S(1)}, u32[]{:S(2)}, u32[]{:S(2)}) collective-permute-start(f32[832,128]{1,0:T(8,128)} %get-tuple-element.63), channel_id=1, source_target_pairs={{4,8},{12,16},{20,24},{8,4},{16,12},{24,20},{5,9},{13,17},{21,25},... | collective-permute-start | bytes 1277960 | tf_op jit(solution)/shard_map/ppermute | solution.py:354
  6.3 17.4 %collective-permute-start.1 = (f32[832,128]{1,0:T(8,128)}, f32[832,128]{1,0:T(8,128)S(1)}, u32[]{:S(2)}, u32[]{:S(2)}) collective-permute-start(f32[832,128]{1,0:T(8,128)} %get-tuple-element.64), channel_id=1, source_target_pairs={{0,4},{8,12},{16,20},{24,28},{4,0},{12,8},{20,16},{28,24},{1,5},{9... | collective-permute-start | bytes 1277960 | tf_op jit(solution)/shard_map/ppermute | solution.py:354
  6.3 6.9 %collective-permute-start.4 = (f32[8,32,128]{2,1,0:T(8,128)}, f32[8,32,128]{2,1,0:T(8,128)S(1)}, u32[]{:S(2)}, u32[]{:S(2)}) collective-permute-start(f32[8,32,128]{2,1,0:T(8,128)} %get-tuple-element.65.refs_6_), channel_id=1, source_target_pairs={{0,3},{1,2},{2,1},{3,0},{4,7},{5,6},{6,5},{7,4},{8,11},{9,10},{10,... | collective-permute-start | bytes 393224 | tf_op jit(solution)/shard_map/ppermute | solution.py:357
  9.7 13.9 %collective-permute-start.3 = (f32[8,32,128]{2,1,0:T(8,128)}, f32[8,32,128]{2,1,0:T(8,128)}, u32[]{:S(2)}, u32[]{:S(2)}) collective-permute-start(f32[8,32,128]{2,1,0:T(8,128)} %get-tuple-element.65.refs_6_), channel_id=1, source_target_pairs={{0,2},{1,3},{2,0},{3,1},{4,6},{5,7},{6,4},{7,5},{8,10},{9,11},{10,... | collective-permute-start | bytes 393224 | tf_op jit(solution)/shard_map/ppermute | solution.py:357
  9.7 13.9 %collective-permute-start.2 = (f32[8,32,128]{2,1,0:T(8,128)}, f32[8,32,128]{2,1,0:T(8,128)}, u32[]{:S(2)}, u32[]{:S(2)}) collective-permute-start(f32[8,32,128]{2,1,0:T(8,128)} %get-tuple-element.65.refs_6_), channel_id=1, source_target_pairs={{0,1},{1,0},{2,3},{3,2},{4,5},{5,4},{6,7},{7,6},{8,9},{9,8},{10,11... | collective-permute-start | bytes 393224 | tf_op jit(solution)/shard_map/ppermute | solution.py:357
  13.2 0.6 copy-start.1
  13.9 19.7 %collective-permute-start.9 = (f32[8,32,128]{2,1,0:T(8,128)S(1)}, f32[8,32,128]{2,1,0:T(8,128)S(1)}, u32[]{:S(2)}, u32[]{:S(2)}) collective-permute-start(f32[8,32,128]{2,1,0:T(8,128)S(1)} %get-tuple-element.73.refs_0_), channel_id=1, source_target_pairs={{0,3},{1,2},{2,1},{3,0},{4,7},{5,6},{6,5},{7,4},{8,11},{9,10},{10,... | collective-permute-start | bytes 393224 | tf_op jit(solution)/shard_map/ppermute | solution.py:357
  19.4 4.2 %copy-start.2 = (f32[8,32,128]{2,1,0:T(8,128)S(1)}, f32[8,32,128]{2,1,0:T(8,128)}, u32[]{:S(2)}) copy-start(f32[8,32,128]{2,1,0:T(8,128)} %copy-done.1) | copy-start | bytes 393220
  23.6 11.8 %collective-permute-start.8 = (f32[8,32,128]{2,1,0:T(8,128)S(1)}, f32[8,32,128]{2,1,0:T(8,128)S(1)}, u32[]{:S(2)}, u32[]{:S(2)}) collective-permute-start(f32[8,32,128]{2,1,0:T(8,128)S(1)} %get-tuple-element.73.refs_0_), channel_id=1, source_target_pairs={{0,2},{1,3},{2,0},{3,1},{4,6},{5,7},{6,4},{7,5},{8,10},{9,11},{10,... | collective-permute-start | bytes 393224 | tf_op jit(solution)/shard_map/ppermute | solution.py:357
  26.0 29.2 %collective-permute-start.5 = (f32[9,80,128]{2,1,0:T(8,128)S(1)}, f32[9,80,128]{2,1,0:T(8,128)S(1)}, u32[]{:S(2)}, u32[]{:S(2)}) collective-permute-start(f32[9,80,128]{2,1,0:T(8,128)S(1)} %get-tuple-element.71), channel_id=1, source_target_pairs={{4,8},{12,16},{20,24},{8,4},{16,12},{24,20},{5,9},{13,17},{21,25},... | collective-permute-start | bytes 1105928 | tf_op jit(solution)/shard_map/ppermute | solution.py:354
  32.5 22.7 %collective-permute-start.6 = (f32[9,80,128]{2,1,0:T(8,128)S(1)}, f32[9,80,128]{2,1,0:T(8,128)S(1)}, u32[]{:S(2)}, u32[]{:S(2)}) collective-permute-start(f32[9,80,128]{2,1,0:T(8,128)S(1)} %get-tuple-element.72), channel_id=1, source_target_pairs={{0,4},{8,12},{16,20},{24,28},{4,0},{12,8},{20,16},{28,24},{1,5},{9... | collective-permute-start | bytes 1105928 | tf_op jit(solution)/shard_map/ppermute | solution.py:354
  32.7 14.7 %collective-permute-start.12 = (f32[384,128]{1,0:T(8,128)S(1)}, f32[384,128]{1,0:T(8,128)S(1)}, u32[]{:S(2)}, u32[]{:S(2)}) collective-permute-start(f32[384,128]{1,0:T(8,128)S(1)} %pad_maximum_fusion.refs_4_), channel_id=1, source_target_pairs={{0,3},{1,2},{2,1},{3,0},{4,7},{5,6},{6,5},{7,4},{8,11},{9,10},{10,... | collective-permute-start | bytes 589832 | tf_op jit(solution)/shard_map/ppermute | solution.py:357
  33.6 19.2 %collective-permute-start.11 = (f32[384,128]{1,0:T(8,128)S(1)}, f32[384,128]{1,0:T(8,128)S(1)}, u32[]{:S(2)}, u32[]{:S(2)}) collective-permute-start(f32[384,128]{1,0:T(8,128)S(1)} %pad_maximum_fusion.refs_4_), channel_id=1, source_target_pairs={{0,2},{1,3},{2,0},{3,1},{4,6},{5,7},{6,4},{7,5},{8,10},{9,11},{10,... | collective-permute-start | bytes 589832 | tf_op jit(solution)/shard_map/ppermute | solution.py:357
  35.5 9.0 %collective-permute-start.7 = (f32[8,32,128]{2,1,0:T(8,128)S(1)}, f32[8,32,128]{2,1,0:T(8,128)S(1)}, u32[]{:S(2)}, u32[]{:S(2)}) collective-permute-start(f32[8,32,128]{2,1,0:T(8,128)S(1)} %get-tuple-element.73.refs_0_), channel_id=1, source_target_pairs={{0,1},{1,0},{2,3},{3,2},{4,5},{5,4},{6,7},{7,6},{8,9},{9,8},{10,11... | collective-permute-start | bytes 393224 | tf_op jit(solution)/shard_map/ppermute | solution.py:357
  44.4 10.7 %collective-permute-start.10 = (f32[384,128]{1,0:T(8,128)S(1)}, f32[384,128]{1,0:T(8,128)S(1)}, u32[]{:S(2)}, u32[]{:S(2)}) collective-permute-start(f32[384,128]{1,0:T(8,128)S(1)} %pad_maximum_fusion.refs_4_), channel_id=1, source_target_pairs={{0,1},{1,0},{2,3},{3,2},{4,5},{5,4},{6,7},{7,6},{8,9},{9,8},{10,11... | collective-permute-start | bytes 589832 | tf_op jit(solution)/shard_map/ppermute | solution.py:357
  47.4 14.5 %collective-permute-start.13 = (f32[9,48,128]{2,1,0:T(8,128)S(1)}, f32[9,48,128]{2,1,0:T(8,128)S(1)}, u32[]{:S(2)}, u32[]{:S(2)}) collective-permute-start(f32[9,48,128]{2,1,0:T(8,128)S(1)} %get-tuple-element.78), channel_id=1, source_target_pairs={{4,8},{12,16},{20,24},{8,4},{16,12},{24,20},{5,9},{13,17},{21,25},... | collective-permute-start | bytes 663560 | tf_op jit(solution)/shard_map/ppermute | solution.py:354
  52.8 9.1 %collective-permute-start.14 = (f32[9,48,128]{2,1,0:T(8,128)S(1)}, f32[9,48,128]{2,1,0:T(8,128)S(1)}, u32[]{:S(2)}, u32[]{:S(2)}) collective-permute-start(f32[9,48,128]{2,1,0:T(8,128)S(1)} %get-tuple-element.79), channel_id=1, source_target_pairs={{0,4},{8,12},{16,20},{24,28},{4,0},{12,8},{20,16},{28,24},{1,5},{9... | collective-permute-start | bytes 663560 | tf_op jit(solution)/shard_map/ppermute | solution.py:354
  57.8 12.9 %collective-permute-start.15 = (f32[9,72,128]{2,1,0:T(8,128)S(1)}, f32[9,72,128]{2,1,0:T(8,128)S(1)}, u32[]{:S(2)}, u32[]{:S(2)}) collective-permute-start(f32[9,72,128]{2,1,0:T(8,128)S(1)} %get-tuple-element.86), channel_id=1, source_target_pairs={{4,8},{12,16},{20,24},{8,4},{16,12},{24,20},{5,9},{13,17},{21,25},... | collective-permute-start | bytes 995336 | tf_op jit(solution)/shard_map/ppermute | solution.py:354
  61.8 8.9 %collective-permute-start.16 = (f32[9,72,128]{2,1,0:T(8,128)S(1)}, f32[9,72,128]{2,1,0:T(8,128)S(1)}, u32[]{:S(2)}, u32[]{:S(2)}) collective-permute-start(f32[9,72,128]{2,1,0:T(8,128)S(1)} %get-tuple-element.87), channel_id=1, source_target_pairs={{0,4},{8,12},{16,20},{24,28},{4,0},{12,8},{20,16},{28,24},{1,5},{9... | collective-permute-start | bytes 995336 | tf_op jit(solution)/shard_map/ppermute | solution.py:354
  63.8 13.3 %collective-permute-start.17 = (f32[9,56,128]{2,1,0:T(8,128)S(1)}, f32[9,56,128]{2,1,0:T(8,128)S(1)}, u32[]{:S(2)}, u32[]{:S(2)}) collective-permute-start(f32[9,56,128]{2,1,0:T(8,128)S(1)} %get-tuple-element.89), channel_id=1, source_target_pairs={{4,8},{12,16},{20,24},{8,4},{16,12},{24,20},{5,9},{13,17},{21,25},... | collective-permute-start | bytes 774152 | tf_op jit(solution)/shard_map/ppermute | solution.py:354
  66.2 10.8 %collective-permute-start.18 = (f32[9,56,128]{2,1,0:T(8,128)S(1)}, f32[9,56,128]{2,1,0:T(8,128)S(1)}, u32[]{:S(2)}, u32[]{:S(2)}) collective-permute-start(f32[9,56,128]{2,1,0:T(8,128)S(1)} %get-tuple-element.90), channel_id=1, source_target_pairs={{0,4},{8,12},{16,20},{24,28},{4,0},{12,8},{20,16},{28,24},{1,5},{9... | collective-permute-start | bytes 774152 | tf_op jit(solution)/shard_map/ppermute | solution.py:354
  73.0 9.2 %collective-permute-start.19 = (f32[9,64,128]{2,1,0:T(8,128)S(1)}, f32[9,64,128]{2,1,0:T(8,128)S(1)}, u32[]{:S(2)}, u32[]{:S(2)}) collective-permute-start(f32[9,64,128]{2,1,0:T(8,128)S(1)} %get-tuple-element.97), channel_id=1, source_target_pairs={{4,8},{12,16},{20,24},{8,4},{16,12},{24,20},{5,9},{13,17},{21,25},... | collective-permute-start | bytes 884744 | tf_op jit(solution)/shard_map/ppermute | solution.py:354
  77.0 5.3 %collective-permute-start.20 = (f32[9,64,128]{2,1,0:T(8,128)S(1)}, f32[9,64,128]{2,1,0:T(8,128)S(1)}, u32[]{:S(2)}, u32[]{:S(2)}) collective-permute-start(f32[9,64,128]{2,1,0:T(8,128)S(1)} %get-tuple-element.98), channel_id=1, source_target_pairs={{0,4},{8,12},{16,20},{24,28},{4,0},{12,8},{20,16},{28,24},{1,5},{9... | collective-permute-start | bytes 884744 | tf_op jit(solution)/shard_map/ppermute | solution.py:354
  79.2 9.8 %collective-permute-start.21 = (f32[9,64,128]{2,1,0:T(8,128)S(1)}, f32[9,64,128]{2,1,0:T(8,128)S(1)}, u32[]{:S(2)}, u32[]{:S(2)}) collective-permute-start(f32[9,64,128]{2,1,0:T(8,128)S(1)} %get-tuple-element.100), channel_id=1, source_target_pairs={{4,8},{12,16},{20,24},{8,4},{16,12},{24,20},{5,9},{13,17},{21,25},... | collective-permute-start | bytes 884744 | tf_op jit(solution)/shard_map/ppermute | solution.py:354
  82.0 7.0 %collective-permute-start.22 = (f32[9,64,128]{2,1,0:T(8,128)S(1)}, f32[9,64,128]{2,1,0:T(8,128)S(1)}, u32[]{:S(2)}, u32[]{:S(2)}) collective-permute-start(f32[9,64,128]{2,1,0:T(8,128)S(1)} %get-tuple-element.101), channel_id=1, source_target_pairs={{0,4},{8,12},{16,20},{24,28},{4,0},{12,8},{20,16},{28,24},{1,5},{9... | collective-permute-start | bytes 884744 | tf_op jit(solution)/shard_map/ppermute | solution.py:354
  91.4 13.8 %collective-permute-start.25 = (f32[5,72,128]{2,1,0:T(8,128)S(1)}, f32[5,72,128]{2,1,0:T(8,128)S(1)}, u32[]{:S(2)}, u32[]{:S(2)}) collective-permute-start(f32[5,72,128]{2,1,0:T(8,128)S(1)} %get-tuple-element.111), channel_id=1, source_target_pairs={{4,8},{12,16},{20,24},{8,4},{16,12},{24,20},{5,9},{13,17},{21,25},... | collective-permute-start | bytes 552968 | tf_op jit(solution)/shard_map/ppermute | solution.py:354
  96.2 9.0 %collective-permute-start.26 = (f32[5,72,128]{2,1,0:T(8,128)S(1)}, f32[5,72,128]{2,1,0:T(8,128)S(1)}, u32[]{:S(2)}, u32[]{:S(2)}) collective-permute-start(f32[5,72,128]{2,1,0:T(8,128)S(1)} %get-tuple-element.112), channel_id=1, source_target_pairs={{0,4},{8,12},{16,20},{24,28},{4,0},{12,8},{20,16},{28,24},{1,5},{9... | collective-permute-start | bytes 552968 | tf_op jit(solution)/shard_map/ppermute | solution.py:354
  96.3 7.3 %collective-permute-start.23 = (f32[5,56,128]{2,1,0:T(8,128)S(1)}, f32[5,56,128]{2,1,0:T(8,128)S(1)}, u32[]{:S(2)}, u32[]{:S(2)}) collective-permute-start(f32[5,56,128]{2,1,0:T(8,128)S(1)} %get-tuple-element.108), channel_id=1, source_target_pairs={{4,8},{12,16},{20,24},{8,4},{16,12},{24,20},{5,9},{13,17},{21,25},... | collective-permute-start | bytes 430088 | tf_op jit(solution)/shard_map/ppermute | solution.py:354
  98.2 5.4 %collective-permute-start.24 = (f32[5,56,128]{2,1,0:T(8,128)S(1)}, f32[5,56,128]{2,1,0:T(8,128)S(1)}, u32[]{:S(2)}, u32[]{:S(2)}) collective-permute-start(f32[5,56,128]{2,1,0:T(8,128)S(1)} %get-tuple-element.109), channel_id=1, source_target_pairs={{0,4},{8,12},{16,20},{24,28},{4,0},{12,8},{20,16},{28,24},{1,5},{9... | collective-permute-start | bytes 430088 | tf_op jit(solution)/shard_map/ppermute | solution.py:354

commit v2 on v1

--- a/solution.py
+++ b/solution.py
@@ -18,7 +18,8 @@
 F32 = jnp.float32
 
 
-def call(body, ins, outs, alias=(), scratch=(), anywhere=(), flops=1_000_000):
+def call(body, ins, outs, alias=(), scratch=(), anywhere=(), us=0.5, waits=()):
+    ins = dict(ins, **{"wait%d" % i: a for i, a in enumerate(waits)})
     in_names, out_names = list(ins), list(outs)
 
     def kernel(*refs):
@@ -30,7 +31,6 @@
             names[name] = ref
         body(names, *refs[len(in_names) + len(out_names):])
 
-    size = sum(4 * a.size for a in ins.values())
     ins = {name: pltpu.with_memory_space_constraint(a, pltpu.HBM) if name in anywhere
            else pltpu.with_memory_space_constraint(a, pltpu.VMEM) if name in alias
            else a for name, a in ins.items()}
@@ -38,12 +38,12 @@
         kernel,
         out_shape=[pltpu.HBM(shape, F32) if name in anywhere else pltpu.VMEM(shape, F32)
                    for name, shape in outs.items()],
-        in_specs=[ANY if name in anywhere else VMEM for name in in_names],
+        in_specs=[ANY if name in anywhere or name[:4] == "wait" else VMEM for name in in_names],
         out_specs=[ANY if name in anywhere else VMEM for name in out_names],
         scratch_shapes=list(scratch),
         input_output_aliases={in_names.index(n): out_names.index(n) for n in alias},
         compiler_params=pltpu.CompilerParams(vmem_limit_bytes=24 * 2**20),
-        cost_estimate=pl.CostEstimate(flops=flops, bytes_accessed=size, transcendentals=0),
+        cost_estimate=pl.CostEstimate(flops=int(us * 1e9), bytes_accessed=int(us * 3.6e6), transcendentals=0),
     )(*ins.values())
     return dict(zip(out_names, results))
 
@@ -138,6 +138,25 @@
         above = [(0, n + 3), (1, n + 4), (1, n + 3), (2, n + 3), (2, n + 4)]
         return list(zip(top, bottom, below, above))
 
+    def inner_forcing(self, refs, sh, so):
+        z = Shifts(self.lanes)
+
+        def tile(k, carry):
+            start = pl.multiple_of(k * ROWS, ROWS)
+            rows = pl.ds(start, ROWS)
+            xy = tile_reader(sh, 1, start)
+            xz = tile_reader(sh, 2, start)
+            yy = tile_reader(so, 0, start)
+            zz = tile_reader(so, 1, start)
+            yz = tile_reader(so, 2, start)
+            for i in range(self.cx):
+                refs["inner"][0, i, rows, :] = bwd(lambda d: xy(i + 2, d)) + z.bz(xz(i + 2))
+                refs["inner"][1, i, rows, :] = fwd(lambda d: yy(i, d)) + z.bz(yz(i))
+                refs["inner"][2, i, rows, :] = bwd(lambda d: yz(i, d)) + z.fz(zz(i))
+            return carry
+
+        lax.fori_loop(0, self.tiles, tile, 0)
+
     def velocity(self, refs, moment, which, sh, so, previous):
         first, last = self.chunk(moment, which)
         z = Shifts(self.lanes)
@@ -151,12 +170,21 @@
             yy = tile_reader(so, 0, start)
             zz = tile_reader(so, 1, start)
             yz = tile_reader(so, 2, start)
+            rows = pl.ds(start, ROWS)
             for i in range(self.cx):
                 keep, gain = factors(here, refs["damp"][i, pl.ds(start, ROWS), :])
                 gain = gain * refs["buoy"][i, pl.ds(start, ROWS), :]
-                gx = fwd(lambda d: xx(i + 1 + d)) + bwd(lambda d: xy(i + 2, d)) + z.bz(xz(i + 2))
-                gy = bwd(lambda d: xy(i + 2 + d)) + fwd(lambda d: yy(i, d)) + z.bz(yz(i))
-                gz = bwd(lambda d: xz(i + 2 + d)) + bwd(lambda d: yz(i, d)) + z.fz(zz(i))
+                gx = fwd(lambda d: xx(i + 1 + d))
+                gy = bwd(lambda d: xy(i + 2 + d))
+                gz = bwd(lambda d: xz(i + 2 + d))
+                if "inner" in refs:
+                    gx = gx + refs["inner"][0, i, rows, :]
+                    gy = gy + refs["inner"][1, i, rows, :]
+                    gz = gz + refs["inner"][2, i, rows, :]
+                else:
+                    gx = gx + bwd(lambda d: xy(i + 2, d)) + z.bz(xz(i + 2))
+                    gy = gy + fwd(lambda d: yy(i, d)) + z.bz(yz(i))
+                    gz = gz + bwd(lambda d: yz(i, d)) + z.fz(zz(i))
                 for f, g in enumerate((gx, gy, gz)):
                     refs["vel_next"][f, REACH + i, pl.ds(start + PAD, ROWS), :] = (
                         keep * previous(f, i, start) + gain * g
@@ -279,8 +307,7 @@
 MODEL_SLOTS = 6
 
 
-def pack(cx, panel_rows, rows, refs, sems):
-    odd = odd_slab()
+def mover(sems):
     copies = []
 
     def move(src, dst):
@@ -288,27 +315,29 @@
         copy.start()
         copies.append(copy)
 
+    return move, copies
+
+
+def pack(cx, refs, sems):
+    odd = odd_slab()
+    move, copies = mover(sems)
+    for i, name in enumerate(("buoy", "q", "lam", "mu")):
+        move(refs[name], refs["first" if i < 2 else "second"].at[pl.ds(i % 2 * cx, cx)])
+    for slot, name in enumerate(("lam", "lam", "mu", "mu", "q", "q")):
+        move(refs[name].at[pick(odd, cx - 2 + slot % 2, slot % 2)], refs["edge"].at[slot])
     top = [(3, cx - 1), (6, cx - 2), (6, cx - 1), (7, cx - 2), (7, cx - 1)]
     bottom = [(3, 0), (3, 1), (6, 0), (7, 0), (7, 0)]
-    for name, flag in (("far", odd), ("near", jnp.logical_not(odd))):
+    for name, flag in (("near", jnp.logical_not(odd)), ("far", odd)):
         for slot in range(STRESS_SLOTS):
             field = pick(flag, top[slot][0], bottom[slot][0])
             layer = pick(flag, top[slot][1], bottom[slot][1])
-            move(refs["wave"].at[0, field, layer], refs[name].at[pl.ds(slot * rows, rows)])
-        base = STRESS_SLOTS * rows
-        for slot in range(MODEL_SLOTS):
-            array = refs[("lam", "lam", "mu", "mu", "q", "q")[slot]]
-            layer = pick(flag, cx - 2 + slot % 2, slot % 2)
-            move(array.at[layer], refs[name].at[pl.ds(base + slot * panel_rows, panel_rows)])
-    for i, name in enumerate(("buoy", "q")):
-        move(refs[name], refs["first"].at[pl.ds(i * cx, cx)])
-    for i, name in enumerate(("lam", "mu")):
-        move(refs[name], refs["second"].at[pl.ds(i * cx, cx)])
+            move(refs["wave"].at[0, field, layer], refs[name].at[slot])
     for copy in copies:
         copy.wait()
 
 
-def prepare(cx, rows, refs):
+def prepare(plan, refs):
+    cx, rows = plan.cx, plan.rows
     zero_pads(refs["sh"], rows)
     zero_pads(refs["so"], rows)
     inner = pl.ds(PAD, rows)
@@ -321,22 +350,40 @@
     for field in range(3):
         for i in range(cx):
             refs["old"][field, i] = refs["wave"][0, field, i]
-
-
-def panel_place(k, shots, panel_rows):
-    return pl.ds(pl.multiple_of(partner(lax.axis_index("shot"), k, shots) * panel_rows, panel_rows), panel_rows)
-
-
-def partner(index, k, shots):
+    plan.inner_forcing(refs, refs["sh"], refs["so"])
+    refs["ready"][...] = jnp.zeros(refs["ready"].shape, F32)
+
+
+def after(array, *others):
+    return lax.optimization_barrier((array,) + others)[0]
+
+
+def spread(mine, shots):
+    pairs = lambda k: [(i, i ^ k) for i in range(shots)]
+    if shots == 4:
+        beside = lax.ppermute(mine, "shot", pairs(1))
+        across = lax.ppermute(mine, "shot", pairs(3))
+
+        def finish(*others):
+            handed = lax.ppermute(after(across, beside, *others), "shot", pairs(1))
+            return {0: mine, 1: beside, 2: handed, 3: across}
+
+        return (beside, across), finish
+    turn = lambda k: [(i, (i + k) % shots) for i in range(shots)]
+    swap = shots & (shots - 1) == 0
+    got = {k: lax.ppermute(mine, "shot", pairs(k) if swap else turn(k)) for k in range(1, shots)}
+    return tuple(got.values()), lambda *others: {0: mine, **got}
+
+
+def origin_of(index, k, shots):
     if shots & (shots - 1) == 0:
         return index ^ k
     return lax.rem(index + shots - k, shots)
 
 
-def panel_pairs(k, shots):
-    if shots & (shots - 1) == 0:
-        return [(i, i ^ k) for i in range(shots)]
-    return [(i, (i + k) % shots) for i in range(shots)]
+def panel_place(k, shots, panel_rows):
+    start = origin_of(lax.axis_index("shot"), k, shots) * panel_rows
+    return pl.ds(pl.multiple_of(start, panel_rows), panel_rows)
 
 
 def per_device(cuts_of, shots, slabs, wave, lam, mu, buoy, q, active):
@@ -353,32 +400,30 @@
     def exchange(to_far, to_near):
         return lax.ppermute(to_far, "aper", far), lax.ppermute(to_near, "aper", near)
 
-    def gather(mine):
-        return [mine] + [lax.ppermute(mine, "shot", panel_pairs(k, shots)) for k in range(1, shots)]
-
-    halo_rows = STRESS_SLOTS * rows + MODEL_SLOTS * panel_rows
+    panel = (panel_rows, lanes)
     sent = call(
-        functools.partial(pack, cx, panel_rows, rows),
-        dict(wave=wave, lam=lam, mu=mu, buoy=buoy, q=q),
-        dict(far=(halo_rows, lanes), near=(halo_rows, lanes),
-             first=(2 * cx, panel_rows, lanes), second=(2 * cx, panel_rows, lanes)),
-        scratch=[pltpu.SemaphoreType.DMA((2 * (STRESS_SLOTS + MODEL_SLOTS) + 4,))],
-        anywhere=("wave", "lam", "mu", "buoy", "q"),
+        functools.partial(pack, cx),
+        dict(lam=lam, mu=mu, buoy=buoy, q=q, wave=wave),
+        dict(first=(2 * cx,) + panel, second=(2 * cx,) + panel, edge=(MODEL_SLOTS,) + panel,
+             far=(STRESS_SLOTS, rows, lanes), near=(STRESS_SLOTS, rows, lanes)),
+        scratch=[pltpu.SemaphoreType.DMA((4 + MODEL_SLOTS + 2 * STRESS_SLOTS,))],
+        anywhere=("lam", "mu", "buoy", "q", "wave"), us=0.02,
     )
     halo_far, halo_near = exchange(sent["far"], sent["near"])
-    firsts = gather(sent["first"])
-    seconds = gather(sent["second"])
-    edge = jnp.concatenate([halo_far[STRESS_SLOTS * rows:], halo_near[STRESS_SLOTS * rows:]])
-    edges = gather(edge)
-
+    edge = lax.ppermute(sent["edge"], "aper", far)
     device = lax.axis_index("aper")
     around = lax.dynamic_slice_in_dim(jnp.pad(active, ((0, 0), (1, 1), (0, 0), (0, 0))), device, 3, 1)
     mask = jnp.repeat(around.astype(F32).reshape(steps * 3 * blocks, lane_blocks), lanes // lane_blocks, axis=1)
 
     sh_shape, so_shape = (3, cx + 3, padded, lanes), (3, cx, padded, lanes)
     vel_shape, slab_shape = (3, cx + 2 * REACH, padded, lanes), (cx, rows, lanes)
-    state = call(functools.partial(prepare, cx, rows), dict(wave=wave),
-                 dict(sh=sh_shape, so=so_shape, old=(3,) + slab_shape))
+    state = call(functools.partial(prepare, plan), dict(wave=wave),
+                 dict(sh=sh_shape, so=so_shape, old=(3,) + slab_shape, inner=(3,) + slab_shape, ready=(ROWS, lanes)), us=0.02)
+
+    first_stage, finish = spread(sent["first"], shots)
+    firsts = finish(halo_near, edge, mask, state["ready"])
+    second = jnp.concatenate([sent["second"], after(edge, *first_stage)])
+    _, finish_second = spread(second, shots)
 
     def sends(step, which):
         first, last = plan.chunk(step, which)
@@ -391,18 +436,17 @@
         below = [(0, 0), (1, 0), (1, 1), (2, 0), (2, 1)]
         above = [(0, cx + 1), (0, cx + 2), (1, cx + 2), (2, cx + 2), (2, cx + 2)]
         for slot in range(STRESS_SLOTS):
-            part = pl.ds(slot * rows, rows)
             field = pick(odd, above[slot][0], below[slot][0])
             layer = pick(odd, above[slot][1], below[slot][1])
-            refs["sh"][field, layer, inner, :] = refs["halo_far"][part, :]
+            refs["sh"][field, layer, inner, :] = refs["halo_far"][slot]
             field = pick(odd, below[slot][0], above[slot][0])
             layer = pick(odd, below[slot][1], above[slot][1])
-            refs["sh"][field, layer, inner, :] = refs["halo_near"][part, :]
-        for k in range(shots):
-            place = panel_place(k, shots, panel_rows)
+            refs["sh"][field, layer, inner, :] = refs["halo_near"][slot]
+        for k in firsts:
+            place, got = panel_place(k, shots, panel_rows), refs["first%d" % k]
             for i in range(cx):
-                refs["buoy"][i, place, :] = refs["first%d" % k][i]
-                refs["damp"][i, place, :] = jnp.exp(-DT * refs["first%d" % k][cx + i])
+                refs["buoy"][i, place, :] = got[i]
+                refs["damp"][i, place, :] = jnp.exp(-DT * got[cx + i])
         zero_pads(refs["vel_next"], rows)
         start_chunk(refs, 0)
 
@@ -410,51 +454,63 @@
         plan.velocity(refs, 0, which, refs["sh"], refs["so"],
                       lambda f, i, start: refs["old"][f, i, pl.ds(start, ROWS), :])
 
-    ins = dict(sh=state["sh"], so=state["so"], old=state["old"], mask=mask,
-               halo_far=halo_far, halo_near=halo_near)
-    ins.update({"first%d" % k: a for k, a in enumerate(firsts)})
+    ins = dict(halo_far=halo_far, halo_near=halo_near, mask=mask,
+               **{name: state[name] for name in ("sh", "so", "old", "inner")})
+    ins.update({"first%d" % k: a for k, a in firsts.items()})
     got = call(start_first, ins,
-               dict(sh=sh_shape, buoy=slab_shape, damp=slab_shape, vel_next=vel_shape, **sends(0, 0)),
-               alias=("sh",))
+               dict(sh=sh_shape, buoy=slab_shape, damp=slab_shape, vel_next=vel_shape,
+                    **sends(0, 0)),
+               alias=("sh",), us=1.2)
     sh, so = got["sh"], state["so"]
     model = dict(mask=mask, buoy=got["buoy"], damp=got["damp"])
     arrived = [exchange(got["send_far"], got["send_near"])]
     got = call(lambda refs: start_chunk(refs, 1),
-               dict(sh=sh, so=so, old=state["old"], vel_next=got["vel_next"], **model),
-               dict(vel_next=vel_shape, **sends(0, 1)), alias=("vel_next",))
+               dict(sh=sh, so=so, old=state["old"], inner=state["inner"], vel_next=got["vel_next"], **model),
+               dict(vel_next=vel_shape, **sends(0, 1)), alias=("vel_next",), us=0.8)
     vel = got["vel_next"]
     arrived.append(exchange(got["send_far"], got["send_near"]))
 
+    seconds = finish_second()
+
+    def put_edge(refs, from_above, place, part):
+        for j in range(2):
+            refs["lam"][pick(from_above, cx + 1 + j, 0), place, :] = part(j)
+            refs["mu"][pick(from_above, cx + 2 + j, j), place, :] = part(2 + j)
+            refs["damp_edge"][pick(from_above, 2 + j, j), place, :] = part(4 + j)
+
     def assemble(refs):
         odd = odd_slab()
-        for k in range(shots):
-            place = panel_place(k, shots, panel_rows)
+        for k in seconds:
+            place, got = panel_place(k, shots, panel_rows), refs["second%d" % k]
             for i in range(cx):
-                refs["lam"][i + 1, place, :] = refs["second%d" % k][i]
-                refs["mu"][i + 2, place, :] = refs["second%d" % k][cx + i]
-            for half, flag in ((0, odd), (1, jnp.logical_not(odd))):
-                def part(slot):
-                    return refs["edge%d" % k][pl.ds((half * MODEL_SLOTS + slot) * panel_rows, panel_rows), :]
-                for j in range(2):
-                    layer = pick(flag, cx + 1 + j, 0)
-                    if j == 1:
-                        refs["lam"][layer, place, :] = part(1)
-                    else:
-                        refs["lam"][layer, place, :] = part(0)
-                    refs["mu"][pick(flag, cx + 2 + j, j), place, :] = part(2 + j)
-                    refs["damp_edge"][pick(flag, 2 + j, j), place, :] = jnp.exp(-DT * part(4 + j))
-
-    ins = {"second%d" % k: a for k, a in enumerate(seconds)}
-    ins.update({"edge%d" % k: a for k, a in enumerate(edges)})
-    model.update(call(assemble, ins, dict(lam=(cx + 3, rows, lanes), mu=(cx + 4, rows, lanes),
-                                          damp_edge=(4, rows, lanes))))
+                refs["lam"][i + 1, place, :] = got[i]
+                refs["mu"][i + 2, place, :] = got[cx + i]
+            put_edge(refs, odd, place, lambda slot: jnp.exp(-DT * got[2 * cx + slot])
+                     if slot >= 4 else got[2 * cx + slot])
+        for j in range(2):
+            at = pick(odd, j, cx - 2 + j)
+            refs["send_model"][j] = refs["lam"][at + 1]
+            refs["send_model"][2 + j] = refs["mu"][at + 2]
+            refs["send_model"][4 + j] = refs["damp"][at]
+
+    edges = dict(lam=(cx + 3, rows, lanes), mu=(cx + 4, rows, lanes), damp_edge=(4, rows, lanes))
+    got = call(assemble, dict(damp=model["damp"], **{"second%d" % k: a for k, a in seconds.items()}),
+               dict(send_model=(MODEL_SLOTS, rows, lanes), **edges), us=0.02, waits=(arrived[1][1],))
+    model_near = lax.ppermute(got["send_model"], "aper", near)
+    model.update({name: got[name] for name in edges})
+    vel = call(lambda refs: plan.arrivals(refs, 0, 0),
+               dict(vel=vel, from_far=arrived[0][0], from_near=arrived[0][1]),
+               dict(vel=vel_shape), alias=("vel",), us=20.0)["vel"]
 
     out_shape = wave.shape
     for step in range(steps):
         final = step == steps - 1
 
         def advance(refs, *scratch, which, step=step, final=final):
-            plan.arrivals(refs, step, which)
+            if step == 0 and which == 0:
+                put_edge(refs, jnp.logical_not(odd_slab()), slice(None), lambda slot: refs["model_near"][slot])
+            else:
+                plan.arrivals(refs, step, which)
             if final:
                 plan.finish(refs, step, which, *scratch)
                 return
@@ -475,6 +531,9 @@
             ins = dict(vel=vel, sh=sh, so=so, from_far=arrived[which][0], from_near=arrived[which][1],
                        **model, **carried)
             outs = dict(vel=vel_shape, **nexts)
+            if step == 0 and which == 0:
+                ins.update(model_near=model_near)
+                outs.update(edges)
             scratch = []
             if final:
                 first, last = plan.stress_tiles(step, which)
@@ -482,9 +541,11 @@
                            pltpu.SemaphoreType.DMA((3 + 6 * len(plan.parts(first, last)),))]
             else:
                 outs.update(sends(step + 1, which))
-            got = call(functools.partial(advance, which=which), ins, outs, alias=("vel",) + tuple(carried),
+            got = call(functools.partial(advance, which=which), ins, outs, alias=("vel",) + tuple(carried) + (tuple(edges) if step + which == 0 else ()),
                        scratch=scratch, anywhere=("out",))
             vel = got["vel"]
+            if step == 0 and which == 0:
+                model.update({name: got[name] for name in edges})
             carried = {name: got[name] for name in nexts}
             if not final:
                 following.append(exchange(got["send_far"], got["send_near"]))

time: 109 us -> 89.6 us (0.82)
  the two profiles are of different devices: /device:TPU:3 before, /device:TPU:12 now
where the time goes in v2:
time: 89.6 us; the launch traced here: 89.1 us
  starting transfers between devices  39 us (44%)
  Pallas kernels  24.3 us (27%)
  waiting for transfers between devices  21.1 us (24%)
  local copies, waits for them, and re-layouts  4.27 us (5%)
    ppermute x9, starting transfers between devices, exchange(): lax.ppermute(to_far, 'aper', far)  27.7 us
    pallas_call x14, Pallas kernels, call(): pl.pallas_call(kernel, out_shape=[pltpu.HBM(shape, F32) if name in anywhe...  24.3 us
    ppermute x9, waiting for transfers between devices, exchange(): lax.ppermute(to_far, 'aper', far)  15.2 us
    ppermute x2, starting transfers between devices, spread(): beside = lax.ppermute(mine, 'shot', pairs(1))  4.69 us
    ppermute x1, starting transfers between devices, per_device(): edge = lax.ppermute(sent['edge'], 'aper', far)  2.82 us
    ppermute x2, waiting for transfers between devices, spread(): beside = lax.ppermute(mine, 'shot', pairs(1))  2.06 us
  transfers between devices with their start and end apart: 26, of which 10 were waited for; matrix products, arithmetic and copies ran while one was open for 4% of the time, Pallas kernels for 22%

profile of v2, /device:TPU:12, one launch (start us, length us, event | category | flops | bytes accessed | tf_op | source)
XLA Modules:
  0.0 89.1 jit_solution(511827609165199043)
XLA Ops:
  0.0 2.4 %shard_map.64 = (f32[8,32,128]{2,1,0:T(8,128)S(1)}, f32[8,32,128]{2,1,0:T(8,128)S(1)}, f32[6,32,128]{2,1,0:T(8,128)}, f32[5,128,128]{2,1,0:T(8,128)}, f32[5,128,128]{2,1,0:T(8,128)}) custom-call(f32[4,32,128]{2,1,0:T(8,128)} %refs_0_.2, f32[4,32,128]{2,1,0:T(8,128)} %refs_1_.1, f32[4,32,128]{2,1,0:T(8,128)} %refs_2_.1, f32[4,32,128]{2,1,0:T(8,128)} %refs_3_.1, ...), custom_call_target="tpu_custom_call" | custom-call | flops 20000000 | bytes 72000 | tf_op jit(solution)/shard_map/pallas_call | solution.py:37
  2.5 1.6 %collective-permute-start.3 = (f32[8,32,128]{2,1,0:T(8,128)S(1)}, f32[8,32,128]{2,1,0:T(8,128)}, u32[]{:S(2)}, u32[]{:S(2)}) collective-permute-start(f32[8,32,128]{2,1,0:T(8,128)S(1)} %get-tuple-element.75.refs_7_), channel_id=1, source_target_pairs={{0,3},{1,2},{2,1},{3,0},{4,7},{5,6},{6,5},{7,4},{8,11},{9,10},{10,... | collective-permute-start | bytes 393224 | tf_op jit(solution)/shard_map/ppermute | solution.py:365
  4.2 2.5 %collective-permute-start.2 = (f32[8,32,128]{2,1,0:T(8,128)S(1)}, f32[8,32,128]{2,1,0:T(8,128)S(1)}, u32[]{:S(2)}, u32[]{:S(2)}) collective-permute-start(f32[8,32,128]{2,1,0:T(8,128)S(1)} %get-tuple-element.75.refs_7_), channel_id=1, source_target_pairs={{0,1},{1,0},{2,3},{3,2},{4,5},{5,4},{6,7},{7,6},{8,9},{9,8},{10,11... | collective-permute-start | bytes 393224 | tf_op jit(solution)/shard_map/ppermute | solution.py:364
  6.6 2.8 %collective-permute-start.4 = (f32[6,32,128]{2,1,0:T(8,128)}, f32[6,32,128]{2,1,0:T(8,128)}, u32[]{:S(2)}, u32[]{:S(2)}) collective-permute-start(f32[6,32,128]{2,1,0:T(8,128)} %get-tuple-element.76), channel_id=1, source_target_pairs={{4,8},{12,16},{20,24},{8,4},{16,12},{24,20},{5,9},{13,17},{21,25},... | collective-permute-start | bytes 294920 | tf_op jit(solution)/shard_map/ppermute | solution.py:413
  9.5 3.6 %collective-permute-start = (f32[5,128,128]{2,1,0:T(8,128)}, f32[5,128,128]{2,1,0:T(8,128)S(1)}, u32[]{:S(2)}, u32[]{:S(2)}) collective-permute-start(f32[5,128,128]{2,1,0:T(8,128)} %get-tuple-element.69), channel_id=1, source_target_pairs={{4,8},{12,16},{20,24},{8,4},{16,12},{24,20},{5,9},{13,17},{21,25},... | collective-permute-start | bytes 983048 | tf_op jit(solution)/shard_map/ppermute | solution.py:401
  16.6 2.2 %collective-permute-start.8 = (f32[14,32,128]{2,1,0:T(8,128)S(1)}, f32[14,32,128]{2,1,0:T(8,128)}, u32[]{:S(2)}, u32[]{:S(2)}) collective-permute-start(f32[14,32,128]{2,1,0:T(8,128)S(1)} %constant_dynamic-update-slice_fusion.refs_1_), channel_id=1, source_target_pairs={{0,1},{1,0},{2,3},{3,2},{4,5},{5,4},{6,7},{7,6},{8,9},{9,8},{10,11... | collective-permute-start | bytes 688136 | tf_op jit(solution)/shard_map/ppermute | solution.py:364
  19.7 2.4 %shard_map.65 = (f32[3,7,144,128]{3,2,1,0:T(8,128)S(1)}, f32[3,4,144,128]{3,2,1,0:T(8,128)S(1)}, f32[3,4,128,128]{3,2,1,0:T(8,128)S(1)}, f32[3,4,128,128]{3,2,1,0:T(8,128)S(1)}, f32[8,128]{1,0:T(8,128)}) custom-call(f32[1,9,4,128,128]{4,3,2,1,0:T(8,128)S(1)} %copy-done), custom_call_target="tpu_custom_call" | custom-call | flops 20000000 | bytes 72000 | tf_op jit(solution)/shard_map/pallas_call | solution.py:37
  22.4 1.4 %shard_map.66 = (f32[3,7,144,128]{3,2,1,0:T(8,128)S(1)}, f32[4,128,128]{2,1,0:T(8,128)S(1)}, f32[4,128,128]{2,1,0:T(8,128)S(1)}, f32[3,10,144,128]{3,2,1,0:T(8,1...) custom-call(f32[5,128,128]{2,1,0:T(8,128)S(1)} %collective-permute-done.refs_0_, ...), custom_call_target="tpu_custom_call", output_to_operand_aliasing={{0}: (3, {})} | custom-call | flops 1200000000 | bytes 4320000 | tf_op jit(solution)/shard_map/pallas_call | solution.py:37
  23.8 2.4 %collective-permute-start.6 = (f32[9,80,128]{2,1,0:T(8,128)S(1)}, f32[9,80,128]{2,1,0:T(8,128)S(1)}, u32[]{:S(2)}, u32[]{:S(2)}) collective-permute-start(f32[9,80,128]{2,1,0:T(8,128)S(1)} %get-tuple-element.83), channel_id=1, source_target_pairs={{4,8},{12,16},{20,24},{8,4},{16,12},{24,20},{5,9},{13,17},{21,25},... | collective-permute-start | bytes 1105928 | tf_op jit(solution)/shard_map/ppermute | solution.py:401
  27.0 1.2 %collective-permute-done.9.refs_4_ = f32[14,32,128]{2,1,0:T(8,128)S(1)} collective-permute-done((f32[14,32,128]{2,1,0:T(8,128)S(1)}, f32[14,32,128]{2,1,0:T(8,128)S(1)}, u32[]{:S(2)}, u32[]{:S(2)}) %collective-permute-start.9) | collective-permute-done | bytes 229408 | tf_op jit(solution)/shard_map/ppermute | solution.py:365
  28.1 2.1 %collective-permute-done.8.refs_2_ = f32[14,32,128]{2,1,0:T(8,128)} collective-permute-done((f32[14,32,128]{2,1,0:T(8,128)S(1)}, f32[14,32,128]{2,1,0:T(8,128)}, u32[]{:S(2)}, u32[]{:S(2)}) %collective-permute-start.8) | collective-permute-done | bytes 229408 | tf_op jit(solution)/shard_map/ppermute | solution.py:364
  31.1 4.1 %collective-permute-start.13 = (f32[9,48,128]{2,1,0:T(8,128)S(1)}, f32[9,48,128]{2,1,0:T(8,128)S(1)}, u32[]{:S(2)}, u32[]{:S(2)}) collective-permute-start(f32[9,48,128]{2,1,0:T(8,128)S(1)} %get-tuple-element.94), channel_id=1, source_target_pairs={{4,8},{12,16},{20,24},{8,4},{16,12},{24,20},{5,9},{13,17},{21,25},... | collective-permute-start | bytes 663560 | tf_op jit(solution)/shard_map/ppermute | solution.py:401
  37.4 1.6 %collective-permute-done.12.refs_11_ = f32[6,128,128]{2,1,0:T(8,128)S(1)} collective-permute-done((f32[6,128,128]{2,1,0:T(8,128)S(1)}, f32[6,128,128]{2,1,0:T(8,128)S(1)}, u32[]{:S(2)}, u32[]{:S(2)}) %collective-permute-start.12) | collective-permute-done | bytes 393248 | tf_op jit(solution)/shard_map/ppermute | solution.py:499
  39.0 2.5 %shard_map.70 = (f32[3,10,144,128]{3,2,1,0:T(8,128)S(1)}, f32[3,7,144,128]{3,2,1,0:T(8,128)S(1)}, f32[3,4,144,128]{3,2,1,0:T(8,128)S(1)}, f32[3,10,144,128]{3,2,...) custom-call(f32[3,10,144,128]{3,2,1,0:T(8,128)S(1)} %shard_map.68.re, ...), custom_call_target="tpu_custom_call", output_to_operand_aliasing={{0}: (0, {}), {4}: (8, {}), {5}: (9, {}), {6}: (10, {})} | custom-call | flops 500000000 | bytes 1800000 | tf_op jit(solution)/shard_map/pallas_call | solution.py:37
  41.6 5.7 %collective-permute-start.14 = (f32[9,72,128]{2,1,0:T(8,128)S(1)}, f32[9,72,128]{2,1,0:T(8,128)S(1)}, u32[]{:S(2)}, u32[]{:S(2)}) collective-permute-start(f32[9,72,128]{2,1,0:T(8,128)S(1)} %get-tuple-element.104), channel_id=1, source_target_pairs={{4,8},{12,16},{20,24},{8,4},{16,12},{24,20},{5,9},{13,17},{21,25},... | collective-permute-start | bytes 995336 | tf_op jit(solution)/shard_map/ppermute | solution.py:401
  47.4 1.9 %shard_map.71 = (f32[3,10,144,128]{3,2,1,0:T(8,128)S(1)}, f32[3,7,144,128]{3,2,1,0:T(8,128)S(1)}, f32[3,4,144,128]{3,2,1,0:T(8,128)S(1)}, f32[3,10,144,128]{3,2,...) custom-call(f32[3,10,144,128]{3,2,1,0:T(8,128)S(1)} %get-tuple-eleme, ...), custom_call_target="tpu_custom_call", output_to_operand_aliasing={{0}: (0, {}), {1}: (11, {}), {2}: (12, {}), {3}: (13, {})} | custom-call | flops 500000000 | bytes 1800000 | tf_op jit(solution)/shard_map/pallas_call | solution.py:37
  49.3 2.3 %collective-permute-start.16 = (f32[9,56,128]{2,1,0:T(8,128)S(1)}, f32[9,56,128]{2,1,0:T(8,128)S(1)}, u32[]{:S(2)}, u32[]{:S(2)}) collective-permute-start(f32[9,56,128]{2,1,0:T(8,128)S(1)} %get-tuple-element.107), channel_id=1, source_target_pairs={{4,8},{12,16},{20,24},{8,4},{16,12},{24,20},{5,9},{13,17},{21,25},... | collective-permute-start | bytes 774152 | tf_op jit(solution)/shard_map/ppermute | solution.py:401
  51.7 3.4 %collective-permute-done.14.refs_3_ = f32[9,72,128]{2,1,0:T(8,128)S(1)} collective-permute-done((f32[9,72,128]{2,1,0:T(8,128)S(1)}, f32[9,72,128]{2,1,0:T(8,128)S(1)}, u32[]{:S(2)}, u32[]{:S(2)}) %collective-permute-start.14) | collective-permute-done | bytes 331808 | tf_op jit(solution)/shard_map/ppermute | solution.py:401
  55.2 2.3 %shard_map.72 = (f32[3,10,144,128]{3,2,1,0:T(8,128)S(1)}, f32[3,7,144,128]{3,2,1,0:T(8,128)S(1)}, f32[3,4,144,128]{3,2,1,0:T(8,128)S(1)}, f32[3,10,144,128]{3,2,...) custom-call(f32[3,10,144,128]{3,2,1,0:T(8,128)S(1)} %get-tuple-element.101, ...), custom_call_target="tpu_custom_call", output_to_operand_aliasing={{0}: (0, {})} | custom-call | flops 500000000 | bytes 1800000 | tf_op jit(solution)/shard_map/pallas_call | solution.py:37
  57.4 2.1 %collective-permute-start.18 = (f32[9,64,128]{2,1,0:T(8,128)S(1)}, f32[9,64,128]{2,1,0:T(8,128)S(1)}, u32[]{:S(2)}, u32[]{:S(2)}) collective-permute-start(f32[9,64,128]{2,1,0:T(8,128)S(1)} %get-tuple-element.115), channel_id=1, source_target_pairs={{4,8},{12,16},{20,24},{8,4},{16,12},{24,20},{5,9},{13,17},{21,25},... | collective-permute-start | bytes 884744 | tf_op jit(solution)/shard_map/ppermute | solution.py:401
  59.6 1.1 %collective-permute-done.16.refs_3_ = f32[9,56,128]{2,1,0:T(8,128)S(1)} collective-permute-done((f32[9,56,128]{2,1,0:T(8,128)S(1)}, f32[9,56,128]{2,1,0:T(8,128)S(1)}, u32[]{:S(2)}, u32[]{:S(2)}) %collective-permute-start.16) | collective-permute-done | bytes 258080 | tf_op jit(solution)/shard_map/ppermute | solution.py:401
  60.7 2.1 %shard_map.73 = (f32[3,10,144,128]{3,2,1,0:T(8,128)S(1)}, f32[3,7,144,128]{3,2,1,0:T(8,128)S(1)}, f32[3,4,144,128]{3,2,1,0:T(8,128)S(1)}, f32[3,10,144,128]{3,2,...) custom-call(f32[3,10,144,128]{3,2,1,0:T(8,128)S(1)} %get-tuple-eleme, ...), custom_call_target="tpu_custom_call", output_to_operand_aliasing={{0}: (0, {}), {1}: (11, {}), {2}: (12, {}), {3}: (13, {})} | custom-call | flops 500000000 | bytes 1800000 | tf_op jit(solution)/shard_map/pallas_call | solution.py:37
  62.8 3.3 %collective-permute-start.20 = (f32[9,64,128]{2,1,0:T(8,128)S(1)}, f32[9,64,128]{2,1,0:T(8,128)S(1)}, u32[]{:S(2)}, u32[]{:S(2)}) collective-permute-start(f32[9,64,128]{2,1,0:T(8,128)S(1)} %get-tuple-element.118), channel_id=1, source_target_pairs={{4,8},{12,16},{20,24},{8,4},{16,12},{24,20},{5,9},{13,17},{21,25},... | collective-permute-start | bytes 884744 | tf_op jit(solution)/shard_map/ppermute | solution.py:401
  66.2 3.3 %collective-permute-done.18.refs_3_ = f32[9,64,128]{2,1,0:T(8,128)S(1)} collective-permute-done((f32[9,64,128]{2,1,0:T(8,128)S(1)}, f32[9,64,128]{2,1,0:T(8,128)S(1)}, u32[]{:S(2)}, u32[]{:S(2)}) %collective-permute-start.18) | collective-permute-done | bytes 294944 | tf_op jit(solution)/shard_map/ppermute | solution.py:401
  69.5 2.0 %shard_map.74 = (f32[3,10,144,128]{3,2,1,0:T(8,128)S(1)}, f32[3,7,144,128]{3,2,1,0:T(8,128)S(1)}, f32[3,4,144,128]{3,2,1,0:T(8,128)S(1)}, f32[3,10,144,128]{3,2,...) custom-call(f32[3,10,144,128]{3,2,1,0:T(8,128)S(1)} %get-tuple-element.112, ...), custom_call_target="tpu_custom_call", output_to_operand_aliasing={{0}: (0, {})} | custom-call | flops 500000000 | bytes 1800000 | tf_op jit(solution)/shard_map/pallas_call | solution.py:37
  71.5 1.9 %collective-permute-start.22 = (f32[5,56,128]{2,1,0:T(8,128)S(1)}, f32[5,56,128]{2,1,0:T(8,128)S(1)}, u32[]{:S(2)}, u32[]{:S(2)}) collective-permute-start(f32[5,56,128]{2,1,0:T(8,128)S(1)} %get-tuple-element.126), channel_id=1, source_target_pairs={{4,8},{12,16},{20,24},{8,4},{16,12},{24,20},{5,9},{13,17},{21,25},... | collective-permute-start | bytes 430088 | tf_op jit(solution)/shard_map/ppermute | solution.py:401
  73.5 2.3 %collective-permute-done.20.refs_3_ = f32[9,64,128]{2,1,0:T(8,128)S(1)} collective-permute-done((f32[9,64,128]{2,1,0:T(8,128)S(1)}, f32[9,64,128]{2,1,0:T(8,128)S(1)}, u32[]{:S(2)}, u32[]{:S(2)}) %collective-permute-start.20) | collective-permute-done | bytes 294944 | tf_op jit(solution)/shard_map/ppermute | solution.py:401
  75.8 2.3 %shard_map.75 = (f32[3,10,144,128]{3,2,1,0:T(8,128)S(1)}, f32[3,7,144,128]{3,2,1,0:T(8,128)S(1)}, f32[3,4,144,128]{3,2,1,0:T(8,128)S(1)}, f32[3,10,144,128]{3,2,...) custom-call(f32[3,10,144,128]{3,2,1,0:T(8,128)S(1)} %get-tuple-eleme, ...), custom_call_target="tpu_custom_call", output_to_operand_aliasing={{0}: (0, {}), {1}: (11, {}), {2}: (12, {}), {3}: (13, {})} | custom-call | flops 500000000 | bytes 1800000 | tf_op jit(solution)/shard_map/pallas_call | solution.py:37
  78.1 2.3 %collective-permute-start.24 = (f32[5,72,128]{2,1,0:T(8,128)S(1)}, f32[5,72,128]{2,1,0:T(8,128)S(1)}, u32[]{:S(2)}, u32[]{:S(2)}) collective-permute-start(f32[5,72,128]{2,1,0:T(8,128)S(1)} %get-tuple-element.129), channel_id=1, source_target_pairs={{4,8},{12,16},{20,24},{8,4},{16,12},{24,20},{5,9},{13,17},{21,25},... | collective-permute-start | bytes 552968 | tf_op jit(solution)/shard_map/ppermute | solution.py:401
  80.5 1.6 %shard_map.76 = (f32[3,10,144,128]{3,2,1,0:T(8,128)S(1)}, f32[1,9,4,128,128]{4,3,2,1,0:T(8,128)}) custom-call(f32[3,10,144,128]{3,2,1,0:T(8,128)S(1)} %get-tuple-element.123.refs_0_, f32[3,7,144,128]{3,2,1,0:T(8,128)S(1)} %get-tuple-element.124.refs_1_, f32[3,4,144,128]{3,2,1,0:T(8,128)S(1)} %get-tuple-element.125.refs_2_, ...), custom_call_target="tpu_custom_call", output_to_operand_aliasing={{0}: (0, {})} | custom-call | flops 500000000 | bytes 1800000 | tf_op jit(solution)/shard_map/pallas_call | solution.py:37
  82.1 4.9 %collective-permute-done.24.refs_3_ = f32[5,72,128]{2,1,0:T(8,128)S(1)} collective-permute-done((f32[5,72,128]{2,1,0:T(8,128)S(1)}, f32[5,72,128]{2,1,0:T(8,128)S(1)}, u32[]{:S(2)}, u32[]{:S(2)}) %collective-permute-start.24) | collective-permute-done | bytes 184352 | tf_op jit(solution)/shard_map/ppermute | solution.py:401
  87.0 2.1 %shard_map.77 = (f32[3,10,144,128]{3,2,1,0:T(8,128)S(1)}, f32[1,9,4,128,128]{4,3,2,1,0:T(8,128)}) custom-call(f32[3,10,144,128]{3,2,1,0:T(8,128)S(1)} %get-tuple-element.128.refs_0_, f32[3,7,144,128]{3,2,1,0:T(8,128)S(1)} %get-tuple-element.124.refs_1_, ...), custom_call_target="tpu_custom_call", output_to_operand_aliasing={{0}: (0, {}), {1}: (11, {})} | custom-call | flops 500000000 | bytes 1800000 | tf_op jit(solution)/shard_map/pallas_call | solution.py:37
  (55 shorter events, 9.0 us)
Async XLA Ops:
  0.0 19.7 %copy-start = (f32[1,9,4,128,128]{4,3,2,1,0:T(8,128)S(1)}, f32[1,9,4,128,128]{4,3,2,1,0:T(8,128)}, u32[]{:S(2)}) copy-start(f32[1,9,4,128,128]{4,3,2,1,0:T(8,128)} %refs_0_.3) | copy-start | bytes 7077892
  0.0 13.1 %copy-start.6 = (s32[4,8,4,4]{1,3,2,0:T(4,128)S(1)}, s32[4,8,4,4]{1,3,2,0:T(4,128)}, u32[]{:S(2)}) copy-start(s32[4,8,4,4]{1,3,2,0:T(4,128)} %param.11) | copy-start | bytes 6148
  2.4 7.0 %copy-start.5 = (f32[8,32,128]{2,1,0:T(8,128)}, f32[8,32,128]{2,1,0:T(8,128)S(1)}, u32[]{:S(2)}) copy-start(f32[8,32,128]{2,1,0:T(8,128)S(1)} %get-tuple-element.85) | copy-start | bytes 393220
  2.4 13.2 %copy-start.1 = (f32[8,32,128]{2,1,0:T(8,128)}, f32[8,32,128]{2,1,0:T(8,128)S(1)}, u32[]{:S(2)}) copy-start(f32[8,32,128]{2,1,0:T(8,128)S(1)} %get-tuple-element.75.refs_7_) | copy-start | bytes 393220
  2.5 12.6 %collective-permute-start.1 = (f32[5,128,128]{2,1,0:T(8,128)}, f32[5,128,128]{2,1,0:T(8,128)S(1)}, u32[]{:S(2)}, u32[]{:S(2)}) collective-permute-start(f32[5,128,128]{2,1,0:T(8,128)} %get-tuple-element.70), channel_id=1, source_target_pairs={{0,4},{8,12},{16,20},{24,28},{4,0},{12,8},{20,16},{28,24},{1,5},{9... | collective-permute-start | bytes 983048 | tf_op jit(solution)/shard_map/ppermute | solution.py:401
  2.5 11.8 %collective-permute-start.3 = (f32[8,32,128]{2,1,0:T(8,128)S(1)}, f32[8,32,128]{2,1,0:T(8,128)}, u32[]{:S(2)}, u32[]{:S(2)}) collective-permute-start(f32[8,32,128]{2,1,0:T(8,128)S(1)} %get-tuple-element.75.refs_7_), channel_id=1, source_target_pairs={{0,3},{1,2},{2,1},{3,0},{4,7},{5,6},{6,5},{7,4},{8,11},{9,10},{10,... | collective-permute-start | bytes 393224 | tf_op jit(solution)/shard_map/ppermute | solution.py:365
  4.2 10.2 %collective-permute-start.2 = (f32[8,32,128]{2,1,0:T(8,128)S(1)}, f32[8,32,128]{2,1,0:T(8,128)S(1)}, u32[]{:S(2)}, u32[]{:S(2)}) collective-permute-start(f32[8,32,128]{2,1,0:T(8,128)S(1)} %get-tuple-element.75.refs_7_), channel_id=1, source_target_pairs={{0,1},{1,0},{2,3},{3,2},{4,5},{5,4},{6,7},{7,6},{8,9},{9,8},{10,11... | collective-permute-start | bytes 393224 | tf_op jit(solution)/shard_map/ppermute | solution.py:364
  6.6 7.7 %collective-permute-start.4 = (f32[6,32,128]{2,1,0:T(8,128)}, f32[6,32,128]{2,1,0:T(8,128)}, u32[]{:S(2)}, u32[]{:S(2)}) collective-permute-start(f32[6,32,128]{2,1,0:T(8,128)} %get-tuple-element.76), channel_id=1, source_target_pairs={{4,8},{12,16},{20,24},{8,4},{16,12},{24,20},{5,9},{13,17},{21,25},... | collective-permute-start | bytes 294920 | tf_op jit(solution)/shard_map/ppermute | solution.py:413
  9.5 12.9 %collective-permute-start = (f32[5,128,128]{2,1,0:T(8,128)}, f32[5,128,128]{2,1,0:T(8,128)S(1)}, u32[]{:S(2)}, u32[]{:S(2)}) collective-permute-start(f32[5,128,128]{2,1,0:T(8,128)} %get-tuple-element.69), channel_id=1, source_target_pairs={{4,8},{12,16},{20,24},{8,4},{16,12},{24,20},{5,9},{13,17},{21,25},... | collective-permute-start | bytes 983048 | tf_op jit(solution)/shard_map/ppermute | solution.py:401
  15.7 6.8 %collective-permute-start.5 = (f32[8,32,128]{2,1,0:T(8,128)}, f32[8,32,128]{2,1,0:T(8,128)}, u32[]{:S(2)}, u32[]{:S(2)}) collective-permute-start(f32[8,32,128]{2,1,0:T(8,128)} %collective-permute-done.3.refs_10_), channel_id=1, source_target_pairs={{0,1},{1,0},{2,3},{3,2},{4,5},{5,4},{6,7},{7,6},{8,9},{9,8},{10,11... | collective-permute-start | bytes 393224 | tf_op jit(solution)/shard_map/ppermute | solution.py:368
  16.6 11.6 %collective-permute-start.9 = (f32[14,32,128]{2,1,0:T(8,128)S(1)}, f32[14,32,128]{2,1,0:T(8,128)S(1)}, u32[]{:S(2)}, u32[]{:S(2)}) collective-permute-start(f32[14,32,128]{2,1,0:T(8,128)S(1)} %constant_dynamic-update-slice_fusion.refs_1_), channel_id=1, source_target_pairs={{0,3},{1,2},{2,1},{3,0},{4,7},{5,6},{6,5},{7,4},{8,11},{9,10},{10,... | collective-permute-start | bytes 688136 | tf_op jit(solution)/shard_map/ppermute | solution.py:365
  16.6 13.6 %collective-permute-start.8 = (f32[14,32,128]{2,1,0:T(8,128)S(1)}, f32[14,32,128]{2,1,0:T(8,128)}, u32[]{:S(2)}, u32[]{:S(2)}) collective-permute-start(f32[14,32,128]{2,1,0:T(8,128)S(1)} %constant_dynamic-update-slice_fusion.refs_1_), channel_id=1, source_target_pairs={{0,1},{1,0},{2,3},{3,2},{4,5},{5,4},{6,7},{7,6},{8,9},{9,8},{10,11... | collective-permute-start | bytes 688136 | tf_op jit(solution)/shard_map/ppermute | solution.py:364
  19.7 2.7 %copy-start.2 = (f32[8,32,128]{2,1,0:T(8,128)S(1)}, f32[8,32,128]{2,1,0:T(8,128)}, u32[]{:S(2)}) copy-start(f32[8,32,128]{2,1,0:T(8,128)} %copy-done.1) | copy-start | bytes 393220
  19.7 2.7 %copy-start.4 = (f32[8,32,128]{2,1,0:T(8,128)S(1)}, f32[8,32,128]{2,1,0:T(8,128)}, u32[]{:S(2)}) copy-start(f32[8,32,128]{2,1,0:T(8,128)} %copy-done.3) | copy-start | bytes 393220
  23.8 13.5 %collective-permute-start.6 = (f32[9,80,128]{2,1,0:T(8,128)S(1)}, f32[9,80,128]{2,1,0:T(8,128)S(1)}, u32[]{:S(2)}, u32[]{:S(2)}) collective-permute-start(f32[9,80,128]{2,1,0:T(8,128)S(1)} %get-tuple-element.83), channel_id=1, source_target_pairs={{4,8},{12,16},{20,24},{8,4},{16,12},{24,20},{5,9},{13,17},{21,25},... | collective-permute-start | bytes 1105928 | tf_op jit(solution)/shard_map/ppermute | solution.py:401
  26.2 11.1 %collective-permute-start.7 = (f32[9,80,128]{2,1,0:T(8,128)S(1)}, f32[9,80,128]{2,1,0:T(8,128)S(1)}, u32[]{:S(2)}, u32[]{:S(2)}) collective-permute-start(f32[9,80,128]{2,1,0:T(8,128)S(1)} %get-tuple-element.84), channel_id=1, source_target_pairs={{0,4},{8,12},{16,20},{24,28},{4,0},{12,8},{20,16},{28,24},{1,5},{9... | collective-permute-start | bytes 1105928 | tf_op jit(solution)/shard_map/ppermute | solution.py:401
  30.2 6.0 %collective-permute-start.10 = (f32[14,32,128]{2,1,0:T(8,128)S(1)}, f32[14,32,128]{2,1,0:T(8,128)S(1)}, u32[]{:S(2)}, u32[]{:S(2)}) collective-permute-start(f32[14,32,128]{2,1,0:T(8,128)S(1)} %collective-permute-done.9.refs_4_), channel_id=1, source_target_pairs={{0,1},{1,0},{2,3},{3,2},{4,5},{5,4},{6,7},{7,6},{8,9},{9,8},{10,11... | collective-permute-start | bytes 688136 | tf_op jit(solution)/shard_map/ppermute | solution.py:368
  31.0 5.2 %collective-permute-start.11 = (f32[9,48,128]{2,1,0:T(8,128)S(1)}, f32[9,48,128]{2,1,0:T(8,128)S(1)}, u32[]{:S(2)}, u32[]{:S(2)}) collective-permute-start(f32[9,48,128]{2,1,0:T(8,128)S(1)} %get-tuple-element.88), channel_id=1, source_target_pairs={{0,4},{8,12},{16,20},{24,28},{4,0},{12,8},{20,16},{28,24},{1,5},{9... | collective-permute-start | bytes 663560 | tf_op jit(solution)/shard_map/ppermute | solution.py:401
  31.1 16.3 %collective-permute-start.13 = (f32[9,48,128]{2,1,0:T(8,128)S(1)}, f32[9,48,128]{2,1,0:T(8,128)S(1)}, u32[]{:S(2)}, u32[]{:S(2)}) collective-permute-start(f32[9,48,128]{2,1,0:T(8,128)S(1)} %get-tuple-element.94), channel_id=1, source_target_pairs={{4,8},{12,16},{20,24},{8,4},{16,12},{24,20},{5,9},{13,17},{21,25},... | collective-permute-start | bytes 663560 | tf_op jit(solution)/shard_map/ppermute | solution.py:401
  37.3 1.8 %collective-permute-start.12 = (f32[6,128,128]{2,1,0:T(8,128)S(1)}, f32[6,128,128]{2,1,0:T(8,128)S(1)}, u32[]{:S(2)}, u32[]{:S(2)}) collective-permute-start(f32[6,128,128]{2,1,0:T(8,128)S(1)} %get-tuple-element.92), channel_id=1, source_target_pairs={{0,4},{8,12},{16,20},{24,28},{4,0},{12,8},{20,16},{28,24},{1,5},{9... | collective-permute-start | bytes 1179656 | tf_op jit(solution)/shard_map/ppermute | solution.py:499
  41.6 13.6 %collective-permute-start.14 = (f32[9,72,128]{2,1,0:T(8,128)S(1)}, f32[9,72,128]{2,1,0:T(8,128)S(1)}, u32[]{:S(2)}, u32[]{:S(2)}) collective-permute-start(f32[9,72,128]{2,1,0:T(8,128)S(1)} %get-tuple-element.104), channel_id=1, source_target_pairs={{4,8},{12,16},{20,24},{8,4},{16,12},{24,20},{5,9},{13,17},{21,25},... | collective-permute-start | bytes 995336 | tf_op jit(solution)/shard_map/ppermute | solution.py:401
  47.3 7.9 %collective-permute-start.15 = (f32[9,72,128]{2,1,0:T(8,128)S(1)}, f32[9,72,128]{2,1,0:T(8,128)S(1)}, u32[]{:S(2)}, u32[]{:S(2)}) collective-permute-start(f32[9,72,128]{2,1,0:T(8,128)S(1)} %get-tuple-element.105), channel_id=1, source_target_pairs={{0,4},{8,12},{16,20},{24,28},{4,0},{12,8},{20,16},{28,24},{1,5},{9... | collective-permute-start | bytes 995336 | tf_op jit(solution)/shard_map/ppermute | solution.py:401
  49.3 11.4 %collective-permute-start.16 = (f32[9,56,128]{2,1,0:T(8,128)S(1)}, f32[9,56,128]{2,1,0:T(8,128)S(1)}, u32[]{:S(2)}, u32[]{:S(2)}) collective-permute-start(f32[9,56,128]{2,1,0:T(8,128)S(1)} %get-tuple-element.107), channel_id=1, source_target_pairs={{4,8},{12,16},{20,24},{8,4},{16,12},{24,20},{5,9},{13,17},{21,25},... | collective-permute-start | bytes 774152 | tf_op jit(solution)/shard_map/ppermute | solution.py:401
  51.5 9.2 %collective-permute-start.17 = (f32[9,56,128]{2,1,0:T(8,128)S(1)}, f32[9,56,128]{2,1,0:T(8,128)S(1)}, u32[]{:S(2)}, u32[]{:S(2)}) collective-permute-start(f32[9,56,128]{2,1,0:T(8,128)S(1)} %get-tuple-element.108), channel_id=1, source_target_pairs={{0,4},{8,12},{16,20},{24,28},{4,0},{12,8},{20,16},{28,24},{1,5},{9... | collective-permute-start | bytes 774152 | tf_op jit(solution)/shard_map/ppermute | solution.py:401
  57.4 12.0 %collective-permute-start.18 = (f32[9,64,128]{2,1,0:T(8,128)S(1)}, f32[9,64,128]{2,1,0:T(8,128)S(1)}, u32[]{:S(2)}, u32[]{:S(2)}) collective-permute-start(f32[9,64,128]{2,1,0:T(8,128)S(1)} %get-tuple-element.115), channel_id=1, source_target_pairs={{4,8},{12,16},{20,24},{8,4},{16,12},{24,20},{5,9},{13,17},{21,25},... | collective-permute-start | bytes 884744 | tf_op jit(solution)/shard_map/ppermute | solution.py:401
  59.6 9.9 %collective-permute-start.19 = (f32[9,64,128]{2,1,0:T(8,128)S(1)}, f32[9,64,128]{2,1,0:T(8,128)S(1)}, u32[]{:S(2)}, u32[]{:S(2)}) collective-permute-start(f32[9,64,128]{2,1,0:T(8,128)S(1)} %get-tuple-element.116), channel_id=1, source_target_pairs={{0,4},{8,12},{16,20},{24,28},{4,0},{12,8},{20,16},{28,24},{1,5},{9... | collective-permute-start | bytes 884744 | tf_op jit(solution)/shard_map/ppermute | solution.py:401
  62.8 13.0 %collective-permute-start.20 = (f32[9,64,128]{2,1,0:T(8,128)S(1)}, f32[9,64,128]{2,1,0:T(8,128)S(1)}, u32[]{:S(2)}, u32[]{:S(2)}) collective-permute-start(f32[9,64,128]{2,1,0:T(8,128)S(1)} %get-tuple-element.118), channel_id=1, source_target_pairs={{4,8},{12,16},{20,24},{8,4},{16,12},{24,20},{5,9},{13,17},{21,25},... | collective-permute-start | bytes 884744 | tf_op jit(solution)/shard_map/ppermute | solution.py:401
  66.1 9.7 %collective-permute-start.21 = (f32[9,64,128]{2,1,0:T(8,128)S(1)}, f32[9,64,128]{2,1,0:T(8,128)S(1)}, u32[]{:S(2)}, u32[]{:S(2)}) collective-permute-start(f32[9,64,128]{2,1,0:T(8,128)S(1)} %get-tuple-element.119), channel_id=1, source_target_pairs={{0,4},{8,12},{16,20},{24,28},{4,0},{12,8},{20,16},{28,24},{1,5},{9... | collective-permute-start | bytes 884744 | tf_op jit(solution)/shard_map/ppermute | solution.py:401
  71.5 9.0 %collective-permute-start.22 = (f32[5,56,128]{2,1,0:T(8,128)S(1)}, f32[5,56,128]{2,1,0:T(8,128)S(1)}, u32[]{:S(2)}, u32[]{:S(2)}) collective-permute-start(f32[5,56,128]{2,1,0:T(8,128)S(1)} %get-tuple-element.126), channel_id=1, source_target_pairs={{4,8},{12,16},{20,24},{8,4},{16,12},{24,20},{5,9},{13,17},{21,25},... | collective-permute-start | bytes 430088 | tf_op jit(solution)/shard_map/ppermute | solution.py:401
  73.4 7.1 %collective-permute-start.23 = (f32[5,56,128]{2,1,0:T(8,128)S(1)}, f32[5,56,128]{2,1,0:T(8,128)S(1)}, u32[]{:S(2)}, u32[]{:S(2)}) collective-permute-start(f32[5,56,128]{2,1,0:T(8,128)S(1)} %get-tuple-element.127), channel_id=1, source_target_pairs={{0,4},{8,12},{16,20},{24,28},{4,0},{12,8},{20,16},{28,24},{1,5},{9... | collective-permute-start | bytes 430088 | tf_op jit(solution)/shard_map/ppermute | solution.py:401
  78.1 8.9 %collective-permute-start.24 = (f32[5,72,128]{2,1,0:T(8,128)S(1)}, f32[5,72,128]{2,1,0:T(8,128)S(1)}, u32[]{:S(2)}, u32[]{:S(2)}) collective-permute-start(f32[5,72,128]{2,1,0:T(8,128)S(1)} %get-tuple-element.129), channel_id=1, source_target_pairs={{4,8},{12,16},{20,24},{8,4},{16,12},{24,20},{5,9},{13,17},{21,25},... | collective-permute-start | bytes 552968 | tf_op jit(solution)/shard_map/ppermute | solution.py:401
  80.4 6.6 %collective-permute-start.25 = (f32[5,72,128]{2,1,0:T(8,128)S(1)}, f32[5,72,128]{2,1,0:T(8,128)S(1)}, u32[]{:S(2)}, u32[]{:S(2)}) collective-permute-start(f32[5,72,128]{2,1,0:T(8,128)S(1)} %get-tuple-element.130), channel_id=1, source_target_pairs={{0,4},{8,12},{16,20},{24,28},{4,0},{12,8},{20,16},{28,24},{1,5},{9... | collective-permute-start | bytes 552968 | tf_op jit(solution)/shard_map/ppermute | solution.py:401
  (1 other events, 0.7 us)

commit v3 on v2

--- a/solution.py
+++ b/solution.py
@@ -9,6 +9,7 @@
 
 NEAR = 1.125
 FAR = -1.0 / 24.0
+RATIO = FAR / NEAR
 DT = 0.2
 ROWS = 8
 PAD = 8
@@ -18,7 +19,7 @@
 F32 = jnp.float32
 
 
-def call(body, ins, outs, alias=(), scratch=(), anywhere=(), us=0.5, waits=()):
+def call(body, ins, outs, alias=(), scratch=(), anywhere=(), us=5.0, waits=()):
     ins = dict(ins, **{"wait%d" % i: a for i, a in enumerate(waits)})
     in_names, out_names = list(ins), list(outs)
 
@@ -60,32 +61,32 @@
     def __init__(self, lanes):
         lane = lax.broadcasted_iota(jnp.int32, (ROWS, lanes), 1)
         self.lanes = lanes
-        self.f_up1 = jnp.where(lane < lanes - 1, F32(NEAR), F32(0))
-        self.f_up2 = jnp.where(lane < lanes - 2, F32(FAR), F32(0))
-        self.f_dn1 = jnp.where(lane >= 1, F32(-FAR), F32(0))
-        self.b_dn1 = jnp.where(lane >= 1, F32(-NEAR), F32(0))
-        self.b_dn2 = jnp.where(lane >= 2, F32(-FAR), F32(0))
-        self.b_up1 = jnp.where(lane < lanes - 1, F32(FAR), F32(0))
+        self.f_up1 = jnp.where(lane < lanes - 1, F32(1), F32(0))
+        self.f_up2 = jnp.where(lane < lanes - 2, F32(RATIO), F32(0))
+        self.f_dn1 = jnp.where(lane >= 1, F32(RATIO), F32(0))
+        self.b_dn1 = jnp.where(lane >= 1, F32(1), F32(0))
+        self.b_dn2 = jnp.where(lane >= 2, F32(RATIO), F32(0))
+        self.b_up1 = jnp.where(lane < lanes - 1, F32(RATIO), F32(0))
 
     def fz(self, f):
         n = self.lanes
-        return (self.f_up1 * pltpu.roll(f, n - 1, 1) - NEAR * f) + (
-            self.f_up2 * pltpu.roll(f, n - 2, 1) + self.f_dn1 * pltpu.roll(f, 1, 1)
+        return (self.f_up1 * pltpu.roll(f, n - 1, 1) - f) + (
+            self.f_up2 * pltpu.roll(f, n - 2, 1) - self.f_dn1 * pltpu.roll(f, 1, 1)
         )
 
     def bz(self, f):
         n = self.lanes
-        return (self.b_dn1 * pltpu.roll(f, 1, 1) + NEAR * f) + (
-            self.b_up1 * pltpu.roll(f, n - 1, 1) + self.b_dn2 * pltpu.roll(f, 2, 1)
+        return (f - self.b_dn1 * pltpu.roll(f, 1, 1)) + (
+            self.b_up1 * pltpu.roll(f, n - 1, 1) - self.b_dn2 * pltpu.roll(f, 2, 1)
         )
 
 
 def fwd(at):
-    return NEAR * (at(1) - at(0)) + FAR * (at(2) - at(-1))
+    return (at(1) - at(0)) + RATIO * (at(2) - at(-1))
 
 
 def bwd(at):
-    return NEAR * (at(0) - at(-1)) + FAR * (at(1) - at(-2))
+    return (at(0) - at(-1)) + RATIO * (at(1) - at(-2))
 
 
 def tile_reader(ref, field, start):
@@ -100,12 +101,7 @@
 
 
 def factors(active_cells, damp):
-    return jnp.where(active_cells, damp, F32(1)), jnp.where(active_cells, DT * damp, F32(0))
-
-
-def mask_rows(refs, moment, slab, start, blocks, block_rows):
-    row = (moment * 3 + slab) * blocks + start // block_rows
-    return jnp.broadcast_to(refs["mask"][pl.ds(row, 1), :], (ROWS, refs["mask"].shape[1])) > 0
+    return jnp.where(active_cells, damp, F32(1)), jnp.where(active_cells, (DT * NEAR) * damp, F32(0))
 
 
 def zero_pads(ref, rows):
@@ -115,11 +111,17 @@
 
 
 class Plan:
-    def __init__(self, cx, rows, lanes, blocks, steps, cuts):
+    def __init__(self, cx, rows, lanes, blocks, steps, slabs, cuts):
+        self.slabs = slabs
         self.cx, self.rows, self.lanes = cx, rows, lanes
         self.blocks, self.steps, self.cuts = blocks, steps, cuts
         self.block_rows = rows // blocks
         self.tiles = rows // ROWS
+
+    def active(self, refs, moment, side, start):
+        slab = jnp.clip(lax.axis_index("aper") + side - 1, 0, self.slabs - 1)
+        row = (moment * self.slabs + slab) * self.blocks + start // self.block_rows
+        return jnp.broadcast_to(refs["mask"][pl.ds(row, 1), :], (ROWS, self.lanes)) > 0
 
     def chunk(self, step, which):
         cut = self.cuts[step]
@@ -163,7 +165,7 @@
 
         def tile(k, carry):
             start = pl.multiple_of(k * ROWS, ROWS)
-            here = mask_rows(refs, moment, 1, start, self.blocks, self.block_rows)
+            here = self.active(refs, moment, 1, start)
             xx = tile_reader(sh, 0, start)
             xy = tile_reader(sh, 1, start)
             xz = tile_reader(sh, 2, start)
@@ -191,7 +193,7 @@
                     )
             return carry
 
-        lax.fori_loop(first, last, tile, 0)
+        lax.fori_loop(first, last, tile, 0, unroll=True)
         odd = odd_slab()
         rows = pl.ds(PAD + first * ROWS, (last - first) * ROWS)
         for slot, (top, bottom, _, _) in enumerate(self.slots(moment)):
@@ -225,7 +227,7 @@
 
         def tile(k, carry):
             start = pl.multiple_of(k * ROWS, ROWS)
-            masks = [mask_rows(refs, moment, slab, start, self.blocks, self.block_rows) for slab in range(3)]
+            masks = [self.active(refs, moment, side, start) for side in range(3)]
             vx = tile_reader(refs["vel"], 0, start)
             vy = tile_reader(refs["vel"], 1, start)
             vz = tile_reader(refs["vel"], 2, start)
@@ -272,7 +274,7 @@
                     put_h(2, i, keep * old_h[2, i + 2, padded, :] + mu * xz)
             return carry
 
-        lax.fori_loop(first, last, tile, 0)
+        lax.fori_loop(first, last, tile, 0, unroll=True)
 
     def finish(self, refs, moment, which, done, sems):
         refs = dict(refs, done=done)
@@ -318,13 +320,22 @@
     return move, copies
 
 
-def pack(cx, refs, sems):
+def pack_model(cx, refs, sems):
     odd = odd_slab()
     move, copies = mover(sems)
-    for i, name in enumerate(("buoy", "q", "lam", "mu")):
-        move(refs[name], refs["first" if i < 2 else "second"].at[pl.ds(i % 2 * cx, cx)])
-    for slot, name in enumerate(("lam", "lam", "mu", "mu", "q", "q")):
-        move(refs[name].at[pick(odd, cx - 2 + slot % 2, slot % 2)], refs["edge"].at[slot])
+    for i, name in enumerate(("buoy", "q")):
+        move(refs[name], refs["first"].at[pl.ds(i * cx, cx)])
+    for i, name in enumerate(("lam", "mu", "q")):
+        move(refs[name].at[pl.ds(pick(odd, cx - 2, 0), 2)], refs["edge"].at[pl.ds(2 * i, 2)])
+    for i, name in enumerate(("lam", "mu")):
+        move(refs[name], refs["second"].at[pl.ds(i * cx, cx)])
+    for copy in copies:
+        copy.wait()
+
+
+def pack_stress(cx, refs, sems):
+    odd = odd_slab()
+    move, copies = mover(sems)
     top = [(3, cx - 1), (6, cx - 2), (6, cx - 1), (7, cx - 2), (7, cx - 1)]
     bottom = [(3, 0), (3, 1), (6, 0), (7, 0), (7, 0)]
     for name, flag in (("near", jnp.logical_not(odd)), ("far", odd)):
@@ -351,11 +362,16 @@
         for i in range(cx):
             refs["old"][field, i] = refs["wave"][0, field, i]
     plan.inner_forcing(refs, refs["sh"], refs["so"])
-    refs["ready"][...] = jnp.zeros(refs["ready"].shape, F32)
-
-
-def after(array, *others):
-    return lax.optimization_barrier((array,) + others)[0]
+    lane_blocks = refs["active"].shape[1]
+    block = lax.broadcasted_iota(jnp.int32, (lane_blocks, plan.lanes), 1) // (plan.lanes // lane_blocks)
+    own = block == lax.broadcasted_iota(jnp.int32, (lane_blocks, plan.lanes), 0)
+    refs["mask"][...] = jnp.dot(refs["active"][...].astype(F32), own.astype(F32),
+                                preferred_element_type=F32)
+
+
+def hold(array, *others):
+    return call(lambda refs: None, dict(array=array), dict(array=array.shape), alias=("array",),
+                us=0.02, waits=others)["array"]
 
 
 def spread(mine, shots):
@@ -365,7 +381,7 @@
         across = lax.ppermute(mine, "shot", pairs(3))
 
         def finish(*others):
-            handed = lax.ppermute(after(across, beside, *others), "shot", pairs(1))
+            handed = lax.ppermute(hold(across, beside, *others), "shot", pairs(1))
             return {0: mine, 1: beside, 2: handed, 3: across}
 
         return (beside, across), finish
@@ -390,7 +406,7 @@
     cx, panel_rows, lanes = lam.shape
     rows = wave.shape[3]
     steps, _, blocks, lane_blocks = active.shape
-    plan = Plan(cx, rows, lanes, blocks, steps, cuts_of(steps, rows // ROWS))
+    plan = Plan(cx, rows, lanes, blocks, steps, slabs, cuts_of(steps, rows // ROWS))
     padded = rows + 2 * PAD
     far = [(i, i + 1) for i in range(1, slabs - 1, 2)]
     near = [(i, i + 1) for i in range(0, slabs - 1, 2)]
@@ -402,27 +418,32 @@
 
     panel = (panel_rows, lanes)
     sent = call(
-        functools.partial(pack, cx),
-        dict(lam=lam, mu=mu, buoy=buoy, q=q, wave=wave),
-        dict(first=(2 * cx,) + panel, second=(2 * cx,) + panel, edge=(MODEL_SLOTS,) + panel,
-             far=(STRESS_SLOTS, rows, lanes), near=(STRESS_SLOTS, rows, lanes)),
-        scratch=[pltpu.SemaphoreType.DMA((4 + MODEL_SLOTS + 2 * STRESS_SLOTS,))],
-        anywhere=("lam", "mu", "buoy", "q", "wave"), us=0.02,
+        functools.partial(pack_model, cx), dict(lam=lam, mu=mu, buoy=buoy, q=q),
+        dict(first=(2 * cx,) + panel, second=(2 * cx,) + panel, edge=(MODEL_SLOTS,) + panel),
+        scratch=[pltpu.SemaphoreType.DMA((7,))], anywhere=("lam", "mu", "buoy", "q"), us=0.02,
     )
+    sent.update(call(
+        functools.partial(pack_stress, cx), dict(wave=wave),
+        dict(far=(STRESS_SLOTS, rows, lanes), near=(STRESS_SLOTS, rows, lanes)),
+        scratch=[pltpu.SemaphoreType.DMA((2 * STRESS_SLOTS,))], anywhere=("wave",), us=5.0, waits=(sent["edge"],),
+    ))
     halo_far, halo_near = exchange(sent["far"], sent["near"])
     edge = lax.ppermute(sent["edge"], "aper", far)
-    device = lax.axis_index("aper")
-    around = lax.dynamic_slice_in_dim(jnp.pad(active, ((0, 0), (1, 1), (0, 0), (0, 0))), device, 3, 1)
-    mask = jnp.repeat(around.astype(F32).reshape(steps * 3 * blocks, lane_blocks), lanes // lane_blocks, axis=1)
-
     sh_shape, so_shape = (3, cx + 3, padded, lanes), (3, cx, padded, lanes)
     vel_shape, slab_shape = (3, cx + 2 * REACH, padded, lanes), (cx, rows, lanes)
-    state = call(functools.partial(prepare, plan), dict(wave=wave),
-                 dict(sh=sh_shape, so=so_shape, old=(3,) + slab_shape, inner=(3,) + slab_shape, ready=(ROWS, lanes)), us=0.02)
+    state = call(functools.partial(prepare, plan), dict(wave=wave, active=active.reshape(-1, lane_blocks)),
+                 dict(sh=sh_shape, so=so_shape, old=(3,) + slab_shape, inner=(3,) + slab_shape, mask=(steps * slabs * blocks, lanes)), us=5.0)
 
     first_stage, finish = spread(sent["first"], shots)
-    firsts = finish(halo_near, edge, mask, state["ready"])
-    second = jnp.concatenate([sent["second"], after(edge, *first_stage)])
+    mask = state["mask"]
+    firsts = finish(edge)
+
+    def join(refs):
+        refs["all"][:2 * cx] = refs["second"][...]
+        refs["all"][2 * cx:] = refs["edge"][...]
+
+    second = call(join, dict(second=sent["second"], edge=edge),
+                  dict(all=(2 * cx + MODEL_SLOTS,) + panel), us=0.02, waits=first_stage + (mask,))["all"]
     _, finish_second = spread(second, shots)
 
     def sends(step, which):
@@ -454,8 +475,7 @@
         plan.velocity(refs, 0, which, refs["sh"], refs["so"],
                       lambda f, i, start: refs["old"][f, i, pl.ds(start, ROWS), :])
 
-    ins = dict(halo_far=halo_far, halo_near=halo_near, mask=mask,
-               **{name: state[name] for name in ("sh", "so", "old", "inner")})
+    ins = dict(halo_far=halo_far, halo_near=halo_near, **state)
     ins.update({"first%d" % k: a for k, a in firsts.items()})
     got = call(start_first, ins,
                dict(sh=sh_shape, buoy=slab_shape, damp=slab_shape, vel_next=vel_shape,
@@ -555,7 +575,7 @@
 
 
 def cuts_of(steps, tiles):
-    middle = tiles // 2 + steps // 2
+    middle = tiles // 2 + 1
     return [max(1, middle - step) for step in range(steps)]
 
 

time: 89.6 us -> 84.5 us (0.943)
  the two profiles are of different devices: /device:TPU:12 before, /device:TPU:3 now
where the time goes in v3:
time: 84.5 us; the launch traced here: 83.9 us
  starting transfers between devices  42.6 us (50%)
  waiting for transfers between devices  24.2 us (29%)
  Pallas kernels  15 us (18%)
  local copies, waits for them, and re-layouts  1.87 us (2%)
    ppermute x9, starting transfers between devices, exchange(): lax.ppermute(to_far, 'aper', far)  29.4 us
    ppermute x9, waiting for transfers between devices, exchange(): lax.ppermute(to_far, 'aper', far)  19.3 us
    pallas_call x18, Pallas kernels, call(): pl.pallas_call(kernel, out_shape=[pltpu.HBM(shape, F32) if name in anywhe...  15 us
    ppermute x1, starting transfers between devices, per_device(): edge = lax.ppermute(sent['edge'], 'aper', far)  4.08 us
    ppermute x2, starting transfers between devices, spread(): across = lax.ppermute(mine, 'shot', pairs(3))  3.46 us
    ppermute x2, waiting for transfers between devices, spread(): beside = lax.ppermute(mine, 'shot', pairs(1))  2.81 us
    ppermute x1, starting transfers between devices, per_device(): model_near = lax.ppermute(got['send_model'], 'aper', near)  2.22 us
    ppermute x2, starting transfers between devices, finish(): handed = lax.ppermute(hold(across, beside, *others), 'shot', pairs(1))  2.18 us
  transfers between devices with their start and end apart: 26, of which 9 were waited for; matrix products, arithmetic and copies ran while one was open for 0% of the time, Pallas kernels for 15%

profile of v3, /device:TPU:3, one launch (start us, length us, event | category | flops | bytes accessed | tf_op | source)
XLA Modules:
  0.0 83.9 jit_solution(16504928769159459175)
XLA Ops:
  0.0 1.0 %shard_map.64 = (f32[8,32,128]{2,1,0:T(8,128)S(1)}, f32[8,32,128]{2,1,0:T(8,128)S(1)}, f32[6,32,128]{2,1,0:T(8,128)S(1)}) custom-call(f32[4,32,128]{2,1,0:T(8,128)} %refs_0_.3, f32[4,32,128]{2,1,0:T(8,128)} %refs_1_.1, f32[4,32,128]{2,1,0:T(8,128)} %refs_2_.1, f32[4,32,128]{2,1,0:T(8,128)} %refs_3_.1), custom_call_target="tpu_custom_call" | custom-call | flops 20000000 | bytes 72000 | tf_op jit(solution)/shard_map/pallas_call | solution.py:38
  1.1 3.4 %collective-permute-start.3 = (f32[8,32,128]{2,1,0:T(8,128)S(1)}, f32[8,32,128]{2,1,0:T(8,128)S(1)}, u32[]{:S(2)}, u32[]{:S(2)}) collective-permute-start(f32[8,32,128]{2,1,0:T(8,128)S(1)} %get-tuple-element.75.refs_7_), channel_id=1, source_target_pairs={{0,3},{1,2},{2,1},{3,0},{4,7},{5,6},{6,5},{7,4},{8,11},{9,10},{10,... | collective-permute-start | bytes 393224 | tf_op jit(solution)/shard_map/ppermute | solution.py:381
  4.4 4.1 %collective-permute-start.4 = (f32[6,32,128]{2,1,0:T(8,128)S(1)}, f32[6,32,128]{2,1,0:T(8,128)S(1)}, u32[]{:S(2)}, u32[]{:S(2)}) collective-permute-start(f32[6,32,128]{2,1,0:T(8,128)S(1)} %get-tuple-element.67.refs_1_), channel_id=1, source_target_pairs={{4,8},{12,16},{20,24},{8,4},{16,12},{24,20},{5,9},{13,17},{21,25},... | collective-permute-start | bytes 294920 | tf_op jit(solution)/shard_map/ppermute | solution.py:431
  8.5 1.2 %shard_map.65 = (f32[5,128,128]{2,1,0:T(8,128)S(1)}, f32[5,128,128]{2,1,0:T(8,128)S(1)}) custom-call(f32[1,9,4,128,128]{4,3,2,1,0:T(8,128)} %refs_0_.5, f32[6,32,128]{2,1,0:T(8,128)S(1)} %get-tuple-element.67.refs_1_), custom_call_target="tpu_custom_call" | custom-call | flops 5000000000 | bytes 18000000 | tf_op jit(solution)/shard_map/pallas_call | solution.py:38
  9.8 2.5 %collective-permute-start = (f32[5,128,128]{2,1,0:T(8,128)S(1)}, f32[5,128,128]{2,1,0:T(8,128)S(1)}, u32[]{:S(2)}, u32[]{:S(2)}) collective-permute-start(f32[5,128,128]{2,1,0:T(8,128)S(1)} %get-tuple-element.68), channel_id=1, source_target_pairs={{4,8},{12,16},{20,24},{8,4},{16,12},{24,20},{5,9},{13,17},{21,25},... | collective-permute-start | bytes 983048 | tf_op jit(solution)/shard_map/ppermute | solution.py:417
  12.6 1.8 %collective-permute-start.5 = (f32[8,32,128]{2,1,0:T(8,128)S(1)}, f32[8,32,128]{2,1,0:T(8,128)S(1)}, u32[]{:S(2)}, u32[]{:S(2)}) collective-permute-start(f32[8,32,128]{2,1,0:T(8,128)S(1)} %shard_map.67), channel_id=1, source_target_pairs={{0,1},{1,0},{2,3},{3,2},{4,5},{5,4},{6,7},{7,6},{8,9},{9,8},{10,11... | collective-permute-start | bytes 393224 | tf_op jit(solution)/shard_map/ppermute | solution.py:384
  14.4 1.7 %copy-done = f32[1,9,4,128,128]{4,3,2,1,0:T(8,128)S(1)} copy-done((f32[1,9,4,128,128]{4,3,2,1,0:T(8,128)S(1)}, f32[1,9,4,128,128]{4,3,2,1,0:T(8,128)}, u32[]{:S(2)}) %copy-start) | copy-done | bytes 2359320
  16.1 2.1 %shard_map.66 = (f32[3,7,144,128]{3,2,1,0:T(8,128)S(1)}, f32[3,4,144,128]{3,2,1,0:T(8,128)S(1)}, f32[3,4,128,128]{3,2,1,0:T(8,128)S(1)}, f32[3,4,128,128]{3,2,1,0:T(8,128)S(1)}, f32[128,128]{1,0:T(8,128)S(1)}) custom-call(f32[1,9,4,128,128]{4,3,2,1,0:T(8,128)S(1)} %copy-done, s32[128,4]{1,0:T(8,128)S(1)} %bitcast.1), custom_call_target="tpu_custom_call" | custom-call | flops 5000000000 | bytes 18000000 | tf_op jit(solution)/shard_map/pallas_call | solution.py:38
  18.3 2.5 %collective-permute-done.refs_0_ = f32[5,128,128]{2,1,0:T(8,128)S(1)} collective-permute-done((f32[5,128,128]{2,1,0:T(8,128)S(1)}, f32[5,128,128]{2,1,0:T(8,128)S(1)}, u32[]{:S(2)}, u32[]{:S(2)}) %collective-permute-start) | collective-permute-done | bytes 327712 | tf_op jit(solution)/shard_map/ppermute | solution.py:417
  21.2 4.0 %collective-permute-start.6 = (f32[9,72,128]{2,1,0:T(8,128)S(1)}, f32[9,72,128]{2,1,0:T(8,128)S(1)}, u32[]{:S(2)}, u32[]{:S(2)}) collective-permute-start(f32[9,72,128]{2,1,0:T(8,128)S(1)} %get-tuple-element.81), channel_id=1, source_target_pairs={{4,8},{12,16},{20,24},{8,4},{16,12},{24,20},{5,9},{13,17},{21,25},... | collective-permute-start | bytes 995336 | tf_op jit(solution)/shard_map/ppermute | solution.py:417
  26.8 2.8 %collective-permute-done.8.refs_1_.refs_2_ = f32[14,32,128]{2,1,0:T(8,128)S(1)} collective-permute-done((f32[14,32,128]{2,1,0:T(8,128)S(1)}, f32[14,32,128]{2,1,0:T(8,128)S(1)}, u32[]{:S(2)}, u32[]{:S(2)}) %collective-permute-start.8) | collective-permute-done | bytes 229408 | tf_op jit(solution)/shard_map/ppermute | solution.py:380
  30.0 5.5 %collective-permute-start.13 = (f32[9,56,128]{2,1,0:T(8,128)S(1)}, f32[9,56,128]{2,1,0:T(8,128)S(1)}, u32[]{:S(2)}, u32[]{:S(2)}) collective-permute-start(f32[9,56,128]{2,1,0:T(8,128)S(1)} %get-tuple-element.90), channel_id=1, source_target_pairs={{4,8},{12,16},{20,24},{8,4},{16,12},{24,20},{5,9},{13,17},{21,25},... | collective-permute-start | bytes 774152 | tf_op jit(solution)/shard_map/ppermute | solution.py:417
  35.6 2.2 %collective-permute-start.12 = (f32[6,128,128]{2,1,0:T(8,128)S(1)}, f32[6,128,128]{2,1,0:T(8,128)S(1)}, u32[]{:S(2)}, u32[]{:S(2)}) collective-permute-start(f32[6,128,128]{2,1,0:T(8,128)S(1)} %get-tuple-element.88), channel_id=1, source_target_pairs={{0,4},{8,12},{16,20},{24,28},{4,0},{12,8},{20,16},{28,24},{1,5},{9... | collective-permute-start | bytes 1179656 | tf_op jit(solution)/shard_map/ppermute | solution.py:519
  37.9 1.3 %collective-permute-done.12.refs_11_ = f32[6,128,128]{2,1,0:T(8,128)S(1)} collective-permute-done((f32[6,128,128]{2,1,0:T(8,128)S(1)}, f32[6,128,128]{2,1,0:T(8,128)S(1)}, u32[]{:S(2)}, u32[]{:S(2)}) %collective-permute-start.12) | collective-permute-done | bytes 393248 | tf_op jit(solution)/shard_map/ppermute | solution.py:519
  39.2 1.1 %shard_map.74 = (f32[3,10,144,128]{3,2,1,0:T(8,128)S(1)}, f32[3,7,144,128]{3,2,1,0:T(8,128)S(1)}, f32[3,4,144,128]{3,2,1,0:T(8,128)S(1)}, f32[3,10,144,128]{3,2,...) custom-call(f32[3,10,144,128]{3,2,1,0:T(8,128)S(1)} %shard_map.70.re, ...), custom_call_target="tpu_custom_call", output_to_operand_aliasing={{0}: (0, {}), {4}: (8, {}), {5}: (9, {}), {6}: (10, {})} | custom-call | flops 5000000000 | bytes 18000000 | tf_op jit(solution)/shard_map/pallas_call | solution.py:38
  40.3 4.6 %collective-permute-start.14 = (f32[9,64,128]{2,1,0:T(8,128)S(1)}, f32[9,64,128]{2,1,0:T(8,128)S(1)}, u32[]{:S(2)}, u32[]{:S(2)}) collective-permute-start(f32[9,64,128]{2,1,0:T(8,128)S(1)} %get-tuple-element.100), channel_id=1, source_target_pairs={{4,8},{12,16},{20,24},{8,4},{16,12},{24,20},{5,9},{13,17},{21,25},... | collective-permute-start | bytes 884744 | tf_op jit(solution)/shard_map/ppermute | solution.py:417
  44.9 1.2 %shard_map.75 = (f32[3,10,144,128]{3,2,1,0:T(8,128)S(1)}, f32[3,7,144,128]{3,2,1,0:T(8,128)S(1)}, f32[3,4,144,128]{3,2,1,0:T(8,128)S(1)}, f32[3,10,144,128]{3,2,...) custom-call(f32[3,10,144,128]{3,2,1,0:T(8,128)S(1)} %get-tuple-eleme, ...), custom_call_target="tpu_custom_call", output_to_operand_aliasing={{0}: (0, {}), {1}: (11, {}), {2}: (12, {}), {3}: (13, {})} | custom-call | flops 5000000000 | bytes 18000000 | tf_op jit(solution)/shard_map/pallas_call | solution.py:38
  46.2 2.6 %collective-permute-start.16 = (f32[9,64,128]{2,1,0:T(8,128)S(1)}, f32[9,64,128]{2,1,0:T(8,128)S(1)}, u32[]{:S(2)}, u32[]{:S(2)}) collective-permute-start(f32[9,64,128]{2,1,0:T(8,128)S(1)} %get-tuple-element.103), channel_id=1, source_target_pairs={{4,8},{12,16},{20,24},{8,4},{16,12},{24,20},{5,9},{13,17},{21,25},... | collective-permute-start | bytes 884744 | tf_op jit(solution)/shard_map/ppermute | solution.py:417
  48.8 3.6 %collective-permute-done.14.refs_3_ = f32[9,64,128]{2,1,0:T(8,128)S(1)} collective-permute-done((f32[9,64,128]{2,1,0:T(8,128)S(1)}, f32[9,64,128]{2,1,0:T(8,128)S(1)}, u32[]{:S(2)}, u32[]{:S(2)}) %collective-permute-start.14) | collective-permute-done | bytes 294944 | tf_op jit(solution)/shard_map/ppermute | solution.py:417
  52.4 1.1 %shard_map.76 = (f32[3,10,144,128]{3,2,1,0:T(8,128)S(1)}, f32[3,7,144,128]{3,2,1,0:T(8,128)S(1)}, f32[3,4,144,128]{3,2,1,0:T(8,128)S(1)}, f32[3,10,144,128]{3,2,...) custom-call(f32[3,10,144,128]{3,2,1,0:T(8,128)S(1)} %get-tuple-element.97., ...), custom_call_target="tpu_custom_call", output_to_operand_aliasing={{0}: (0, {})} | custom-call | flops 5000000000 | bytes 18000000 | tf_op jit(solution)/shard_map/pallas_call | solution.py:38
  53.5 2.6 %collective-permute-start.18 = (f32[9,56,128]{2,1,0:T(8,128)S(1)}, f32[9,56,128]{2,1,0:T(8,128)S(1)}, u32[]{:S(2)}, u32[]{:S(2)}) collective-permute-start(f32[9,56,128]{2,1,0:T(8,128)S(1)} %get-tuple-element.111), channel_id=1, source_target_pairs={{4,8},{12,16},{20,24},{8,4},{16,12},{24,20},{5,9},{13,17},{21,25},... | collective-permute-start | bytes 774152 | tf_op jit(solution)/shard_map/ppermute | solution.py:417
  56.3 2.5 %collective-permute-done.16.refs_3_ = f32[9,64,128]{2,1,0:T(8,128)S(1)} collective-permute-done((f32[9,64,128]{2,1,0:T(8,128)S(1)}, f32[9,64,128]{2,1,0:T(8,128)S(1)}, u32[]{:S(2)}, u32[]{:S(2)}) %collective-permute-start.16) | collective-permute-done | bytes 294944 | tf_op jit(solution)/shard_map/ppermute | solution.py:417
  58.7 1.3 %shard_map.77 = (f32[3,10,144,128]{3,2,1,0:T(8,128)S(1)}, f32[3,7,144,128]{3,2,1,0:T(8,128)S(1)}, f32[3,4,144,128]{3,2,1,0:T(8,128)S(1)}, f32[3,10,144,128]{3,2,...) custom-call(f32[3,10,144,128]{3,2,1,0:T(8,128)S(1)} %get-tuple-eleme, ...), custom_call_target="tpu_custom_call", output_to_operand_aliasing={{0}: (0, {}), {1}: (11, {}), {2}: (12, {}), {3}: (13, {})} | custom-call | flops 5000000000 | bytes 18000000 | tf_op jit(solution)/shard_map/pallas_call | solution.py:38
  60.0 2.6 %collective-permute-start.20 = (f32[9,72,128]{2,1,0:T(8,128)S(1)}, f32[9,72,128]{2,1,0:T(8,128)S(1)}, u32[]{:S(2)}, u32[]{:S(2)}) collective-permute-start(f32[9,72,128]{2,1,0:T(8,128)S(1)} %get-tuple-element.114), channel_id=1, source_target_pairs={{4,8},{12,16},{20,24},{8,4},{16,12},{24,20},{5,9},{13,17},{21,25},... | collective-permute-start | bytes 995336 | tf_op jit(solution)/shard_map/ppermute | solution.py:417
  62.7 1.5 %collective-permute-done.18.refs_3_ = f32[9,56,128]{2,1,0:T(8,128)S(1)} collective-permute-done((f32[9,56,128]{2,1,0:T(8,128)S(1)}, f32[9,56,128]{2,1,0:T(8,128)S(1)}, u32[]{:S(2)}, u32[]{:S(2)}) %collective-permute-start.18) | collective-permute-done | bytes 258080 | tf_op jit(solution)/shard_map/ppermute | solution.py:417
  65.2 2.4 %collective-permute-start.22 = (f32[5,48,128]{2,1,0:T(8,128)S(1)}, f32[5,48,128]{2,1,0:T(8,128)S(1)}, u32[]{:S(2)}, u32[]{:S(2)}) collective-permute-start(f32[5,48,128]{2,1,0:T(8,128)S(1)} %get-tuple-element.122), channel_id=1, source_target_pairs={{4,8},{12,16},{20,24},{8,4},{16,12},{24,20},{5,9},{13,17},{21,25},... | collective-permute-start | bytes 368648 | tf_op jit(solution)/shard_map/ppermute | solution.py:417
  67.7 5.1 %collective-permute-done.20.refs_3_ = f32[9,72,128]{2,1,0:T(8,128)S(1)} collective-permute-done((f32[9,72,128]{2,1,0:T(8,128)S(1)}, f32[9,72,128]{2,1,0:T(8,128)S(1)}, u32[]{:S(2)}, u32[]{:S(2)}) %collective-permute-start.20) | collective-permute-done | bytes 331808 | tf_op jit(solution)/shard_map/ppermute | solution.py:417
  72.9 1.4 %shard_map.79 = (f32[3,10,144,128]{3,2,1,0:T(8,128)S(1)}, f32[3,7,144,128]{3,2,1,0:T(8,128)S(1)}, f32[3,4,144,128]{3,2,1,0:T(8,128)S(1)}, f32[3,10,144,128]{3,2,...) custom-call(f32[3,10,144,128]{3,2,1,0:T(8,128)S(1)} %get-tuple-eleme, ...), custom_call_target="tpu_custom_call", output_to_operand_aliasing={{0}: (0, {}), {1}: (11, {}), {2}: (12, {}), {3}: (13, {})} | custom-call | flops 5000000000 | bytes 18000000 | tf_op jit(solution)/shard_map/pallas_call | solution.py:38
  74.3 2.6 %collective-permute-start.24 = (f32[5,80,128]{2,1,0:T(8,128)S(1)}, f32[5,80,128]{2,1,0:T(8,128)S(1)}, u32[]{:S(2)}, u32[]{:S(2)}) collective-permute-start(f32[5,80,128]{2,1,0:T(8,128)S(1)} %get-tuple-element.125), channel_id=1, source_target_pairs={{4,8},{12,16},{20,24},{8,4},{16,12},{24,20},{5,9},{13,17},{21,25},... | collective-permute-start | bytes 614408 | tf_op jit(solution)/shard_map/ppermute | solution.py:417
  77.0 1.2 %shard_map.80 = (f32[3,10,144,128]{3,2,1,0:T(8,128)S(1)}, f32[1,9,4,128,128]{4,3,2,1,0:T(8,128)}) custom-call(f32[3,10,144,128]{3,2,1,0:T(8,128)S(1)} %get-tuple-element.119.refs_0_, f32[3,7,144,128]{3,2,1,0:T(8,128)S(1)} %get-tuple-element.120.refs_1_, f32[3,4,144,128]{3,2,1,0:T(8,128)S(1)} %get-tuple-element.121.refs_2_, ...), custom_call_target="tpu_custom_call", output_to_operand_aliasing={{0}: (0, {})} | custom-call | flops 5000000000 | bytes 18000000 | tf_op jit(solution)/shard_map/pallas_call | solution.py:38
  78.2 4.1 %collective-permute-done.24.refs_3_ = f32[5,80,128]{2,1,0:T(8,128)S(1)} collective-permute-done((f32[5,80,128]{2,1,0:T(8,128)S(1)}, f32[5,80,128]{2,1,0:T(8,128)S(1)}, u32[]{:S(2)}, u32[]{:S(2)}) %collective-permute-start.24) | collective-permute-done | bytes 204832 | tf_op jit(solution)/shard_map/ppermute | solution.py:417
  82.3 1.7 %shard_map.81 = (f32[3,10,144,128]{3,2,1,0:T(8,128)S(1)}, f32[1,9,4,128,128]{4,3,2,1,0:T(8,128)}) custom-call(f32[3,10,144,128]{3,2,1,0:T(8,128)S(1)} %get-tuple-element.124.refs_0_, f32[3,7,144,128]{3,2,1,0:T(8,128)S(1)} %get-tuple-element.120.refs_1_, ...), custom_call_target="tpu_custom_call", output_to_operand_aliasing={{0}: (0, {}), {1}: (11, {})} | custom-call | flops 5000000000 | bytes 18000000 | tf_op jit(solution)/shard_map/pallas_call | solution.py:38
  (45 shorter events, 4.4 us)
Async XLA Ops:
  1.1 11.5 %collective-permute-start.3 = (f32[8,32,128]{2,1,0:T(8,128)S(1)}, f32[8,32,128]{2,1,0:T(8,128)S(1)}, u32[]{:S(2)}, u32[]{:S(2)}) collective-permute-start(f32[8,32,128]{2,1,0:T(8,128)S(1)} %get-tuple-element.75.refs_7_), channel_id=1, source_target_pairs={{0,3},{1,2},{2,1},{3,0},{4,7},{5,6},{6,5},{7,4},{8,11},{9,10},{10,... | collective-permute-start | bytes 393224 | tf_op jit(solution)/shard_map/ppermute | solution.py:381
  4.4 8.2 %collective-permute-start.2 = (f32[8,32,128]{2,1,0:T(8,128)S(1)}, f32[8,32,128]{2,1,0:T(8,128)S(1)}, u32[]{:S(2)}, u32[]{:S(2)}) collective-permute-start(f32[8,32,128]{2,1,0:T(8,128)S(1)} %get-tuple-element.75.refs_7_), channel_id=1, source_target_pairs={{0,1},{1,0},{2,3},{3,2},{4,5},{5,4},{6,7},{7,6},{8,9},{9,8},{10,11... | collective-permute-start | bytes 393224 | tf_op jit(solution)/shard_map/ppermute | solution.py:380
  4.4 8.0 %copy-start.1 = (s32[4,8,4,4]{1,3,2,0:T(4,128)S(1)}, s32[4,8,4,4]{1,3,2,0:T(4,128)}, u32[]{:S(2)}) copy-start(s32[4,8,4,4]{1,3,2,0:T(4,128)} %param.11) | copy-start | bytes 6148
  4.4 8.1 %collective-permute-start.4 = (f32[6,32,128]{2,1,0:T(8,128)S(1)}, f32[6,32,128]{2,1,0:T(8,128)S(1)}, u32[]{:S(2)}, u32[]{:S(2)}) collective-permute-start(f32[6,32,128]{2,1,0:T(8,128)S(1)} %get-tuple-element.67.refs_1_), channel_id=1, source_target_pairs={{4,8},{12,16},{20,24},{8,4},{16,12},{24,20},{5,9},{13,17},{21,25},... | collective-permute-start | bytes 294920 | tf_op jit(solution)/shard_map/ppermute | solution.py:431
  9.8 11.1 %collective-permute-start = (f32[5,128,128]{2,1,0:T(8,128)S(1)}, f32[5,128,128]{2,1,0:T(8,128)S(1)}, u32[]{:S(2)}, u32[]{:S(2)}) collective-permute-start(f32[5,128,128]{2,1,0:T(8,128)S(1)} %get-tuple-element.68), channel_id=1, source_target_pairs={{4,8},{12,16},{20,24},{8,4},{16,12},{24,20},{5,9},{13,17},{21,25},... | collective-permute-start | bytes 983048 | tf_op jit(solution)/shard_map/ppermute | solution.py:417
  12.3 8.6 %collective-permute-start.1 = (f32[5,128,128]{2,1,0:T(8,128)S(1)}, f32[5,128,128]{2,1,0:T(8,128)S(1)}, u32[]{:S(2)}, u32[]{:S(2)}) collective-permute-start(f32[5,128,128]{2,1,0:T(8,128)S(1)} %get-tuple-element.69), channel_id=1, source_target_pairs={{0,4},{8,12},{16,20},{24,28},{4,0},{12,8},{20,16},{28,24},{1,5},{9... | collective-permute-start | bytes 983048 | tf_op jit(solution)/shard_map/ppermute | solution.py:417
  12.6 5.7 %collective-permute-start.5 = (f32[8,32,128]{2,1,0:T(8,128)S(1)}, f32[8,32,128]{2,1,0:T(8,128)S(1)}, u32[]{:S(2)}, u32[]{:S(2)}) collective-permute-start(f32[8,32,128]{2,1,0:T(8,128)S(1)} %shard_map.67), channel_id=1, source_target_pairs={{0,1},{1,0},{2,3},{3,2},{4,5},{5,4},{6,7},{7,6},{8,9},{9,8},{10,11... | collective-permute-start | bytes 393224 | tf_op jit(solution)/shard_map/ppermute | solution.py:384
  14.4 1.7 %copy-start = (f32[1,9,4,128,128]{4,3,2,1,0:T(8,128)S(1)}, f32[1,9,4,128,128]{4,3,2,1,0:T(8,128)}, u32[]{:S(2)}) copy-start(f32[1,9,4,128,128]{4,3,2,1,0:T(8,128)} %refs_0_.5) | copy-start | bytes 7077892
  18.2 8.6 %collective-permute-start.9 = (f32[14,32,128]{2,1,0:T(8,128)S(1)}, f32[14,32,128]{2,1,0:T(8,128)S(1)}, u32[]{:S(2)}, u32[]{:S(2)}) collective-permute-start(f32[14,32,128]{2,1,0:T(8,128)S(1)} %shard_map.71.refs_1_), channel_id=1, source_target_pairs={{0,3},{1,2},{2,1},{3,0},{4,7},{5,6},{6,5},{7,4},{8,11},{9,10},{10,... | collective-permute-start | bytes 688136 | tf_op jit(solution)/shard_map/ppermute | solution.py:381
  18.3 11.4 %collective-permute-start.8 = (f32[14,32,128]{2,1,0:T(8,128)S(1)}, f32[14,32,128]{2,1,0:T(8,128)S(1)}, u32[]{:S(2)}, u32[]{:S(2)}) collective-permute-start(f32[14,32,128]{2,1,0:T(8,128)S(1)} %shard_map.71.refs_1_), channel_id=1, source_target_pairs={{0,1},{1,0},{2,3},{3,2},{4,5},{5,4},{6,7},{7,6},{8,9},{9,8},{10,11... | collective-permute-start | bytes 688136 | tf_op jit(solution)/shard_map/ppermute | solution.py:380
  21.2 16.6 %collective-permute-start.6 = (f32[9,72,128]{2,1,0:T(8,128)S(1)}, f32[9,72,128]{2,1,0:T(8,128)S(1)}, u32[]{:S(2)}, u32[]{:S(2)}) collective-permute-start(f32[9,72,128]{2,1,0:T(8,128)S(1)} %get-tuple-element.81), channel_id=1, source_target_pairs={{4,8},{12,16},{20,24},{8,4},{16,12},{24,20},{5,9},{13,17},{21,25},... | collective-permute-start | bytes 995336 | tf_op jit(solution)/shard_map/ppermute | solution.py:417
  25.2 12.6 %collective-permute-start.7 = (f32[9,72,128]{2,1,0:T(8,128)S(1)}, f32[9,72,128]{2,1,0:T(8,128)S(1)}, u32[]{:S(2)}, u32[]{:S(2)}) collective-permute-start(f32[9,72,128]{2,1,0:T(8,128)S(1)} %get-tuple-element.82), channel_id=1, source_target_pairs={{0,4},{8,12},{16,20},{24,28},{4,0},{12,8},{20,16},{28,24},{1,5},{9... | collective-permute-start | bytes 995336 | tf_op jit(solution)/shard_map/ppermute | solution.py:417
  25.5 10.0 %collective-permute-start.11 = (f32[9,56,128]{2,1,0:T(8,128)S(1)}, f32[9,56,128]{2,1,0:T(8,128)S(1)}, u32[]{:S(2)}, u32[]{:S(2)}) collective-permute-start(f32[9,56,128]{2,1,0:T(8,128)S(1)} %get-tuple-element.84), channel_id=1, source_target_pairs={{0,4},{8,12},{16,20},{24,28},{4,0},{12,8},{20,16},{28,24},{1,5},{9... | collective-permute-start | bytes 774152 | tf_op jit(solution)/shard_map/ppermute | solution.py:417
  29.6 5.9 %collective-permute-start.10 = (f32[14,32,128]{2,1,0:T(8,128)S(1)}, f32[14,32,128]{2,1,0:T(8,128)S(1)}, u32[]{:S(2)}, u32[]{:S(2)}) collective-permute-start(f32[14,32,128]{2,1,0:T(8,128)S(1)} %shard_map.72), channel_id=1, source_target_pairs={{0,1},{1,0},{2,3},{3,2},{4,5},{5,4},{6,7},{7,6},{8,9},{9,8},{10,11... | collective-permute-start | bytes 688136 | tf_op jit(solution)/shard_map/ppermute | solution.py:384
  30.0 14.9 %collective-permute-start.13 = (f32[9,56,128]{2,1,0:T(8,128)S(1)}, f32[9,56,128]{2,1,0:T(8,128)S(1)}, u32[]{:S(2)}, u32[]{:S(2)}) collective-permute-start(f32[9,56,128]{2,1,0:T(8,128)S(1)} %get-tuple-element.90), channel_id=1, source_target_pairs={{4,8},{12,16},{20,24},{8,4},{16,12},{24,20},{5,9},{13,17},{21,25},... | collective-permute-start | bytes 774152 | tf_op jit(solution)/shard_map/ppermute | solution.py:417
  35.6 3.6 %collective-permute-start.12 = (f32[6,128,128]{2,1,0:T(8,128)S(1)}, f32[6,128,128]{2,1,0:T(8,128)S(1)}, u32[]{:S(2)}, u32[]{:S(2)}) collective-permute-start(f32[6,128,128]{2,1,0:T(8,128)S(1)} %get-tuple-element.88), channel_id=1, source_target_pairs={{0,4},{8,12},{16,20},{24,28},{4,0},{12,8},{20,16},{28,24},{1,5},{9... | collective-permute-start | bytes 1179656 | tf_op jit(solution)/shard_map/ppermute | solution.py:519
  40.3 12.1 %collective-permute-start.14 = (f32[9,64,128]{2,1,0:T(8,128)S(1)}, f32[9,64,128]{2,1,0:T(8,128)S(1)}, u32[]{:S(2)}, u32[]{:S(2)}) collective-permute-start(f32[9,64,128]{2,1,0:T(8,128)S(1)} %get-tuple-element.100), channel_id=1, source_target_pairs={{4,8},{12,16},{20,24},{8,4},{16,12},{24,20},{5,9},{13,17},{21,25},... | collective-permute-start | bytes 884744 | tf_op jit(solution)/shard_map/ppermute | solution.py:417
  44.9 7.5 %collective-permute-start.15 = (f32[9,64,128]{2,1,0:T(8,128)S(1)}, f32[9,64,128]{2,1,0:T(8,128)S(1)}, u32[]{:S(2)}, u32[]{:S(2)}) collective-permute-start(f32[9,64,128]{2,1,0:T(8,128)S(1)} %get-tuple-element.101), channel_id=1, source_target_pairs={{0,4},{8,12},{16,20},{24,28},{4,0},{12,8},{20,16},{28,24},{1,5},{9... | collective-permute-start | bytes 884744 | tf_op jit(solution)/shard_map/ppermute | solution.py:417
  46.2 12.6 %collective-permute-start.16 = (f32[9,64,128]{2,1,0:T(8,128)S(1)}, f32[9,64,128]{2,1,0:T(8,128)S(1)}, u32[]{:S(2)}, u32[]{:S(2)}) collective-permute-start(f32[9,64,128]{2,1,0:T(8,128)S(1)} %get-tuple-element.103), channel_id=1, source_target_pairs={{4,8},{12,16},{20,24},{8,4},{16,12},{24,20},{5,9},{13,17},{21,25},... | collective-permute-start | bytes 884744 | tf_op jit(solution)/shard_map/ppermute | solution.py:417
  48.7 10.0 %collective-permute-start.17 = (f32[9,64,128]{2,1,0:T(8,128)S(1)}, f32[9,64,128]{2,1,0:T(8,128)S(1)}, u32[]{:S(2)}, u32[]{:S(2)}) collective-permute-start(f32[9,64,128]{2,1,0:T(8,128)S(1)} %get-tuple-element.104), channel_id=1, source_target_pairs={{0,4},{8,12},{16,20},{24,28},{4,0},{12,8},{20,16},{28,24},{1,5},{9... | collective-permute-start | bytes 884744 | tf_op jit(solution)/shard_map/ppermute | solution.py:417
  53.5 10.7 %collective-permute-start.18 = (f32[9,56,128]{2,1,0:T(8,128)S(1)}, f32[9,56,128]{2,1,0:T(8,128)S(1)}, u32[]{:S(2)}, u32[]{:S(2)}) collective-permute-start(f32[9,56,128]{2,1,0:T(8,128)S(1)} %get-tuple-element.111), channel_id=1, source_target_pairs={{4,8},{12,16},{20,24},{8,4},{16,12},{24,20},{5,9},{13,17},{21,25},... | collective-permute-start | bytes 774152 | tf_op jit(solution)/shard_map/ppermute | solution.py:417
  56.2 8.1 %collective-permute-start.19 = (f32[9,56,128]{2,1,0:T(8,128)S(1)}, f32[9,56,128]{2,1,0:T(8,128)S(1)}, u32[]{:S(2)}, u32[]{:S(2)}) collective-permute-start(f32[9,56,128]{2,1,0:T(8,128)S(1)} %get-tuple-element.112), channel_id=1, source_target_pairs={{0,4},{8,12},{16,20},{24,28},{4,0},{12,8},{20,16},{28,24},{1,5},{9... | collective-permute-start | bytes 774152 | tf_op jit(solution)/shard_map/ppermute | solution.py:417
  60.0 12.9 %collective-permute-start.20 = (f32[9,72,128]{2,1,0:T(8,128)S(1)}, f32[9,72,128]{2,1,0:T(8,128)S(1)}, u32[]{:S(2)}, u32[]{:S(2)}) collective-permute-start(f32[9,72,128]{2,1,0:T(8,128)S(1)} %get-tuple-element.114), channel_id=1, source_target_pairs={{4,8},{12,16},{20,24},{8,4},{16,12},{24,20},{5,9},{13,17},{21,25},... | collective-permute-start | bytes 995336 | tf_op jit(solution)/shard_map/ppermute | solution.py:417
  62.7 10.2 %collective-permute-start.21 = (f32[9,72,128]{2,1,0:T(8,128)S(1)}, f32[9,72,128]{2,1,0:T(8,128)S(1)}, u32[]{:S(2)}, u32[]{:S(2)}) collective-permute-start(f32[9,72,128]{2,1,0:T(8,128)S(1)} %get-tuple-element.115), channel_id=1, source_target_pairs={{0,4},{8,12},{16,20},{24,28},{4,0},{12,8},{20,16},{28,24},{1,5},{9... | collective-permute-start | bytes 995336 | tf_op jit(solution)/shard_map/ppermute | solution.py:417
  65.2 11.7 %collective-permute-start.22 = (f32[5,48,128]{2,1,0:T(8,128)S(1)}, f32[5,48,128]{2,1,0:T(8,128)S(1)}, u32[]{:S(2)}, u32[]{:S(2)}) collective-permute-start(f32[5,48,128]{2,1,0:T(8,128)S(1)} %get-tuple-element.122), channel_id=1, source_target_pairs={{4,8},{12,16},{20,24},{8,4},{16,12},{24,20},{5,9},{13,17},{21,25},... | collective-permute-start | bytes 368648 | tf_op jit(solution)/shard_map/ppermute | solution.py:417
  67.7 9.3 %collective-permute-start.23 = (f32[5,48,128]{2,1,0:T(8,128)S(1)}, f32[5,48,128]{2,1,0:T(8,128)S(1)}, u32[]{:S(2)}, u32[]{:S(2)}) collective-permute-start(f32[5,48,128]{2,1,0:T(8,128)S(1)} %get-tuple-element.123), channel_id=1, source_target_pairs={{0,4},{8,12},{16,20},{24,28},{4,0},{12,8},{20,16},{28,24},{1,5},{9... | collective-permute-start | bytes 368648 | tf_op jit(solution)/shard_map/ppermute | solution.py:417
  74.3 8.0 %collective-permute-start.24 = (f32[5,80,128]{2,1,0:T(8,128)S(1)}, f32[5,80,128]{2,1,0:T(8,128)S(1)}, u32[]{:S(2)}, u32[]{:S(2)}) collective-permute-start(f32[5,80,128]{2,1,0:T(8,128)S(1)} %get-tuple-element.125), channel_id=1, source_target_pairs={{4,8},{12,16},{20,24},{8,4},{16,12},{24,20},{5,9},{13,17},{21,25},... | collective-permute-start | bytes 614408 | tf_op jit(solution)/shard_map/ppermute | solution.py:417
  76.9 5.4 %collective-permute-start.25 = (f32[5,80,128]{2,1,0:T(8,128)S(1)}, f32[5,80,128]{2,1,0:T(8,128)S(1)}, u32[]{:S(2)}, u32[]{:S(2)}) collective-permute-start(f32[5,80,128]{2,1,0:T(8,128)S(1)} %get-tuple-element.126), channel_id=1, source_target_pairs={{0,4},{8,12},{16,20},{24,28},{4,0},{12,8},{20,16},{28,24},{1,5},{9... | collective-permute-start | bytes 614408 | tf_op jit(solution)/shard_map/ppermute | solution.py:417

commit v4 on v3

--- a/solution.py
+++ b/solution.py
@@ -378,11 +378,11 @@
     pairs = lambda k: [(i, i ^ k) for i in range(shots)]
     if shots == 4:
         beside = lax.ppermute(mine, "shot", pairs(1))
-        across = lax.ppermute(mine, "shot", pairs(3))
+        across = lax.ppermute(mine, "shot", pairs(2))
 
         def finish(*others):
             handed = lax.ppermute(hold(across, beside, *others), "shot", pairs(1))
-            return {0: mine, 1: beside, 2: handed, 3: across}
+            return {0: mine, 1: beside, 2: across, 3: handed}
 
         return (beside, across), finish
     turn = lambda k: [(i, (i + k) % shots) for i in range(shots)]
@@ -422,13 +422,13 @@
         dict(first=(2 * cx,) + panel, second=(2 * cx,) + panel, edge=(MODEL_SLOTS,) + panel),
         scratch=[pltpu.SemaphoreType.DMA((7,))], anywhere=("lam", "mu", "buoy", "q"), us=0.02,
     )
+    edge = lax.ppermute(sent["edge"], "aper", far)
     sent.update(call(
         functools.partial(pack_stress, cx), dict(wave=wave),
         dict(far=(STRESS_SLOTS, rows, lanes), near=(STRESS_SLOTS, rows, lanes)),
-        scratch=[pltpu.SemaphoreType.DMA((2 * STRESS_SLOTS,))], anywhere=("wave",), us=5.0, waits=(sent["edge"],),
+        scratch=[pltpu.SemaphoreType.DMA((2 * STRESS_SLOTS,))], anywhere=("wave",), us=5.0, waits=(edge,),
     ))
     halo_far, halo_near = exchange(sent["far"], sent["near"])
-    edge = lax.ppermute(sent["edge"], "aper", far)
     sh_shape, so_shape = (3, cx + 3, padded, lanes), (3, cx, padded, lanes)
     vel_shape, slab_shape = (3, cx + 2 * REACH, padded, lanes), (cx, rows, lanes)
     state = call(functools.partial(prepare, plan), dict(wave=wave, active=active.reshape(-1, lane_blocks)),

time: 84.5 us -> 83.3 us (0.986)
  waiting for transfers between devices: 24.2 us -> 20.1 us
  starting transfers between devices: 42.6 us -> 46.3 us
  local copies, waits for them, and re-layouts: 1.87 us -> 0.95 us
    ppermute x9, starting transfers between devices: 29.4 us -> 32.3 us  [exchange(): lax.ppermute(to_far, 'aper', far)]
    ppermute x9, waiting for transfers between devices: 19.3 us -> 16.4 us  [exchange(): lax.ppermute(to_far, 'aper', far)]
    ppermute x2, waiting for transfers between devices: 2.81 us -> 0.01 us  [spread(): beside = lax.ppermute(mine, 'shot', pairs(1))]
    ppermute x2, waiting for transfers between devices: 0.78 us -> 2.4 us  [spread(): across = lax.ppermute(mine, 'shot', pairs(2))]
    ppermute x2, starting transfers between devices: 0.08 us -> 1.32 us  [spread(): beside = lax.ppermute(mine, 'shot', pairs(1))]
    ppermute x2, starting transfers between devices: 3.46 us -> 4.52 us  [spread(): across = lax.ppermute(mine, 'shot', pairs(2))]
    unnamed x7 -> x5, local copies, waits for them, and re-layouts: 1.87 us -> 0.95 us
  transfers between devices with their start and end apart: 26 -> 26, of which waited for: 9 -> 7; matrix products, arithmetic and copies ran while one was open for 0% -> 1% of each run, Pallas kernels for 15% -> 15%
where the time goes in v4:
time: 83.3 us; the launch traced here: 82.8 us
  starting transfers between devices  46.3 us (56%)
  waiting for transfers between devices  20.1 us (24%)
  Pallas kernels  15.1 us (18%)
  local copies, waits for them, and re-layouts  0.95 us (1%)
    ppermute x9, starting transfers between devices, exchange(): lax.ppermute(to_far, 'aper', far)  32.3 us
    ppermute x9, waiting for transfers between devices, exchange(): lax.ppermute(to_far, 'aper', far)  16.4 us
    pallas_call x18, Pallas kernels, call(): pl.pallas_call(kernel, out_shape=[pltpu.HBM(shape, F32) if name in anywhe...  15.1 us
    ppermute x2, starting transfers between devices, spread(): across = lax.ppermute(mine, 'shot', pairs(2))  4.52 us
    ppermute x1, starting transfers between devices, per_device(): edge = lax.ppermute(sent['edge'], 'aper', far)  3.68 us
    ppermute x2, waiting for transfers between devices, spread(): across = lax.ppermute(mine, 'shot', pairs(2))  2.4 us
    ppermute x1, starting transfers between devices, per_device(): model_near = lax.ppermute(got['send_model'], 'aper', near)  1.96 us
  transfers between devices with their start and end apart: 26, of which 7 were waited for; matrix products, arithmetic and copies ran while one was open for 1% of the time, Pallas kernels for 15%

profile of v4, /device:TPU:3, one launch (start us, length us, event | category | flops | bytes accessed | tf_op | source)
XLA Modules:
  0.0 82.8 jit_solution(17270970344159435311)
XLA Ops:
  0.0 1.0 %shard_map.64 = (f32[8,32,128]{2,1,0:T(8,128)S(1)}, f32[8,32,128]{2,1,0:T(8,128)S(1)}, f32[6,32,128]{2,1,0:T(8,128)S(1)}) custom-call(f32[4,32,128]{2,1,0:T(8,128)} %refs_0_.3, f32[4,32,128]{2,1,0:T(8,128)} %refs_1_.1, f32[4,32,128]{2,1,0:T(8,128)} %refs_2_.1, f32[4,32,128]{2,1,0:T(8,128)} %refs_3_.1), custom_call_target="tpu_custom_call" | custom-call | flops 20000000 | bytes 72000 | tf_op jit(solution)/shard_map/pallas_call | solution.py:38
  1.1 3.7 %collective-permute-start = (f32[6,32,128]{2,1,0:T(8,128)S(1)}, f32[6,32,128]{2,1,0:T(8,128)S(1)}, u32[]{:S(2)}, u32[]{:S(2)}) collective-permute-start(f32[6,32,128]{2,1,0:T(8,128)S(1)} %get-tuple-element.67), channel_id=1, source_target_pairs={{4,8},{12,16},{20,24},{8,4},{16,12},{24,20},{5,9},{13,17},{21,25},... | collective-permute-start | bytes 294920 | tf_op jit(solution)/shard_map/ppermute | solution.py:425
  4.7 2.4 %collective-permute-start.4 = (f32[8,32,128]{2,1,0:T(8,128)S(1)}, f32[8,32,128]{2,1,0:T(8,128)S(1)}, u32[]{:S(2)}, u32[]{:S(2)}) collective-permute-start(f32[8,32,128]{2,1,0:T(8,128)S(1)} %get-tuple-element.75.refs_7_), channel_id=1, source_target_pairs={{0,2},{1,3},{2,0},{3,1},{4,6},{5,7},{6,4},{7,5},{8,10},{9,11},{10,... | collective-permute-start | bytes 393224 | tf_op jit(solution)/shard_map/ppermute | solution.py:381
  7.1 1.3 %collective-permute-start.3 = (f32[8,32,128]{2,1,0:T(8,128)S(1)}, f32[8,32,128]{2,1,0:T(8,128)S(1)}, u32[]{:S(2)}, u32[]{:S(2)}) collective-permute-start(f32[8,32,128]{2,1,0:T(8,128)S(1)} %get-tuple-element.75.refs_7_), channel_id=1, source_target_pairs={{0,1},{1,0},{2,3},{3,2},{4,5},{5,4},{6,7},{7,6},{8,9},{9,8},{10,11... | collective-permute-start | bytes 393224 | tf_op jit(solution)/shard_map/ppermute | solution.py:380
  9.3 1.4 %shard_map.65 = (f32[5,128,128]{2,1,0:T(8,128)S(1)}, f32[5,128,128]{2,1,0:T(8,128)S(1)}) custom-call(f32[1,9,4,128,128]{4,3,2,1,0:T(8,128)} %refs_0_.5, f32[6,32,128]{2,1,0:T(8,128)S(1)} %collective-permute-done.refs_1_.refs_2_), custom_call_target="tpu_custom_call" | custom-call | flops 5000000000 | bytes 18000000 | tf_op jit(solution)/shard_map/pallas_call | solution.py:38
  10.7 3.3 %collective-permute-start.1 = (f32[5,128,128]{2,1,0:T(8,128)S(1)}, f32[5,128,128]{2,1,0:T(8,128)S(1)}, u32[]{:S(2)}, u32[]{:S(2)}) collective-permute-start(f32[5,128,128]{2,1,0:T(8,128)S(1)} %get-tuple-element.68), channel_id=1, source_target_pairs={{4,8},{12,16},{20,24},{8,4},{16,12},{24,20},{5,9},{13,17},{21,25},... | collective-permute-start | bytes 983048 | tf_op jit(solution)/shard_map/ppermute | solution.py:417
  14.9 2.1 %shard_map.66 = (f32[3,7,144,128]{3,2,1,0:T(8,128)S(1)}, f32[3,4,144,128]{3,2,1,0:T(8,128)S(1)}, f32[3,4,128,128]{3,2,1,0:T(8,128)S(1)}, f32[3,4,128,128]{3,2,1,0:T(8,128)S(1)}, f32[128,128]{1,0:T(8,128)S(1)}) custom-call(f32[1,9,4,128,128]{4,3,2,1,0:T(8,128)S(1)} %copy-done, s32[128,4]{1,0:T(8,128)S(1)} %bitcast.1), custom_call_target="tpu_custom_call" | custom-call | flops 5000000000 | bytes 18000000 | tf_op jit(solution)/shard_map/pallas_call | solution.py:38
  16.9 2.1 %collective-permute-start.9 = (f32[14,32,128]{2,1,0:T(8,128)S(1)}, f32[14,32,128]{2,1,0:T(8,128)S(1)}, u32[]{:S(2)}, u32[]{:S(2)}) collective-permute-start(f32[14,32,128]{2,1,0:T(8,128)S(1)} %shard_map.71.refs_1_), channel_id=1, source_target_pairs={{0,2},{1,3},{2,0},{3,1},{4,6},{5,7},{6,4},{7,5},{8,10},{9,11},{10,... | collective-permute-start | bytes 688136 | tf_op jit(solution)/shard_map/ppermute | solution.py:381
  19.1 3.2 %collective-permute-done.1.refs_0_ = f32[5,128,128]{2,1,0:T(8,128)S(1)} collective-permute-done((f32[5,128,128]{2,1,0:T(8,128)S(1)}, f32[5,128,128]{2,1,0:T(8,128)S(1)}, u32[]{:S(2)}, u32[]{:S(2)}) %collective-permute-start.1) | collective-permute-done | bytes 327712 | tf_op jit(solution)/shard_map/ppermute | solution.py:417
  22.7 3.9 %collective-permute-start.6 = (f32[9,72,128]{2,1,0:T(8,128)S(1)}, f32[9,72,128]{2,1,0:T(8,128)S(1)}, u32[]{:S(2)}, u32[]{:S(2)}) collective-permute-start(f32[9,72,128]{2,1,0:T(8,128)S(1)} %get-tuple-element.81), channel_id=1, source_target_pairs={{4,8},{12,16},{20,24},{8,4},{16,12},{24,20},{5,9},{13,17},{21,25},... | collective-permute-start | bytes 995336 | tf_op jit(solution)/shard_map/ppermute | solution.py:417
  27.4 2.4 %collective-permute-done.9.refs_3_ = f32[14,32,128]{2,1,0:T(8,128)S(1)} collective-permute-done((f32[14,32,128]{2,1,0:T(8,128)S(1)}, f32[14,32,128]{2,1,0:T(8,128)S(1)}, u32[]{:S(2)}, u32[]{:S(2)}) %collective-permute-start.9) | collective-permute-done | bytes 229408 | tf_op jit(solution)/shard_map/ppermute | solution.py:381
  30.6 5.5 %collective-permute-start.13 = (f32[9,56,128]{2,1,0:T(8,128)S(1)}, f32[9,56,128]{2,1,0:T(8,128)S(1)}, u32[]{:S(2)}, u32[]{:S(2)}) collective-permute-start(f32[9,56,128]{2,1,0:T(8,128)S(1)} %get-tuple-element.90), channel_id=1, source_target_pairs={{4,8},{12,16},{20,24},{8,4},{16,12},{24,20},{5,9},{13,17},{21,25},... | collective-permute-start | bytes 774152 | tf_op jit(solution)/shard_map/ppermute | solution.py:417
  36.2 2.0 %collective-permute-start.12 = (f32[6,128,128]{2,1,0:T(8,128)S(1)}, f32[6,128,128]{2,1,0:T(8,128)S(1)}, u32[]{:S(2)}, u32[]{:S(2)}) collective-permute-start(f32[6,128,128]{2,1,0:T(8,128)S(1)} %get-tuple-element.88), channel_id=1, source_target_pairs={{0,4},{8,12},{16,20},{24,28},{4,0},{12,8},{20,16},{28,24},{1,5},{9... | collective-permute-start | bytes 1179656 | tf_op jit(solution)/shard_map/ppermute | solution.py:519
  38.2 1.3 %collective-permute-done.12.refs_11_ = f32[6,128,128]{2,1,0:T(8,128)S(1)} collective-permute-done((f32[6,128,128]{2,1,0:T(8,128)S(1)}, f32[6,128,128]{2,1,0:T(8,128)S(1)}, u32[]{:S(2)}, u32[]{:S(2)}) %collective-permute-start.12) | collective-permute-done | bytes 393248 | tf_op jit(solution)/shard_map/ppermute | solution.py:519
  39.5 1.1 %shard_map.74 = (f32[3,10,144,128]{3,2,1,0:T(8,128)S(1)}, f32[3,7,144,128]{3,2,1,0:T(8,128)S(1)}, f32[3,4,144,128]{3,2,1,0:T(8,128)S(1)}, f32[3,10,144,128]{3,2,...) custom-call(f32[3,10,144,128]{3,2,1,0:T(8,128)S(1)} %shard_map.70.re, ...), custom_call_target="tpu_custom_call", output_to_operand_aliasing={{0}: (0, {}), {4}: (8, {}), {5}: (9, {}), {6}: (10, {})} | custom-call | flops 5000000000 | bytes 18000000 | tf_op jit(solution)/shard_map/pallas_call | solution.py:38
  40.6 3.8 %collective-permute-start.14 = (f32[9,64,128]{2,1,0:T(8,128)S(1)}, f32[9,64,128]{2,1,0:T(8,128)S(1)}, u32[]{:S(2)}, u32[]{:S(2)}) collective-permute-start(f32[9,64,128]{2,1,0:T(8,128)S(1)} %get-tuple-element.100), channel_id=1, source_target_pairs={{4,8},{12,16},{20,24},{8,4},{16,12},{24,20},{5,9},{13,17},{21,25},... | collective-permute-start | bytes 884744 | tf_op jit(solution)/shard_map/ppermute | solution.py:417
  44.5 1.2 %shard_map.75 = (f32[3,10,144,128]{3,2,1,0:T(8,128)S(1)}, f32[3,7,144,128]{3,2,1,0:T(8,128)S(1)}, f32[3,4,144,128]{3,2,1,0:T(8,128)S(1)}, f32[3,10,144,128]{3,2,...) custom-call(f32[3,10,144,128]{3,2,1,0:T(8,128)S(1)} %get-tuple-eleme, ...), custom_call_target="tpu_custom_call", output_to_operand_aliasing={{0}: (0, {}), {1}: (11, {}), {2}: (12, {}), {3}: (13, {})} | custom-call | flops 5000000000 | bytes 18000000 | tf_op jit(solution)/shard_map/pallas_call | solution.py:38
  45.7 2.6 %collective-permute-start.16 = (f32[9,64,128]{2,1,0:T(8,128)S(1)}, f32[9,64,128]{2,1,0:T(8,128)S(1)}, u32[]{:S(2)}, u32[]{:S(2)}) collective-permute-start(f32[9,64,128]{2,1,0:T(8,128)S(1)} %get-tuple-element.103), channel_id=1, source_target_pairs={{4,8},{12,16},{20,24},{8,4},{16,12},{24,20},{5,9},{13,17},{21,25},... | collective-permute-start | bytes 884744 | tf_op jit(solution)/shard_map/ppermute | solution.py:417
  48.4 4.3 %collective-permute-done.14.refs_3_ = f32[9,64,128]{2,1,0:T(8,128)S(1)} collective-permute-done((f32[9,64,128]{2,1,0:T(8,128)S(1)}, f32[9,64,128]{2,1,0:T(8,128)S(1)}, u32[]{:S(2)}, u32[]{:S(2)}) %collective-permute-start.14) | collective-permute-done | bytes 294944 | tf_op jit(solution)/shard_map/ppermute | solution.py:417
  52.7 1.1 %shard_map.76 = (f32[3,10,144,128]{3,2,1,0:T(8,128)S(1)}, f32[3,7,144,128]{3,2,1,0:T(8,128)S(1)}, f32[3,4,144,128]{3,2,1,0:T(8,128)S(1)}, f32[3,10,144,128]{3,2,...) custom-call(f32[3,10,144,128]{3,2,1,0:T(8,128)S(1)} %get-tuple-element.97., ...), custom_call_target="tpu_custom_call", output_to_operand_aliasing={{0}: (0, {})} | custom-call | flops 5000000000 | bytes 18000000 | tf_op jit(solution)/shard_map/pallas_call | solution.py:38
  53.9 3.4 %collective-permute-start.18 = (f32[9,56,128]{2,1,0:T(8,128)S(1)}, f32[9,56,128]{2,1,0:T(8,128)S(1)}, u32[]{:S(2)}, u32[]{:S(2)}) collective-permute-start(f32[9,56,128]{2,1,0:T(8,128)S(1)} %get-tuple-element.111), channel_id=1, source_target_pairs={{4,8},{12,16},{20,24},{8,4},{16,12},{24,20},{5,9},{13,17},{21,25},... | collective-permute-start | bytes 774152 | tf_op jit(solution)/shard_map/ppermute | solution.py:417
  57.3 1.7 %collective-permute-done.16.refs_3_ = f32[9,64,128]{2,1,0:T(8,128)S(1)} collective-permute-done((f32[9,64,128]{2,1,0:T(8,128)S(1)}, f32[9,64,128]{2,1,0:T(8,128)S(1)}, u32[]{:S(2)}, u32[]{:S(2)}) %collective-permute-start.16) | collective-permute-done | bytes 294944 | tf_op jit(solution)/shard_map/ppermute | solution.py:417
  59.0 1.3 %shard_map.77 = (f32[3,10,144,128]{3,2,1,0:T(8,128)S(1)}, f32[3,7,144,128]{3,2,1,0:T(8,128)S(1)}, f32[3,4,144,128]{3,2,1,0:T(8,128)S(1)}, f32[3,10,144,128]{3,2,...) custom-call(f32[3,10,144,128]{3,2,1,0:T(8,128)S(1)} %get-tuple-eleme, ...), custom_call_target="tpu_custom_call", output_to_operand_aliasing={{0}: (0, {}), {1}: (11, {}), {2}: (12, {}), {3}: (13, {})} | custom-call | flops 5000000000 | bytes 18000000 | tf_op jit(solution)/shard_map/pallas_call | solution.py:38
  60.3 3.4 %collective-permute-start.20 = (f32[9,72,128]{2,1,0:T(8,128)S(1)}, f32[9,72,128]{2,1,0:T(8,128)S(1)}, u32[]{:S(2)}, u32[]{:S(2)}) collective-permute-start(f32[9,72,128]{2,1,0:T(8,128)S(1)} %get-tuple-element.114), channel_id=1, source_target_pairs={{4,8},{12,16},{20,24},{8,4},{16,12},{24,20},{5,9},{13,17},{21,25},... | collective-permute-start | bytes 995336 | tf_op jit(solution)/shard_map/ppermute | solution.py:417
  63.8 1.0 %shard_map.78 = (f32[3,10,144,128]{3,2,1,0:T(8,128)S(1)}, f32[3,7,144,128]{3,2,1,0:T(8,128)S(1)}, f32[3,4,144,128]{3,2,1,0:T(8,128)S(1)}, f32[3,10,144,128]{3,2,...) custom-call(f32[3,10,144,128]{3,2,1,0:T(8,128)S(1)} %get-tuple-element.108, ...), custom_call_target="tpu_custom_call", output_to_operand_aliasing={{0}: (0, {})} | custom-call | flops 5000000000 | bytes 18000000 | tf_op jit(solution)/shard_map/pallas_call | solution.py:38
  64.8 3.2 %collective-permute-start.22 = (f32[5,48,128]{2,1,0:T(8,128)S(1)}, f32[5,48,128]{2,1,0:T(8,128)S(1)}, u32[]{:S(2)}, u32[]{:S(2)}) collective-permute-start(f32[5,48,128]{2,1,0:T(8,128)S(1)} %get-tuple-element.122), channel_id=1, source_target_pairs={{4,8},{12,16},{20,24},{8,4},{16,12},{24,20},{5,9},{13,17},{21,25},... | collective-permute-start | bytes 368648 | tf_op jit(solution)/shard_map/ppermute | solution.py:417
  68.1 3.7 %collective-permute-done.20.refs_3_ = f32[9,72,128]{2,1,0:T(8,128)S(1)} collective-permute-done((f32[9,72,128]{2,1,0:T(8,128)S(1)}, f32[9,72,128]{2,1,0:T(8,128)S(1)}, u32[]{:S(2)}, u32[]{:S(2)}) %collective-permute-start.20) | collective-permute-done | bytes 331808 | tf_op jit(solution)/shard_map/ppermute | solution.py:417
  71.7 1.4 %shard_map.79 = (f32[3,10,144,128]{3,2,1,0:T(8,128)S(1)}, f32[3,7,144,128]{3,2,1,0:T(8,128)S(1)}, f32[3,4,144,128]{3,2,1,0:T(8,128)S(1)}, f32[3,10,144,128]{3,2,...) custom-call(f32[3,10,144,128]{3,2,1,0:T(8,128)S(1)} %get-tuple-eleme, ...), custom_call_target="tpu_custom_call", output_to_operand_aliasing={{0}: (0, {}), {1}: (11, {}), {2}: (12, {}), {3}: (13, {})} | custom-call | flops 5000000000 | bytes 18000000 | tf_op jit(solution)/shard_map/pallas_call | solution.py:38
  73.1 3.2 %collective-permute-start.24 = (f32[5,80,128]{2,1,0:T(8,128)S(1)}, f32[5,80,128]{2,1,0:T(8,128)S(1)}, u32[]{:S(2)}, u32[]{:S(2)}) collective-permute-start(f32[5,80,128]{2,1,0:T(8,128)S(1)} %get-tuple-element.125), channel_id=1, source_target_pairs={{4,8},{12,16},{20,24},{8,4},{16,12},{24,20},{5,9},{13,17},{21,25},... | collective-permute-start | bytes 614408 | tf_op jit(solution)/shard_map/ppermute | solution.py:417
  76.5 1.2 %shard_map.80 = (f32[3,10,144,128]{3,2,1,0:T(8,128)S(1)}, f32[1,9,4,128,128]{4,3,2,1,0:T(8,128)}) custom-call(f32[3,10,144,128]{3,2,1,0:T(8,128)S(1)} %get-tuple-element.119.refs_0_, f32[3,7,144,128]{3,2,1,0:T(8,128)S(1)} %get-tuple-element.120.refs_1_, f32[3,4,144,128]{3,2,1,0:T(8,128)S(1)} %get-tuple-element.121.refs_2_, ...), custom_call_target="tpu_custom_call", output_to_operand_aliasing={{0}: (0, {})} | custom-call | flops 5000000000 | bytes 18000000 | tf_op jit(solution)/shard_map/pallas_call | solution.py:38
  77.6 3.5 %collective-permute-done.24.refs_3_ = f32[5,80,128]{2,1,0:T(8,128)S(1)} collective-permute-done((f32[5,80,128]{2,1,0:T(8,128)S(1)}, f32[5,80,128]{2,1,0:T(8,128)S(1)}, u32[]{:S(2)}, u32[]{:S(2)}) %collective-permute-start.24) | collective-permute-done | bytes 204832 | tf_op jit(solution)/shard_map/ppermute | solution.py:417
  81.1 1.7 %shard_map.81 = (f32[3,10,144,128]{3,2,1,0:T(8,128)S(1)}, f32[1,9,4,128,128]{4,3,2,1,0:T(8,128)}) custom-call(f32[3,10,144,128]{3,2,1,0:T(8,128)S(1)} %get-tuple-element.124.refs_0_, f32[3,7,144,128]{3,2,1,0:T(8,128)S(1)} %get-tuple-element.120.refs_1_, ...), custom_call_target="tpu_custom_call", output_to_operand_aliasing={{0}: (0, {}), {1}: (11, {})} | custom-call | flops 5000000000 | bytes 18000000 | tf_op jit(solution)/shard_map/pallas_call | solution.py:38
  (43 shorter events, 4.2 us)
Async XLA Ops:
  1.1 8.3 %collective-permute-start = (f32[6,32,128]{2,1,0:T(8,128)S(1)}, f32[6,32,128]{2,1,0:T(8,128)S(1)}, u32[]{:S(2)}, u32[]{:S(2)}) collective-permute-start(f32[6,32,128]{2,1,0:T(8,128)S(1)} %get-tuple-element.67), channel_id=1, source_target_pairs={{4,8},{12,16},{20,24},{8,4},{16,12},{24,20},{5,9},{13,17},{21,25},... | collective-permute-start | bytes 294920 | tf_op jit(solution)/shard_map/ppermute | solution.py:425
  4.7 9.4 %collective-permute-start.4 = (f32[8,32,128]{2,1,0:T(8,128)S(1)}, f32[8,32,128]{2,1,0:T(8,128)S(1)}, u32[]{:S(2)}, u32[]{:S(2)}) collective-permute-start(f32[8,32,128]{2,1,0:T(8,128)S(1)} %get-tuple-element.75.refs_7_), channel_id=1, source_target_pairs={{0,2},{1,3},{2,0},{3,1},{4,6},{5,7},{6,4},{7,5},{8,10},{9,11},{10,... | collective-permute-start | bytes 393224 | tf_op jit(solution)/shard_map/ppermute | solution.py:381
  7.1 7.1 %collective-permute-start.3 = (f32[8,32,128]{2,1,0:T(8,128)S(1)}, f32[8,32,128]{2,1,0:T(8,128)S(1)}, u32[]{:S(2)}, u32[]{:S(2)}) collective-permute-start(f32[8,32,128]{2,1,0:T(8,128)S(1)} %get-tuple-element.75.refs_7_), channel_id=1, source_target_pairs={{0,1},{1,0},{2,3},{3,2},{4,5},{5,4},{6,7},{7,6},{8,9},{9,8},{10,11... | collective-permute-start | bytes 393224 | tf_op jit(solution)/shard_map/ppermute | solution.py:380
  9.3 5.5 %copy-start = (f32[1,9,4,128,128]{4,3,2,1,0:T(8,128)S(1)}, f32[1,9,4,128,128]{4,3,2,1,0:T(8,128)}, u32[]{:S(2)}) copy-start(f32[1,9,4,128,128]{4,3,2,1,0:T(8,128)} %refs_0_.5) | copy-start | bytes 7077892
  10.7 11.6 %collective-permute-start.1 = (f32[5,128,128]{2,1,0:T(8,128)S(1)}, f32[5,128,128]{2,1,0:T(8,128)S(1)}, u32[]{:S(2)}, u32[]{:S(2)}) collective-permute-start(f32[5,128,128]{2,1,0:T(8,128)S(1)} %get-tuple-element.68), channel_id=1, source_target_pairs={{4,8},{12,16},{20,24},{8,4},{16,12},{24,20},{5,9},{13,17},{21,25},... | collective-permute-start | bytes 983048 | tf_op jit(solution)/shard_map/ppermute | solution.py:417
  14.1 8.3 %collective-permute-start.2 = (f32[5,128,128]{2,1,0:T(8,128)S(1)}, f32[5,128,128]{2,1,0:T(8,128)S(1)}, u32[]{:S(2)}, u32[]{:S(2)}) collective-permute-start(f32[5,128,128]{2,1,0:T(8,128)S(1)} %get-tuple-element.69), channel_id=1, source_target_pairs={{0,4},{8,12},{16,20},{24,28},{4,0},{12,8},{20,16},{28,24},{1,5},{9... | collective-permute-start | bytes 983048 | tf_op jit(solution)/shard_map/ppermute | solution.py:417
  14.2 4.9 %collective-permute-start.5 = (f32[8,32,128]{2,1,0:T(8,128)S(1)}, f32[8,32,128]{2,1,0:T(8,128)S(1)}, u32[]{:S(2)}, u32[]{:S(2)}) collective-permute-start(f32[8,32,128]{2,1,0:T(8,128)S(1)} %shard_map.67), channel_id=1, source_target_pairs={{0,1},{1,0},{2,3},{3,2},{4,5},{5,4},{6,7},{7,6},{8,9},{9,8},{10,11... | collective-permute-start | bytes 393224 | tf_op jit(solution)/shard_map/ppermute | solution.py:384
  16.9 12.9 %collective-permute-start.9 = (f32[14,32,128]{2,1,0:T(8,128)S(1)}, f32[14,32,128]{2,1,0:T(8,128)S(1)}, u32[]{:S(2)}, u32[]{:S(2)}) collective-permute-start(f32[14,32,128]{2,1,0:T(8,128)S(1)} %shard_map.71.refs_1_), channel_id=1, source_target_pairs={{0,2},{1,3},{2,0},{3,1},{4,6},{5,7},{6,4},{7,5},{8,10},{9,11},{10,... | collective-permute-start | bytes 688136 | tf_op jit(solution)/shard_map/ppermute | solution.py:381
  19.1 10.8 %collective-permute-start.8 = (f32[14,32,128]{2,1,0:T(8,128)S(1)}, f32[14,32,128]{2,1,0:T(8,128)S(1)}, u32[]{:S(2)}, u32[]{:S(2)}) collective-permute-start(f32[14,32,128]{2,1,0:T(8,128)S(1)} %shard_map.71.refs_1_), channel_id=1, source_target_pairs={{0,1},{1,0},{2,3},{3,2},{4,5},{5,4},{6,7},{7,6},{8,9},{9,8},{10,11... | collective-permute-start | bytes 688136 | tf_op jit(solution)/shard_map/ppermute | solution.py:380
  22.7 15.4 %collective-permute-start.6 = (f32[9,72,128]{2,1,0:T(8,128)S(1)}, f32[9,72,128]{2,1,0:T(8,128)S(1)}, u32[]{:S(2)}, u32[]{:S(2)}) collective-permute-start(f32[9,72,128]{2,1,0:T(8,128)S(1)} %get-tuple-element.81), channel_id=1, source_target_pairs={{4,8},{12,16},{20,24},{8,4},{16,12},{24,20},{5,9},{13,17},{21,25},... | collective-permute-start | bytes 995336 | tf_op jit(solution)/shard_map/ppermute | solution.py:417
  26.6 11.5 %collective-permute-start.7 = (f32[9,72,128]{2,1,0:T(8,128)S(1)}, f32[9,72,128]{2,1,0:T(8,128)S(1)}, u32[]{:S(2)}, u32[]{:S(2)}) collective-permute-start(f32[9,72,128]{2,1,0:T(8,128)S(1)} %get-tuple-element.82), channel_id=1, source_target_pairs={{0,4},{8,12},{16,20},{24,28},{4,0},{12,8},{20,16},{28,24},{1,5},{9... | collective-permute-start | bytes 995336 | tf_op jit(solution)/shard_map/ppermute | solution.py:417
  26.9 9.2 %collective-permute-start.11 = (f32[9,56,128]{2,1,0:T(8,128)S(1)}, f32[9,56,128]{2,1,0:T(8,128)S(1)}, u32[]{:S(2)}, u32[]{:S(2)}) collective-permute-start(f32[9,56,128]{2,1,0:T(8,128)S(1)} %get-tuple-element.84), channel_id=1, source_target_pairs={{0,4},{8,12},{16,20},{24,28},{4,0},{12,8},{20,16},{28,24},{1,5},{9... | collective-permute-start | bytes 774152 | tf_op jit(solution)/shard_map/ppermute | solution.py:417
  29.9 6.2 %collective-permute-start.10 = (f32[14,32,128]{2,1,0:T(8,128)S(1)}, f32[14,32,128]{2,1,0:T(8,128)S(1)}, u32[]{:S(2)}, u32[]{:S(2)}) collective-permute-start(f32[14,32,128]{2,1,0:T(8,128)S(1)} %shard_map.72), channel_id=1, source_target_pairs={{0,1},{1,0},{2,3},{3,2},{4,5},{5,4},{6,7},{7,6},{8,9},{9,8},{10,11... | collective-permute-start | bytes 688136 | tf_op jit(solution)/shard_map/ppermute | solution.py:384
  30.6 13.9 %collective-permute-start.13 = (f32[9,56,128]{2,1,0:T(8,128)S(1)}, f32[9,56,128]{2,1,0:T(8,128)S(1)}, u32[]{:S(2)}, u32[]{:S(2)}) collective-permute-start(f32[9,56,128]{2,1,0:T(8,128)S(1)} %get-tuple-element.90), channel_id=1, source_target_pairs={{4,8},{12,16},{20,24},{8,4},{16,12},{24,20},{5,9},{13,17},{21,25},... | collective-permute-start | bytes 774152 | tf_op jit(solution)/shard_map/ppermute | solution.py:417
  36.2 3.3 %collective-permute-start.12 = (f32[6,128,128]{2,1,0:T(8,128)S(1)}, f32[6,128,128]{2,1,0:T(8,128)S(1)}, u32[]{:S(2)}, u32[]{:S(2)}) collective-permute-start(f32[6,128,128]{2,1,0:T(8,128)S(1)} %get-tuple-element.88), channel_id=1, source_target_pairs={{0,4},{8,12},{16,20},{24,28},{4,0},{12,8},{20,16},{28,24},{1,5},{9... | collective-permute-start | bytes 1179656 | tf_op jit(solution)/shard_map/ppermute | solution.py:519
  40.6 12.1 %collective-permute-start.14 = (f32[9,64,128]{2,1,0:T(8,128)S(1)}, f32[9,64,128]{2,1,0:T(8,128)S(1)}, u32[]{:S(2)}, u32[]{:S(2)}) collective-permute-start(f32[9,64,128]{2,1,0:T(8,128)S(1)} %get-tuple-element.100), channel_id=1, source_target_pairs={{4,8},{12,16},{20,24},{8,4},{16,12},{24,20},{5,9},{13,17},{21,25},... | collective-permute-start | bytes 884744 | tf_op jit(solution)/shard_map/ppermute | solution.py:417
  44.4 8.3 %collective-permute-start.15 = (f32[9,64,128]{2,1,0:T(8,128)S(1)}, f32[9,64,128]{2,1,0:T(8,128)S(1)}, u32[]{:S(2)}, u32[]{:S(2)}) collective-permute-start(f32[9,64,128]{2,1,0:T(8,128)S(1)} %get-tuple-element.101), channel_id=1, source_target_pairs={{0,4},{8,12},{16,20},{24,28},{4,0},{12,8},{20,16},{28,24},{1,5},{9... | collective-permute-start | bytes 884744 | tf_op jit(solution)/shard_map/ppermute | solution.py:417
  45.7 13.3 %collective-permute-start.16 = (f32[9,64,128]{2,1,0:T(8,128)S(1)}, f32[9,64,128]{2,1,0:T(8,128)S(1)}, u32[]{:S(2)}, u32[]{:S(2)}) collective-permute-start(f32[9,64,128]{2,1,0:T(8,128)S(1)} %get-tuple-element.103), channel_id=1, source_target_pairs={{4,8},{12,16},{20,24},{8,4},{16,12},{24,20},{5,9},{13,17},{21,25},... | collective-permute-start | bytes 884744 | tf_op jit(solution)/shard_map/ppermute | solution.py:417
  48.3 10.7 %collective-permute-start.17 = (f32[9,64,128]{2,1,0:T(8,128)S(1)}, f32[9,64,128]{2,1,0:T(8,128)S(1)}, u32[]{:S(2)}, u32[]{:S(2)}) collective-permute-start(f32[9,64,128]{2,1,0:T(8,128)S(1)} %get-tuple-element.104), channel_id=1, source_target_pairs={{0,4},{8,12},{16,20},{24,28},{4,0},{12,8},{20,16},{28,24},{1,5},{9... | collective-permute-start | bytes 884744 | tf_op jit(solution)/shard_map/ppermute | solution.py:417
  53.9 9.9 %collective-permute-start.18 = (f32[9,56,128]{2,1,0:T(8,128)S(1)}, f32[9,56,128]{2,1,0:T(8,128)S(1)}, u32[]{:S(2)}, u32[]{:S(2)}) collective-permute-start(f32[9,56,128]{2,1,0:T(8,128)S(1)} %get-tuple-element.111), channel_id=1, source_target_pairs={{4,8},{12,16},{20,24},{8,4},{16,12},{24,20},{5,9},{13,17},{21,25},... | collective-permute-start | bytes 774152 | tf_op jit(solution)/shard_map/ppermute | solution.py:417
  57.2 6.6 %collective-permute-start.19 = (f32[9,56,128]{2,1,0:T(8,128)S(1)}, f32[9,56,128]{2,1,0:T(8,128)S(1)}, u32[]{:S(2)}, u32[]{:S(2)}) collective-permute-start(f32[9,56,128]{2,1,0:T(8,128)S(1)} %get-tuple-element.112), channel_id=1, source_target_pairs={{0,4},{8,12},{16,20},{24,28},{4,0},{12,8},{20,16},{28,24},{1,5},{9... | collective-permute-start | bytes 774152 | tf_op jit(solution)/shard_map/ppermute | solution.py:417
  60.3 11.4 %collective-permute-start.20 = (f32[9,72,128]{2,1,0:T(8,128)S(1)}, f32[9,72,128]{2,1,0:T(8,128)S(1)}, u32[]{:S(2)}, u32[]{:S(2)}) collective-permute-start(f32[9,72,128]{2,1,0:T(8,128)S(1)} %get-tuple-element.114), channel_id=1, source_target_pairs={{4,8},{12,16},{20,24},{8,4},{16,12},{24,20},{5,9},{13,17},{21,25},... | collective-permute-start | bytes 995336 | tf_op jit(solution)/shard_map/ppermute | solution.py:417
  63.7 8.0 %collective-permute-start.21 = (f32[9,72,128]{2,1,0:T(8,128)S(1)}, f32[9,72,128]{2,1,0:T(8,128)S(1)}, u32[]{:S(2)}, u32[]{:S(2)}) collective-permute-start(f32[9,72,128]{2,1,0:T(8,128)S(1)} %get-tuple-element.115), channel_id=1, source_target_pairs={{0,4},{8,12},{16,20},{24,28},{4,0},{12,8},{20,16},{28,24},{1,5},{9... | collective-permute-start | bytes 995336 | tf_op jit(solution)/shard_map/ppermute | solution.py:417
  64.8 11.6 %collective-permute-start.22 = (f32[5,48,128]{2,1,0:T(8,128)S(1)}, f32[5,48,128]{2,1,0:T(8,128)S(1)}, u32[]{:S(2)}, u32[]{:S(2)}) collective-permute-start(f32[5,48,128]{2,1,0:T(8,128)S(1)} %get-tuple-element.122), channel_id=1, source_target_pairs={{4,8},{12,16},{20,24},{8,4},{16,12},{24,20},{5,9},{13,17},{21,25},... | collective-permute-start | bytes 368648 | tf_op jit(solution)/shard_map/ppermute | solution.py:417
  68.0 8.5 %collective-permute-start.23 = (f32[5,48,128]{2,1,0:T(8,128)S(1)}, f32[5,48,128]{2,1,0:T(8,128)S(1)}, u32[]{:S(2)}, u32[]{:S(2)}) collective-permute-start(f32[5,48,128]{2,1,0:T(8,128)S(1)} %get-tuple-element.123), channel_id=1, source_target_pairs={{0,4},{8,12},{16,20},{24,28},{4,0},{12,8},{20,16},{28,24},{1,5},{9... | collective-permute-start | bytes 368648 | tf_op jit(solution)/shard_map/ppermute | solution.py:417
  73.1 8.0 %collective-permute-start.24 = (f32[5,80,128]{2,1,0:T(8,128)S(1)}, f32[5,80,128]{2,1,0:T(8,128)S(1)}, u32[]{:S(2)}, u32[]{:S(2)}) collective-permute-start(f32[5,80,128]{2,1,0:T(8,128)S(1)} %get-tuple-element.125), channel_id=1, source_target_pairs={{4,8},{12,16},{20,24},{8,4},{16,12},{24,20},{5,9},{13,17},{21,25},... | collective-permute-start | bytes 614408 | tf_op jit(solution)/shard_map/ppermute | solution.py:417
  76.4 4.8 %collective-permute-start.25 = (f32[5,80,128]{2,1,0:T(8,128)S(1)}, f32[5,80,128]{2,1,0:T(8,128)S(1)}, u32[]{:S(2)}, u32[]{:S(2)}) collective-permute-start(f32[5,80,128]{2,1,0:T(8,128)S(1)} %get-tuple-element.126), channel_id=1, source_target_pairs={{0,4},{8,12},{16,20},{24,28},{4,0},{12,8},{20,16},{28,24},{1,5},{9... | collective-permute-start | bytes 614408 | tf_op jit(solution)/shard_map/ppermute | solution.py:417

commit v5 on v4

--- a/solution.py
+++ b/solution.py
@@ -286,10 +286,9 @@
             copy.start()
             copies.append(copy)
 
-        for f in range(3):
-            span = (last - first) * ROWS
-            move(refs["vel"].at[f, pl.ds(REACH, self.cx), pl.ds(PAD + first * ROWS, span)],
-                 refs["out"].at[0, f, :, pl.ds(first * ROWS, span)])
+        if which == 0:
+            for f in range(3):
+                move(refs["vel"].at[f, pl.ds(REACH, self.cx), pl.ds(PAD, self.rows)], refs["out"].at[0, f])
         for a, b in self.parts(first, last):
             self.stress(refs, moment, which, True, (a, b))
             span = (b - a) * ROWS
@@ -301,8 +300,8 @@
 
     @staticmethod
     def parts(first, last):
-        middle = (first + last + 1) // 2
-        return [(a, b) for a, b in ((first, middle), (middle, last)) if b > a]
+        marks = [first, (first + last) // 2, last - (last - first) // 5, last]
+        return [(a, b) for a, b in zip(marks, marks[1:]) if b > a]
 
 
 STRESS_SLOTS = 5
@@ -381,14 +380,15 @@
         across = lax.ppermute(mine, "shot", pairs(2))
 
         def finish(*others):
-            handed = lax.ppermute(hold(across, beside, *others), "shot", pairs(1))
-            return {0: mine, 1: beside, 2: across, 3: handed}
+            held = hold(across, beside, *others)
+            handed = lax.ppermute(held, "shot", pairs(1))
+            return {0: mine, 1: beside, 2: across, 3: handed}, held
 
         return (beside, across), finish
     turn = lambda k: [(i, (i + k) % shots) for i in range(shots)]
     swap = shots & (shots - 1) == 0
     got = {k: lax.ppermute(mine, "shot", pairs(k) if swap else turn(k)) for k in range(1, shots)}
-    return tuple(got.values()), lambda *others: {0: mine, **got}
+    return tuple(got.values()), lambda *others: ({0: mine, **got}, mine)
 
 
 def origin_of(index, k, shots):
@@ -436,14 +436,19 @@
 
     first_stage, finish = spread(sent["first"], shots)
     mask = state["mask"]
-    firsts = finish(edge)
+    firsts, held = finish(edge)
+
+    def mark(refs):
+        refs["tick"][...] = jnp.zeros(refs["tick"].shape, F32)
+
+    tick = call(mark, {}, dict(tick=(ROWS, lanes)), waits=(held,))["tick"]
 
     def join(refs):
         refs["all"][:2 * cx] = refs["second"][...]
         refs["all"][2 * cx:] = refs["edge"][...]
 
     second = call(join, dict(second=sent["second"], edge=edge),
-                  dict(all=(2 * cx + MODEL_SLOTS,) + panel), us=0.02, waits=first_stage + (mask,))["all"]
+                  dict(all=(2 * cx + MODEL_SLOTS,) + panel), us=0.02, waits=first_stage + (tick,))["all"]
     _, finish_second = spread(second, shots)
 
     def sends(step, which):
@@ -490,7 +495,7 @@
     vel = got["vel_next"]
     arrived.append(exchange(got["send_far"], got["send_near"]))
 
-    seconds = finish_second()
+    seconds, _ = finish_second()
 
     def put_edge(refs, from_above, place, part):
         for j in range(2):
@@ -558,7 +563,7 @@
             if final:
                 first, last = plan.stress_tiles(step, which)
                 scratch = [pltpu.VMEM((6, cx, (last - first) * ROWS, lanes), F32),
-                           pltpu.SemaphoreType.DMA((3 + 6 * len(plan.parts(first, last)),))]
+                           pltpu.SemaphoreType.DMA((3 * (1 - which) + 6 * len(plan.parts(first, last)),))]
             else:
                 outs.update(sends(step + 1, which))
             got = call(functools.partial(advance, which=which), ins, outs, alias=("vel",) + tuple(carried) + (tuple(edges) if step + which == 0 else ()),
@@ -575,7 +580,7 @@
 
 
 def cuts_of(steps, tiles):
-    middle = tiles // 2 + 1
+    middle = tiles // 2 + 2
     return [max(1, middle - step) for step in range(steps)]
 
 

time: 83.3 us -> 82 us (0.984)
  waiting for transfers between devices: 20.1 us -> 19.2 us
    ppermute x9, starting transfers between devices: 32.3 us -> 30.2 us  [exchange(): lax.ppermute(to_far, 'aper', far)]
    ppermute x2, waiting for transfers between devices: 2.4 us -> 0.99 us  [spread(): across = lax.ppermute(mine, 'shot', pairs(2))]
    ppermute x2, starting transfers between devices: 1.36 us -> 2.76 us  [finish(): handed = lax.ppermute(held, 'shot', pairs(1))]
    ppermute x2, waiting for transfers between devices: 0.01 us -> 0.91 us  [finish(): handed = lax.ppermute(held, 'shot', pairs(1))]
    pallas_call x18 -> x19, Pallas kernels: 15.1 us -> 15 us  [call(): pl.pallas_call(kernel, out_shape=[pltpu.HBM(shape, F32) if name in anywhe...]
  transfers between devices with their start and end apart: 26 -> 26, of which waited for: 7 -> 8; matrix products, arithmetic and copies ran while one was open for 1% -> 1% of each run, Pallas kernels for 15% -> 15%
where the time goes in v5:
time: 82 us; the launch traced here: 81.5 us
  starting transfers between devices  46 us (56%)
  waiting for transfers between devices  19.2 us (23%)
  Pallas kernels  15 us (18%)
  local copies, waits for them, and re-layouts  0.96 us (1%)
    ppermute x9, starting transfers between devices, exchange(): lax.ppermute(to_far, 'aper', far)  30.2 us
    ppermute x9, waiting for transfers between devices, exchange(): lax.ppermute(to_far, 'aper', far)  16 us
    pallas_call x19, Pallas kernels, call(): pl.pallas_call(kernel, out_shape=[pltpu.HBM(shape, F32) if name in anywhe...  15 us
    ppermute x2, starting transfers between devices, spread(): across = lax.ppermute(mine, 'shot', pairs(2))  4.53 us
    ppermute x1, starting transfers between devices, per_device(): edge = lax.ppermute(sent['edge'], 'aper', far)  3.68 us
    ppermute x2, starting transfers between devices, finish(): handed = lax.ppermute(held, 'shot', pairs(1))  2.76 us
    ppermute x9, starting transfers between devices, exchange(): lax.ppermute(to_near, 'aper', near)  1.88 us
  transfers between devices with their start and end apart: 26, of which 8 were waited for; matrix products, arithmetic and copies ran while one was open for 1% of the time, Pallas kernels for 15%

profile of v5, /device:TPU:3, one launch (start us, length us, event | category | flops | bytes accessed | tf_op | source)
XLA Modules:
  0.0 81.5 jit_solution(2531798938779180379)
XLA Ops:
  1.1 3.7 %collective-permute-start = (f32[6,32,128]{2,1,0:T(8,128)S(1)}, f32[6,32,128]{2,1,0:T(8,128)S(1)}, u32[]{:S(2)}, u32[]{:S(2)}) collective-permute-start(f32[6,32,128]{2,1,0:T(8,128)S(1)} %get-tuple-element.67), channel_id=1, source_target_pairs={{4,8},{12,16},{20,24},{8,4},{16,12},{24,20},{5,9},{13,17},{21,25},... | collective-permute-start | bytes 294920 | tf_op jit(solution)/shard_map/ppermute | solution.py:425
  4.7 2.4 %collective-permute-start.4 = (f32[8,32,128]{2,1,0:T(8,128)S(1)}, f32[8,32,128]{2,1,0:T(8,128)S(1)}, u32[]{:S(2)}, u32[]{:S(2)}) collective-permute-start(f32[8,32,128]{2,1,0:T(8,128)S(1)} %get-tuple-element.75.refs_7_), channel_id=1, source_target_pairs={{0,2},{1,3},{2,0},{3,1},{4,6},{5,7},{6,4},{7,5},{8,10},{9,11},{10,... | collective-permute-start | bytes 393224 | tf_op jit(solution)/shard_map/ppermute | solution.py:380
  7.1 1.3 %collective-permute-start.3 = (f32[8,32,128]{2,1,0:T(8,128)S(1)}, f32[8,32,128]{2,1,0:T(8,128)S(1)}, u32[]{:S(2)}, u32[]{:S(2)}) collective-permute-start(f32[8,32,128]{2,1,0:T(8,128)S(1)} %get-tuple-element.75.refs_7_), channel_id=1, source_target_pairs={{0,1},{1,0},{2,3},{3,2},{4,5},{5,4},{6,7},{7,6},{8,9},{9,8},{10,11... | collective-permute-start | bytes 393224 | tf_op jit(solution)/shard_map/ppermute | solution.py:379
  9.3 1.2 %shard_map.65 = (f32[5,128,128]{2,1,0:T(8,128)S(1)}, f32[5,128,128]{2,1,0:T(8,128)S(1)}) custom-call(f32[1,9,4,128,128]{4,3,2,1,0:T(8,128)} %refs_0_.5, f32[6,32,128]{2,1,0:T(8,128)S(1)} %collective-permute-done.refs_1_.refs_2_), custom_call_target="tpu_custom_call" | custom-call | flops 5000000000 | bytes 18000000 | tf_op jit(solution)/shard_map/pallas_call | solution.py:38
  10.6 3.3 %collective-permute-start.1 = (f32[5,128,128]{2,1,0:T(8,128)S(1)}, f32[5,128,128]{2,1,0:T(8,128)S(1)}, u32[]{:S(2)}, u32[]{:S(2)}) collective-permute-start(f32[5,128,128]{2,1,0:T(8,128)S(1)} %get-tuple-element.68), channel_id=1, source_target_pairs={{4,8},{12,16},{20,24},{8,4},{16,12},{24,20},{5,9},{13,17},{21,25},... | collective-permute-start | bytes 983048 | tf_op jit(solution)/shard_map/ppermute | solution.py:417
  14.9 2.2 %collective-permute-start.9 = (f32[14,32,128]{2,1,0:T(8,128)S(1)}, f32[14,32,128]{2,1,0:T(8,128)S(1)}, u32[]{:S(2)}, u32[]{:S(2)}) collective-permute-start(f32[14,32,128]{2,1,0:T(8,128)S(1)} %shard_map.72.refs_1_), channel_id=1, source_target_pairs={{0,2},{1,3},{2,0},{3,1},{4,6},{5,7},{6,4},{7,5},{8,10},{9,11},{10,... | collective-permute-start | bytes 688136 | tf_op jit(solution)/shard_map/ppermute | solution.py:380
  17.1 2.1 %shard_map.66 = (f32[3,7,144,128]{3,2,1,0:T(8,128)S(1)}, f32[3,4,144,128]{3,2,1,0:T(8,128)S(1)}, f32[3,4,128,128]{3,2,1,0:T(8,128)S(1)}, f32[3,4,128,128]{3,2,1,0:T(8,128)S(1)}, f32[128,128]{1,0:T(8,128)S(1)}) custom-call(f32[1,9,4,128,128]{4,3,2,1,0:T(8,128)S(1)} %copy-done, s32[128,4]{1,0:T(8,128)S(1)} %bitcast.1), custom_call_target="tpu_custom_call" | custom-call | flops 5000000000 | bytes 18000000 | tf_op jit(solution)/shard_map/pallas_call | solution.py:38
  20.0 2.5 %collective-permute-done.1.refs_0_ = f32[5,128,128]{2,1,0:T(8,128)S(1)} collective-permute-done((f32[5,128,128]{2,1,0:T(8,128)S(1)}, f32[5,128,128]{2,1,0:T(8,128)S(1)}, u32[]{:S(2)}, u32[]{:S(2)}) %collective-permute-start.1) | collective-permute-done | bytes 327712 | tf_op jit(solution)/shard_map/ppermute | solution.py:417
  22.9 3.8 %collective-permute-start.6 = (f32[9,80,128]{2,1,0:T(8,128)S(1)}, f32[9,80,128]{2,1,0:T(8,128)S(1)}, u32[]{:S(2)}, u32[]{:S(2)}) collective-permute-start(f32[9,80,128]{2,1,0:T(8,128)S(1)} %get-tuple-element.81), channel_id=1, source_target_pairs={{4,8},{12,16},{20,24},{8,4},{16,12},{24,20},{5,9},{13,17},{21,25},... | collective-permute-start | bytes 1105928 | tf_op jit(solution)/shard_map/ppermute | solution.py:417
  27.7 1.9 %collective-permute-start.10 = (f32[14,32,128]{2,1,0:T(8,128)S(1)}, f32[14,32,128]{2,1,0:T(8,128)S(1)}, u32[]{:S(2)}, u32[]{:S(2)}) collective-permute-start(f32[14,32,128]{2,1,0:T(8,128)S(1)} %shard_map.73), channel_id=1, source_target_pairs={{0,1},{1,0},{2,3},{3,2},{4,5},{5,4},{6,7},{7,6},{8,9},{9,8},{10,11... | collective-permute-start | bytes 688136 | tf_op jit(solution)/shard_map/ppermute | solution.py:384
  29.9 1.3 %collective-permute-start.11 = (f32[9,48,128]{2,1,0:T(8,128)S(1)}, f32[9,48,128]{2,1,0:T(8,128)S(1)}, u32[]{:S(2)}, u32[]{:S(2)}) collective-permute-start(f32[9,48,128]{2,1,0:T(8,128)S(1)} %get-tuple-element.84), channel_id=1, source_target_pairs={{0,4},{8,12},{16,20},{24,28},{4,0},{12,8},{20,16},{28,24},{1,5},{9... | collective-permute-start | bytes 663560 | tf_op jit(solution)/shard_map/ppermute | solution.py:417
  31.2 3.5 %collective-permute-start.13 = (f32[9,48,128]{2,1,0:T(8,128)S(1)}, f32[9,48,128]{2,1,0:T(8,128)S(1)}, u32[]{:S(2)}, u32[]{:S(2)}) collective-permute-start(f32[9,48,128]{2,1,0:T(8,128)S(1)} %get-tuple-element.90), channel_id=1, source_target_pairs={{4,8},{12,16},{20,24},{8,4},{16,12},{24,20},{5,9},{13,17},{21,25},... | collective-permute-start | bytes 663560 | tf_op jit(solution)/shard_map/ppermute | solution.py:417
  34.8 1.6 %collective-permute-start.12 = (f32[6,128,128]{2,1,0:T(8,128)S(1)}, f32[6,128,128]{2,1,0:T(8,128)S(1)}, u32[]{:S(2)}, u32[]{:S(2)}) collective-permute-start(f32[6,128,128]{2,1,0:T(8,128)S(1)} %get-tuple-element.88), channel_id=1, source_target_pairs={{0,4},{8,12},{16,20},{24,28},{4,0},{12,8},{20,16},{28,24},{1,5},{9... | collective-permute-start | bytes 1179656 | tf_op jit(solution)/shard_map/ppermute | solution.py:524
  36.5 1.3 %collective-permute-done.12.refs_11_ = f32[6,128,128]{2,1,0:T(8,128)S(1)} collective-permute-done((f32[6,128,128]{2,1,0:T(8,128)S(1)}, f32[6,128,128]{2,1,0:T(8,128)S(1)}, u32[]{:S(2)}, u32[]{:S(2)}) %collective-permute-start.12) | collective-permute-done | bytes 393248 | tf_op jit(solution)/shard_map/ppermute | solution.py:524
  37.8 1.2 %shard_map.75 = (f32[3,10,144,128]{3,2,1,0:T(8,128)S(1)}, f32[3,7,144,128]{3,2,1,0:T(8,128)S(1)}, f32[3,4,144,128]{3,2,1,0:T(8,128)S(1)}, f32[3,10,144,128]{3,2,...) custom-call(f32[3,10,144,128]{3,2,1,0:T(8,128)S(1)} %shard_map.70.re, ...), custom_call_target="tpu_custom_call", output_to_operand_aliasing={{0}: (0, {}), {4}: (8, {}), {5}: (9, {}), {6}: (10, {})} | custom-call | flops 5000000000 | bytes 18000000 | tf_op jit(solution)/shard_map/pallas_call | solution.py:38
  39.0 4.2 %collective-permute-start.14 = (f32[9,72,128]{2,1,0:T(8,128)S(1)}, f32[9,72,128]{2,1,0:T(8,128)S(1)}, u32[]{:S(2)}, u32[]{:S(2)}) collective-permute-start(f32[9,72,128]{2,1,0:T(8,128)S(1)} %get-tuple-element.100), channel_id=1, source_target_pairs={{4,8},{12,16},{20,24},{8,4},{16,12},{24,20},{5,9},{13,17},{21,25},... | collective-permute-start | bytes 995336 | tf_op jit(solution)/shard_map/ppermute | solution.py:417
  43.2 1.0 %shard_map.76 = (f32[3,10,144,128]{3,2,1,0:T(8,128)S(1)}, f32[3,7,144,128]{3,2,1,0:T(8,128)S(1)}, f32[3,4,144,128]{3,2,1,0:T(8,128)S(1)}, f32[3,10,144,128]{3,2,...) custom-call(f32[3,10,144,128]{3,2,1,0:T(8,128)S(1)} %get-tuple-eleme, ...), custom_call_target="tpu_custom_call", output_to_operand_aliasing={{0}: (0, {}), {1}: (11, {}), {2}: (12, {}), {3}: (13, {})} | custom-call | flops 5000000000 | bytes 18000000 | tf_op jit(solution)/shard_map/pallas_call | solution.py:38
  44.3 2.7 %collective-permute-start.16 = (f32[9,56,128]{2,1,0:T(8,128)S(1)}, f32[9,56,128]{2,1,0:T(8,128)S(1)}, u32[]{:S(2)}, u32[]{:S(2)}) collective-permute-start(f32[9,56,128]{2,1,0:T(8,128)S(1)} %get-tuple-element.103), channel_id=1, source_target_pairs={{4,8},{12,16},{20,24},{8,4},{16,12},{24,20},{5,9},{13,17},{21,25},... | collective-permute-start | bytes 774152 | tf_op jit(solution)/shard_map/ppermute | solution.py:417
  47.1 4.8 %collective-permute-done.14.refs_3_ = f32[9,72,128]{2,1,0:T(8,128)S(1)} collective-permute-done((f32[9,72,128]{2,1,0:T(8,128)S(1)}, f32[9,72,128]{2,1,0:T(8,128)S(1)}, u32[]{:S(2)}, u32[]{:S(2)}) %collective-permute-start.14) | collective-permute-done | bytes 331808 | tf_op jit(solution)/shard_map/ppermute | solution.py:417
  51.9 1.3 %shard_map.77 = (f32[3,10,144,128]{3,2,1,0:T(8,128)S(1)}, f32[3,7,144,128]{3,2,1,0:T(8,128)S(1)}, f32[3,4,144,128]{3,2,1,0:T(8,128)S(1)}, f32[3,10,144,128]{3,2,...) custom-call(f32[3,10,144,128]{3,2,1,0:T(8,128)S(1)} %get-tuple-element.97., ...), custom_call_target="tpu_custom_call", output_to_operand_aliasing={{0}: (0, {})} | custom-call | flops 5000000000 | bytes 18000000 | tf_op jit(solution)/shard_map/pallas_call | solution.py:38
  53.2 4.0 %collective-permute-start.18 = (f32[9,64,128]{2,1,0:T(8,128)S(1)}, f32[9,64,128]{2,1,0:T(8,128)S(1)}, u32[]{:S(2)}, u32[]{:S(2)}) collective-permute-start(f32[9,64,128]{2,1,0:T(8,128)S(1)} %get-tuple-element.111), channel_id=1, source_target_pairs={{4,8},{12,16},{20,24},{8,4},{16,12},{24,20},{5,9},{13,17},{21,25},... | collective-permute-start | bytes 884744 | tf_op jit(solution)/shard_map/ppermute | solution.py:417
  57.3 1.2 %shard_map.78 = (f32[3,10,144,128]{3,2,1,0:T(8,128)S(1)}, f32[3,7,144,128]{3,2,1,0:T(8,128)S(1)}, f32[3,4,144,128]{3,2,1,0:T(8,128)S(1)}, f32[3,10,144,128]{3,2,...) custom-call(f32[3,10,144,128]{3,2,1,0:T(8,128)S(1)} %get-tuple-eleme, ...), custom_call_target="tpu_custom_call", output_to_operand_aliasing={{0}: (0, {}), {1}: (11, {}), {2}: (12, {}), {3}: (13, {})} | custom-call | flops 5000000000 | bytes 18000000 | tf_op jit(solution)/shard_map/pallas_call | solution.py:38
  58.5 3.6 %collective-permute-start.20 = (f32[9,64,128]{2,1,0:T(8,128)S(1)}, f32[9,64,128]{2,1,0:T(8,128)S(1)}, u32[]{:S(2)}, u32[]{:S(2)}) collective-permute-start(f32[9,64,128]{2,1,0:T(8,128)S(1)} %get-tuple-element.114), channel_id=1, source_target_pairs={{4,8},{12,16},{20,24},{8,4},{16,12},{24,20},{5,9},{13,17},{21,25},... | collective-permute-start | bytes 884744 | tf_op jit(solution)/shard_map/ppermute | solution.py:417
  62.2 2.5 %collective-permute-done.18.refs_3_ = f32[9,64,128]{2,1,0:T(8,128)S(1)} collective-permute-done((f32[9,64,128]{2,1,0:T(8,128)S(1)}, f32[9,64,128]{2,1,0:T(8,128)S(1)}, u32[]{:S(2)}, u32[]{:S(2)}) %collective-permute-start.18) | collective-permute-done | bytes 294944 | tf_op jit(solution)/shard_map/ppermute | solution.py:417
  64.7 1.1 %shard_map.79 = (f32[3,10,144,128]{3,2,1,0:T(8,128)S(1)}, f32[3,7,144,128]{3,2,1,0:T(8,128)S(1)}, f32[3,4,144,128]{3,2,1,0:T(8,128)S(1)}, f32[3,10,144,128]{3,2,...) custom-call(f32[3,10,144,128]{3,2,1,0:T(8,128)S(1)} %get-tuple-element.108, ...), custom_call_target="tpu_custom_call", output_to_operand_aliasing={{0}: (0, {})} | custom-call | flops 5000000000 | bytes 18000000 | tf_op jit(solution)/shard_map/pallas_call | solution.py:38
  65.8 1.9 %collective-permute-start.22 = (f32[5,56,128]{2,1,0:T(8,128)S(1)}, f32[5,56,128]{2,1,0:T(8,128)S(1)}, u32[]{:S(2)}, u32[]{:S(2)}) collective-permute-start(f32[5,56,128]{2,1,0:T(8,128)S(1)} %get-tuple-element.122), channel_id=1, source_target_pairs={{4,8},{12,16},{20,24},{8,4},{16,12},{24,20},{5,9},{13,17},{21,25},... | collective-permute-start | bytes 430088 | tf_op jit(solution)/shard_map/ppermute | solution.py:417
  67.8 3.2 %collective-permute-done.20.refs_3_ = f32[9,64,128]{2,1,0:T(8,128)S(1)} collective-permute-done((f32[9,64,128]{2,1,0:T(8,128)S(1)}, f32[9,64,128]{2,1,0:T(8,128)S(1)}, u32[]{:S(2)}, u32[]{:S(2)}) %collective-permute-start.20) | collective-permute-done | bytes 294944 | tf_op jit(solution)/shard_map/ppermute | solution.py:417
  71.0 1.2 %shard_map.80 = (f32[3,10,144,128]{3,2,1,0:T(8,128)S(1)}, f32[3,7,144,128]{3,2,1,0:T(8,128)S(1)}, f32[3,4,144,128]{3,2,1,0:T(8,128)S(1)}, f32[3,10,144,128]{3,2,...) custom-call(f32[3,10,144,128]{3,2,1,0:T(8,128)S(1)} %get-tuple-eleme, ...), custom_call_target="tpu_custom_call", output_to_operand_aliasing={{0}: (0, {}), {1}: (11, {}), {2}: (12, {}), {3}: (13, {})} | custom-call | flops 5000000000 | bytes 18000000 | tf_op jit(solution)/shard_map/pallas_call | solution.py:38
  72.2 3.2 %collective-permute-start.24 = (f32[5,72,128]{2,1,0:T(8,128)S(1)}, f32[5,72,128]{2,1,0:T(8,128)S(1)}, u32[]{:S(2)}, u32[]{:S(2)}) collective-permute-start(f32[5,72,128]{2,1,0:T(8,128)S(1)} %get-tuple-element.125), channel_id=1, source_target_pairs={{4,8},{12,16},{20,24},{8,4},{16,12},{24,20},{5,9},{13,17},{21,25},... | collective-permute-start | bytes 552968 | tf_op jit(solution)/shard_map/ppermute | solution.py:417
  75.5 1.4 %shard_map.81 = (f32[3,10,144,128]{3,2,1,0:T(8,128)S(1)}, f32[1,9,4,128,128]{4,3,2,1,0:T(8,128)}) custom-call(f32[3,10,144,128]{3,2,1,0:T(8,128)S(1)} %get-tuple-element.119.refs_0_, f32[3,7,144,128]{3,2,1,0:T(8,128)S(1)} %get-tuple-element.120.refs_1_, f32[3,4,144,128]{3,2,1,0:T(8,128)S(1)} %get-tuple-element.121.refs_2_, ...), custom_call_target="tpu_custom_call", output_to_operand_aliasing={{0}: (0, {})} | custom-call | flops 5000000000 | bytes 18000000 | tf_op jit(solution)/shard_map/pallas_call | solution.py:38
  77.0 3.0 %collective-permute-done.24.refs_3_ = f32[5,72,128]{2,1,0:T(8,128)S(1)} collective-permute-done((f32[5,72,128]{2,1,0:T(8,128)S(1)}, f32[5,72,128]{2,1,0:T(8,128)S(1)}, u32[]{:S(2)}, u32[]{:S(2)}) %collective-permute-start.24) | collective-permute-done | bytes 184352 | tf_op jit(solution)/shard_map/ppermute | solution.py:417
  80.0 1.5 %shard_map.82 = (f32[3,10,144,128]{3,2,1,0:T(8,128)S(1)}, f32[1,9,4,128,128]{4,3,2,1,0:T(8,128)}) custom-call(f32[3,10,144,128]{3,2,1,0:T(8,128)S(1)} %get-tuple-element.124.refs_0_, f32[3,7,144,128]{3,2,1,0:T(8,128)S(1)} %get-tuple-element.120.refs_1_, ...), custom_call_target="tpu_custom_call", output_to_operand_aliasing={{0}: (0, {}), {1}: (11, {})} | custom-call | flops 5000000000 | bytes 18000000 | tf_op jit(solution)/shard_map/pallas_call | solution.py:38
  (44 shorter events, 6.1 us)
Async XLA Ops:
  1.1 8.3 %collective-permute-start = (f32[6,32,128]{2,1,0:T(8,128)S(1)}, f32[6,32,128]{2,1,0:T(8,128)S(1)}, u32[]{:S(2)}, u32[]{:S(2)}) collective-permute-start(f32[6,32,128]{2,1,0:T(8,128)S(1)} %get-tuple-element.67), channel_id=1, source_target_pairs={{4,8},{12,16},{20,24},{8,4},{16,12},{24,20},{5,9},{13,17},{21,25},... | collective-permute-start | bytes 294920 | tf_op jit(solution)/shard_map/ppermute | solution.py:425
  4.7 9.2 %collective-permute-start.4 = (f32[8,32,128]{2,1,0:T(8,128)S(1)}, f32[8,32,128]{2,1,0:T(8,128)S(1)}, u32[]{:S(2)}, u32[]{:S(2)}) collective-permute-start(f32[8,32,128]{2,1,0:T(8,128)S(1)} %get-tuple-element.75.refs_7_), channel_id=1, source_target_pairs={{0,2},{1,3},{2,0},{3,1},{4,6},{5,7},{6,4},{7,5},{8,10},{9,11},{10,... | collective-permute-start | bytes 393224 | tf_op jit(solution)/shard_map/ppermute | solution.py:380
  7.1 6.9 %collective-permute-start.3 = (f32[8,32,128]{2,1,0:T(8,128)S(1)}, f32[8,32,128]{2,1,0:T(8,128)S(1)}, u32[]{:S(2)}, u32[]{:S(2)}) collective-permute-start(f32[8,32,128]{2,1,0:T(8,128)S(1)} %get-tuple-element.75.refs_7_), channel_id=1, source_target_pairs={{0,1},{1,0},{2,3},{3,2},{4,5},{5,4},{6,7},{7,6},{8,9},{9,8},{10,11... | collective-permute-start | bytes 393224 | tf_op jit(solution)/shard_map/ppermute | solution.py:379
  10.6 11.9 %collective-permute-start.1 = (f32[5,128,128]{2,1,0:T(8,128)S(1)}, f32[5,128,128]{2,1,0:T(8,128)S(1)}, u32[]{:S(2)}, u32[]{:S(2)}) collective-permute-start(f32[5,128,128]{2,1,0:T(8,128)S(1)} %get-tuple-element.68), channel_id=1, source_target_pairs={{4,8},{12,16},{20,24},{8,4},{16,12},{24,20},{5,9},{13,17},{21,25},... | collective-permute-start | bytes 983048 | tf_op jit(solution)/shard_map/ppermute | solution.py:417
  13.9 8.6 %collective-permute-start.2 = (f32[5,128,128]{2,1,0:T(8,128)S(1)}, f32[5,128,128]{2,1,0:T(8,128)S(1)}, u32[]{:S(2)}, u32[]{:S(2)}) collective-permute-start(f32[5,128,128]{2,1,0:T(8,128)S(1)} %get-tuple-element.69), channel_id=1, source_target_pairs={{0,4},{8,12},{16,20},{24,28},{4,0},{12,8},{20,16},{28,24},{1,5},{9... | collective-permute-start | bytes 983048 | tf_op jit(solution)/shard_map/ppermute | solution.py:417
  14.0 3.0 %copy-start = (f32[1,9,4,128,128]{4,3,2,1,0:T(8,128)S(1)}, f32[1,9,4,128,128]{4,3,2,1,0:T(8,128)}, u32[]{:S(2)}) copy-start(f32[1,9,4,128,128]{4,3,2,1,0:T(8,128)} %refs_0_.5) | copy-start | bytes 7077892
  14.1 6.0 %collective-permute-start.5 = (f32[8,32,128]{2,1,0:T(8,128)S(1)}, f32[8,32,128]{2,1,0:T(8,128)S(1)}, u32[]{:S(2)}, u32[]{:S(2)}) collective-permute-start(f32[8,32,128]{2,1,0:T(8,128)S(1)} %shard_map.67.refs_0_), channel_id=1, source_target_pairs={{0,1},{1,0},{2,3},{3,2},{4,5},{5,4},{6,7},{7,6},{8,9},{9,8},{10,11... | collective-permute-start | bytes 393224 | tf_op jit(solution)/shard_map/ppermute | solution.py:384
  14.9 12.8 %collective-permute-start.9 = (f32[14,32,128]{2,1,0:T(8,128)S(1)}, f32[14,32,128]{2,1,0:T(8,128)S(1)}, u32[]{:S(2)}, u32[]{:S(2)}) collective-permute-start(f32[14,32,128]{2,1,0:T(8,128)S(1)} %shard_map.72.refs_1_), channel_id=1, source_target_pairs={{0,2},{1,3},{2,0},{3,1},{4,6},{5,7},{6,4},{7,5},{8,10},{9,11},{10,... | collective-permute-start | bytes 688136 | tf_op jit(solution)/shard_map/ppermute | solution.py:380
  17.0 10.7 %collective-permute-start.8 = (f32[14,32,128]{2,1,0:T(8,128)S(1)}, f32[14,32,128]{2,1,0:T(8,128)S(1)}, u32[]{:S(2)}, u32[]{:S(2)}) collective-permute-start(f32[14,32,128]{2,1,0:T(8,128)S(1)} %shard_map.72.refs_1_), channel_id=1, source_target_pairs={{0,1},{1,0},{2,3},{3,2},{4,5},{5,4},{6,7},{7,6},{8,9},{9,8},{10,11... | collective-permute-start | bytes 688136 | tf_op jit(solution)/shard_map/ppermute | solution.py:379
  22.9 13.6 %collective-permute-start.6 = (f32[9,80,128]{2,1,0:T(8,128)S(1)}, f32[9,80,128]{2,1,0:T(8,128)S(1)}, u32[]{:S(2)}, u32[]{:S(2)}) collective-permute-start(f32[9,80,128]{2,1,0:T(8,128)S(1)} %get-tuple-element.81), channel_id=1, source_target_pairs={{4,8},{12,16},{20,24},{8,4},{16,12},{24,20},{5,9},{13,17},{21,25},... | collective-permute-start | bytes 1105928 | tf_op jit(solution)/shard_map/ppermute | solution.py:417
  26.6 9.8 %collective-permute-start.7 = (f32[9,80,128]{2,1,0:T(8,128)S(1)}, f32[9,80,128]{2,1,0:T(8,128)S(1)}, u32[]{:S(2)}, u32[]{:S(2)}) collective-permute-start(f32[9,80,128]{2,1,0:T(8,128)S(1)} %get-tuple-element.82), channel_id=1, source_target_pairs={{0,4},{8,12},{16,20},{24,28},{4,0},{12,8},{20,16},{28,24},{1,5},{9... | collective-permute-start | bytes 1105928 | tf_op jit(solution)/shard_map/ppermute | solution.py:417
  27.7 7.0 %collective-permute-start.10 = (f32[14,32,128]{2,1,0:T(8,128)S(1)}, f32[14,32,128]{2,1,0:T(8,128)S(1)}, u32[]{:S(2)}, u32[]{:S(2)}) collective-permute-start(f32[14,32,128]{2,1,0:T(8,128)S(1)} %shard_map.73), channel_id=1, source_target_pairs={{0,1},{1,0},{2,3},{3,2},{4,5},{5,4},{6,7},{7,6},{8,9},{9,8},{10,11... | collective-permute-start | bytes 688136 | tf_op jit(solution)/shard_map/ppermute | solution.py:384
  29.9 4.8 %collective-permute-start.11 = (f32[9,48,128]{2,1,0:T(8,128)S(1)}, f32[9,48,128]{2,1,0:T(8,128)S(1)}, u32[]{:S(2)}, u32[]{:S(2)}) collective-permute-start(f32[9,48,128]{2,1,0:T(8,128)S(1)} %get-tuple-element.84), channel_id=1, source_target_pairs={{0,4},{8,12},{16,20},{24,28},{4,0},{12,8},{20,16},{28,24},{1,5},{9... | collective-permute-start | bytes 663560 | tf_op jit(solution)/shard_map/ppermute | solution.py:417
  31.2 12.1 %collective-permute-start.13 = (f32[9,48,128]{2,1,0:T(8,128)S(1)}, f32[9,48,128]{2,1,0:T(8,128)S(1)}, u32[]{:S(2)}, u32[]{:S(2)}) collective-permute-start(f32[9,48,128]{2,1,0:T(8,128)S(1)} %get-tuple-element.90), channel_id=1, source_target_pairs={{4,8},{12,16},{20,24},{8,4},{16,12},{24,20},{5,9},{13,17},{21,25},... | collective-permute-start | bytes 663560 | tf_op jit(solution)/shard_map/ppermute | solution.py:417
  34.8 2.9 %collective-permute-start.12 = (f32[6,128,128]{2,1,0:T(8,128)S(1)}, f32[6,128,128]{2,1,0:T(8,128)S(1)}, u32[]{:S(2)}, u32[]{:S(2)}) collective-permute-start(f32[6,128,128]{2,1,0:T(8,128)S(1)} %get-tuple-element.88), channel_id=1, source_target_pairs={{0,4},{8,12},{16,20},{24,28},{4,0},{12,8},{20,16},{28,24},{1,5},{9... | collective-permute-start | bytes 1179656 | tf_op jit(solution)/shard_map/ppermute | solution.py:524
  39.0 12.9 %collective-permute-start.14 = (f32[9,72,128]{2,1,0:T(8,128)S(1)}, f32[9,72,128]{2,1,0:T(8,128)S(1)}, u32[]{:S(2)}, u32[]{:S(2)}) collective-permute-start(f32[9,72,128]{2,1,0:T(8,128)S(1)} %get-tuple-element.100), channel_id=1, source_target_pairs={{4,8},{12,16},{20,24},{8,4},{16,12},{24,20},{5,9},{13,17},{21,25},... | collective-permute-start | bytes 995336 | tf_op jit(solution)/shard_map/ppermute | solution.py:417
  43.2 8.7 %collective-permute-start.15 = (f32[9,72,128]{2,1,0:T(8,128)S(1)}, f32[9,72,128]{2,1,0:T(8,128)S(1)}, u32[]{:S(2)}, u32[]{:S(2)}) collective-permute-start(f32[9,72,128]{2,1,0:T(8,128)S(1)} %get-tuple-element.101), channel_id=1, source_target_pairs={{0,4},{8,12},{16,20},{24,28},{4,0},{12,8},{20,16},{28,24},{1,5},{9... | collective-permute-start | bytes 995336 | tf_op jit(solution)/shard_map/ppermute | solution.py:417
  44.3 13.0 %collective-permute-start.16 = (f32[9,56,128]{2,1,0:T(8,128)S(1)}, f32[9,56,128]{2,1,0:T(8,128)S(1)}, u32[]{:S(2)}, u32[]{:S(2)}) collective-permute-start(f32[9,56,128]{2,1,0:T(8,128)S(1)} %get-tuple-element.103), channel_id=1, source_target_pairs={{4,8},{12,16},{20,24},{8,4},{16,12},{24,20},{5,9},{13,17},{21,25},... | collective-permute-start | bytes 774152 | tf_op jit(solution)/shard_map/ppermute | solution.py:417
  47.0 10.3 %collective-permute-start.17 = (f32[9,56,128]{2,1,0:T(8,128)S(1)}, f32[9,56,128]{2,1,0:T(8,128)S(1)}, u32[]{:S(2)}, u32[]{:S(2)}) collective-permute-start(f32[9,56,128]{2,1,0:T(8,128)S(1)} %get-tuple-element.104), channel_id=1, source_target_pairs={{0,4},{8,12},{16,20},{24,28},{4,0},{12,8},{20,16},{28,24},{1,5},{9... | collective-permute-start | bytes 774152 | tf_op jit(solution)/shard_map/ppermute | solution.py:417
  53.2 11.5 %collective-permute-start.18 = (f32[9,64,128]{2,1,0:T(8,128)S(1)}, f32[9,64,128]{2,1,0:T(8,128)S(1)}, u32[]{:S(2)}, u32[]{:S(2)}) collective-permute-start(f32[9,64,128]{2,1,0:T(8,128)S(1)} %get-tuple-element.111), channel_id=1, source_target_pairs={{4,8},{12,16},{20,24},{8,4},{16,12},{24,20},{5,9},{13,17},{21,25},... | collective-permute-start | bytes 884744 | tf_op jit(solution)/shard_map/ppermute | solution.py:417
  57.2 7.5 %collective-permute-start.19 = (f32[9,64,128]{2,1,0:T(8,128)S(1)}, f32[9,64,128]{2,1,0:T(8,128)S(1)}, u32[]{:S(2)}, u32[]{:S(2)}) collective-permute-start(f32[9,64,128]{2,1,0:T(8,128)S(1)} %get-tuple-element.112), channel_id=1, source_target_pairs={{0,4},{8,12},{16,20},{24,28},{4,0},{12,8},{20,16},{28,24},{1,5},{9... | collective-permute-start | bytes 884744 | tf_op jit(solution)/shard_map/ppermute | solution.py:417
  58.5 12.5 %collective-permute-start.20 = (f32[9,64,128]{2,1,0:T(8,128)S(1)}, f32[9,64,128]{2,1,0:T(8,128)S(1)}, u32[]{:S(2)}, u32[]{:S(2)}) collective-permute-start(f32[9,64,128]{2,1,0:T(8,128)S(1)} %get-tuple-element.114), channel_id=1, source_target_pairs={{4,8},{12,16},{20,24},{8,4},{16,12},{24,20},{5,9},{13,17},{21,25},... | collective-permute-start | bytes 884744 | tf_op jit(solution)/shard_map/ppermute | solution.py:417
  62.1 8.9 %collective-permute-start.21 = (f32[9,64,128]{2,1,0:T(8,128)S(1)}, f32[9,64,128]{2,1,0:T(8,128)S(1)}, u32[]{:S(2)}, u32[]{:S(2)}) collective-permute-start(f32[9,64,128]{2,1,0:T(8,128)S(1)} %get-tuple-element.115), channel_id=1, source_target_pairs={{0,4},{8,12},{16,20},{24,28},{4,0},{12,8},{20,16},{28,24},{1,5},{9... | collective-permute-start | bytes 884744 | tf_op jit(solution)/shard_map/ppermute | solution.py:417
  65.8 9.7 %collective-permute-start.22 = (f32[5,56,128]{2,1,0:T(8,128)S(1)}, f32[5,56,128]{2,1,0:T(8,128)S(1)}, u32[]{:S(2)}, u32[]{:S(2)}) collective-permute-start(f32[5,56,128]{2,1,0:T(8,128)S(1)} %get-tuple-element.122), channel_id=1, source_target_pairs={{4,8},{12,16},{20,24},{8,4},{16,12},{24,20},{5,9},{13,17},{21,25},... | collective-permute-start | bytes 430088 | tf_op jit(solution)/shard_map/ppermute | solution.py:417
  67.7 7.8 %collective-permute-start.23 = (f32[5,56,128]{2,1,0:T(8,128)S(1)}, f32[5,56,128]{2,1,0:T(8,128)S(1)}, u32[]{:S(2)}, u32[]{:S(2)}) collective-permute-start(f32[5,56,128]{2,1,0:T(8,128)S(1)} %get-tuple-element.123), channel_id=1, source_target_pairs={{0,4},{8,12},{16,20},{24,28},{4,0},{12,8},{20,16},{28,24},{1,5},{9... | collective-permute-start | bytes 430088 | tf_op jit(solution)/shard_map/ppermute | solution.py:417
  72.2 7.8 %collective-permute-start.24 = (f32[5,72,128]{2,1,0:T(8,128)S(1)}, f32[5,72,128]{2,1,0:T(8,128)S(1)}, u32[]{:S(2)}, u32[]{:S(2)}) collective-permute-start(f32[5,72,128]{2,1,0:T(8,128)S(1)} %get-tuple-element.125), channel_id=1, source_target_pairs={{4,8},{12,16},{20,24},{8,4},{16,12},{24,20},{5,9},{13,17},{21,25},... | collective-permute-start | bytes 552968 | tf_op jit(solution)/shard_map/ppermute | solution.py:417
  75.4 4.6 %collective-permute-start.25 = (f32[5,72,128]{2,1,0:T(8,128)S(1)}, f32[5,72,128]{2,1,0:T(8,128)S(1)}, u32[]{:S(2)}, u32[]{:S(2)}) collective-permute-start(f32[5,72,128]{2,1,0:T(8,128)S(1)} %get-tuple-element.126), channel_id=1, source_target_pairs={{0,4},{8,12},{16,20},{24,28},{4,0},{12,8},{20,16},{28,24},{1,5},{9... | collective-permute-start | bytes 552968 | tf_op jit(solution)/shard_map/ppermute | solution.py:417

commit v6 on v5

--- a/solution.py
+++ b/solution.py
@@ -108,6 +108,10 @@
     zeros = jnp.zeros((ref.shape[0], ref.shape[1], PAD, ref.shape[3]), F32)
     ref[:, :, :PAD, :] = zeros
     ref[:, :, PAD + rows:, :] = zeros
+
+
+def zero_pad(ref, first):
+    ref[:, :, first:first + PAD, :] = jnp.zeros((ref.shape[0], ref.shape[1], PAD, ref.shape[3]), F32)
 
 
 class Plan:
@@ -539,10 +543,8 @@
             if final:
                 plan.finish(refs, step, which, *scratch)
                 return
-            if which == 0:
-                zero_pads(refs["sh_next"], rows)
-                zero_pads(refs["so_next"], rows)
-                zero_pads(refs["vel_next"], rows)
+            for name in ("sh_next", "so_next", "vel_next"):
+                zero_pad(refs[name], 0 if which == 0 else PAD + rows)
             plan.stress(refs, step, which, False)
             plan.velocity(
                 refs, step + 1, which, refs["sh_next"], refs["so_next"],

time: 82 us -> 82 us (level)
  no operation moved by 1% of the time
where the time goes in v6:
time: 82 us; the launch traced here: 81.5 us
  starting transfers between devices  46 us (56%)
  waiting for transfers between devices  19.2 us (23%)
  Pallas kernels  15 us (18%)
  local copies, waits for them, and re-layouts  0.96 us (1%)
    ppermute x9, starting transfers between devices, exchange(): lax.ppermute(to_far, 'aper', far)  30.2 us
    ppermute x9, waiting for transfers between devices, exchange(): lax.ppermute(to_far, 'aper', far)  15.9 us
    pallas_call x19, Pallas kernels, call(): pl.pallas_call(kernel, out_shape=[pltpu.HBM(shape, F32) if name in anywhe...  15 us
    ppermute x2, starting transfers between devices, spread(): across = lax.ppermute(mine, 'shot', pairs(2))  4.53 us
    ppermute x1, starting transfers between devices, per_device(): edge = lax.ppermute(sent['edge'], 'aper', far)  3.68 us
    ppermute x2, starting transfers between devices, finish(): handed = lax.ppermute(held, 'shot', pairs(1))  2.76 us
    ppermute x9, starting transfers between devices, exchange(): lax.ppermute(to_near, 'aper', near)  1.88 us
  transfers between devices with their start and end apart: 26, of which 8 were waited for; matrix products, arithmetic and copies ran while one was open for 1% of the time, Pallas kernels for 15%

profile of v6, /device:TPU:3, one launch (start us, length us, event | category | flops | bytes accessed | tf_op | source)
XLA Modules:
  0.0 81.5 jit_solution(10222248134711052110)
XLA Ops:
  1.1 3.7 %collective-permute-start = (f32[6,32,128]{2,1,0:T(8,128)S(1)}, f32[6,32,128]{2,1,0:T(8,128)S(1)}, u32[]{:S(2)}, u32[]{:S(2)}) collective-permute-start(f32[6,32,128]{2,1,0:T(8,128)S(1)} %get-tuple-element.67), channel_id=1, source_target_pairs={{4,8},{12,16},{20,24},{8,4},{16,12},{24,20},{5,9},{13,17},{21,25},... | collective-permute-start | bytes 294920 | tf_op jit(solution)/shard_map/ppermute | solution.py:429
  4.7 2.4 %collective-permute-start.4 = (f32[8,32,128]{2,1,0:T(8,128)S(1)}, f32[8,32,128]{2,1,0:T(8,128)S(1)}, u32[]{:S(2)}, u32[]{:S(2)}) collective-permute-start(f32[8,32,128]{2,1,0:T(8,128)S(1)} %get-tuple-element.75.refs_7_), channel_id=1, source_target_pairs={{0,2},{1,3},{2,0},{3,1},{4,6},{5,7},{6,4},{7,5},{8,10},{9,11},{10,... | collective-permute-start | bytes 393224 | tf_op jit(solution)/shard_map/ppermute | solution.py:384
  7.1 1.3 %collective-permute-start.3 = (f32[8,32,128]{2,1,0:T(8,128)S(1)}, f32[8,32,128]{2,1,0:T(8,128)S(1)}, u32[]{:S(2)}, u32[]{:S(2)}) collective-permute-start(f32[8,32,128]{2,1,0:T(8,128)S(1)} %get-tuple-element.75.refs_7_), channel_id=1, source_target_pairs={{0,1},{1,0},{2,3},{3,2},{4,5},{5,4},{6,7},{7,6},{8,9},{9,8},{10,11... | collective-permute-start | bytes 393224 | tf_op jit(solution)/shard_map/ppermute | solution.py:383
  9.3 1.2 %shard_map.65 = (f32[5,128,128]{2,1,0:T(8,128)S(1)}, f32[5,128,128]{2,1,0:T(8,128)S(1)}) custom-call(f32[1,9,4,128,128]{4,3,2,1,0:T(8,128)} %refs_0_.5, f32[6,32,128]{2,1,0:T(8,128)S(1)} %collective-permute-done.refs_1_.refs_2_), custom_call_target="tpu_custom_call" | custom-call | flops 5000000000 | bytes 18000000 | tf_op jit(solution)/shard_map/pallas_call | solution.py:38
  10.6 3.3 %collective-permute-start.1 = (f32[5,128,128]{2,1,0:T(8,128)S(1)}, f32[5,128,128]{2,1,0:T(8,128)S(1)}, u32[]{:S(2)}, u32[]{:S(2)}) collective-permute-start(f32[5,128,128]{2,1,0:T(8,128)S(1)} %get-tuple-element.68), channel_id=1, source_target_pairs={{4,8},{12,16},{20,24},{8,4},{16,12},{24,20},{5,9},{13,17},{21,25},... | collective-permute-start | bytes 983048 | tf_op jit(solution)/shard_map/ppermute | solution.py:421
  14.9 2.2 %collective-permute-start.9 = (f32[14,32,128]{2,1,0:T(8,128)S(1)}, f32[14,32,128]{2,1,0:T(8,128)S(1)}, u32[]{:S(2)}, u32[]{:S(2)}) collective-permute-start(f32[14,32,128]{2,1,0:T(8,128)S(1)} %shard_map.72.refs_1_), channel_id=1, source_target_pairs={{0,2},{1,3},{2,0},{3,1},{4,6},{5,7},{6,4},{7,5},{8,10},{9,11},{10,... | collective-permute-start | bytes 688136 | tf_op jit(solution)/shard_map/ppermute | solution.py:384
  17.1 2.1 %shard_map.66 = (f32[3,7,144,128]{3,2,1,0:T(8,128)S(1)}, f32[3,4,144,128]{3,2,1,0:T(8,128)S(1)}, f32[3,4,128,128]{3,2,1,0:T(8,128)S(1)}, f32[3,4,128,128]{3,2,1,0:T(8,128)S(1)}, f32[128,128]{1,0:T(8,128)S(1)}) custom-call(f32[1,9,4,128,128]{4,3,2,1,0:T(8,128)S(1)} %copy-done, s32[128,4]{1,0:T(8,128)S(1)} %bitcast.1), custom_call_target="tpu_custom_call" | custom-call | flops 5000000000 | bytes 18000000 | tf_op jit(solution)/shard_map/pallas_call | solution.py:38
  20.0 2.5 %collective-permute-done.1.refs_0_ = f32[5,128,128]{2,1,0:T(8,128)S(1)} collective-permute-done((f32[5,128,128]{2,1,0:T(8,128)S(1)}, f32[5,128,128]{2,1,0:T(8,128)S(1)}, u32[]{:S(2)}, u32[]{:S(2)}) %collective-permute-start.1) | collective-permute-done | bytes 327712 | tf_op jit(solution)/shard_map/ppermute | solution.py:421
  22.9 3.8 %collective-permute-start.6 = (f32[9,80,128]{2,1,0:T(8,128)S(1)}, f32[9,80,128]{2,1,0:T(8,128)S(1)}, u32[]{:S(2)}, u32[]{:S(2)}) collective-permute-start(f32[9,80,128]{2,1,0:T(8,128)S(1)} %get-tuple-element.81), channel_id=1, source_target_pairs={{4,8},{12,16},{20,24},{8,4},{16,12},{24,20},{5,9},{13,17},{21,25},... | collective-permute-start | bytes 1105928 | tf_op jit(solution)/shard_map/ppermute | solution.py:421
  27.7 1.9 %collective-permute-start.10 = (f32[14,32,128]{2,1,0:T(8,128)S(1)}, f32[14,32,128]{2,1,0:T(8,128)S(1)}, u32[]{:S(2)}, u32[]{:S(2)}) collective-permute-start(f32[14,32,128]{2,1,0:T(8,128)S(1)} %shard_map.73), channel_id=1, source_target_pairs={{0,1},{1,0},{2,3},{3,2},{4,5},{5,4},{6,7},{7,6},{8,9},{9,8},{10,11... | collective-permute-start | bytes 688136 | tf_op jit(solution)/shard_map/ppermute | solution.py:388
  29.9 1.3 %collective-permute-start.11 = (f32[9,48,128]{2,1,0:T(8,128)S(1)}, f32[9,48,128]{2,1,0:T(8,128)S(1)}, u32[]{:S(2)}, u32[]{:S(2)}) collective-permute-start(f32[9,48,128]{2,1,0:T(8,128)S(1)} %get-tuple-element.84), channel_id=1, source_target_pairs={{0,4},{8,12},{16,20},{24,28},{4,0},{12,8},{20,16},{28,24},{1,5},{9... | collective-permute-start | bytes 663560 | tf_op jit(solution)/shard_map/ppermute | solution.py:421
  31.2 3.5 %collective-permute-start.13 = (f32[9,48,128]{2,1,0:T(8,128)S(1)}, f32[9,48,128]{2,1,0:T(8,128)S(1)}, u32[]{:S(2)}, u32[]{:S(2)}) collective-permute-start(f32[9,48,128]{2,1,0:T(8,128)S(1)} %get-tuple-element.90), channel_id=1, source_target_pairs={{4,8},{12,16},{20,24},{8,4},{16,12},{24,20},{5,9},{13,17},{21,25},... | collective-permute-start | bytes 663560 | tf_op jit(solution)/shard_map/ppermute | solution.py:421
  34.8 1.6 %collective-permute-start.12 = (f32[6,128,128]{2,1,0:T(8,128)S(1)}, f32[6,128,128]{2,1,0:T(8,128)S(1)}, u32[]{:S(2)}, u32[]{:S(2)}) collective-permute-start(f32[6,128,128]{2,1,0:T(8,128)S(1)} %get-tuple-element.88), channel_id=1, source_target_pairs={{0,4},{8,12},{16,20},{24,28},{4,0},{12,8},{20,16},{28,24},{1,5},{9... | collective-permute-start | bytes 1179656 | tf_op jit(solution)/shard_map/ppermute | solution.py:528
  36.5 1.3 %collective-permute-done.12.refs_11_ = f32[6,128,128]{2,1,0:T(8,128)S(1)} collective-permute-done((f32[6,128,128]{2,1,0:T(8,128)S(1)}, f32[6,128,128]{2,1,0:T(8,128)S(1)}, u32[]{:S(2)}, u32[]{:S(2)}) %collective-permute-start.12) | collective-permute-done | bytes 393248 | tf_op jit(solution)/shard_map/ppermute | solution.py:528
  37.8 1.2 %shard_map.75 = (f32[3,10,144,128]{3,2,1,0:T(8,128)S(1)}, f32[3,7,144,128]{3,2,1,0:T(8,128)S(1)}, f32[3,4,144,128]{3,2,1,0:T(8,128)S(1)}, f32[3,10,144,128]{3,2,...) custom-call(f32[3,10,144,128]{3,2,1,0:T(8,128)S(1)} %shard_map.70.re, ...), custom_call_target="tpu_custom_call", output_to_operand_aliasing={{0}: (0, {}), {4}: (8, {}), {5}: (9, {}), {6}: (10, {})} | custom-call | flops 5000000000 | bytes 18000000 | tf_op jit(solution)/shard_map/pallas_call | solution.py:38
  39.0 4.2 %collective-permute-start.14 = (f32[9,72,128]{2,1,0:T(8,128)S(1)}, f32[9,72,128]{2,1,0:T(8,128)S(1)}, u32[]{:S(2)}, u32[]{:S(2)}) collective-permute-start(f32[9,72,128]{2,1,0:T(8,128)S(1)} %get-tuple-element.100), channel_id=1, source_target_pairs={{4,8},{12,16},{20,24},{8,4},{16,12},{24,20},{5,9},{13,17},{21,25},... | collective-permute-start | bytes 995336 | tf_op jit(solution)/shard_map/ppermute | solution.py:421
  43.2 1.1 %shard_map.76 = (f32[3,10,144,128]{3,2,1,0:T(8,128)S(1)}, f32[3,7,144,128]{3,2,1,0:T(8,128)S(1)}, f32[3,4,144,128]{3,2,1,0:T(8,128)S(1)}, f32[3,10,144,128]{3,2,...) custom-call(f32[3,10,144,128]{3,2,1,0:T(8,128)S(1)} %get-tuple-eleme, ...), custom_call_target="tpu_custom_call", output_to_operand_aliasing={{0}: (0, {}), {1}: (11, {}), {2}: (12, {}), {3}: (13, {})} | custom-call | flops 5000000000 | bytes 18000000 | tf_op jit(solution)/shard_map/pallas_call | solution.py:38
  44.3 2.7 %collective-permute-start.16 = (f32[9,56,128]{2,1,0:T(8,128)S(1)}, f32[9,56,128]{2,1,0:T(8,128)S(1)}, u32[]{:S(2)}, u32[]{:S(2)}) collective-permute-start(f32[9,56,128]{2,1,0:T(8,128)S(1)} %get-tuple-element.103), channel_id=1, source_target_pairs={{4,8},{12,16},{20,24},{8,4},{16,12},{24,20},{5,9},{13,17},{21,25},... | collective-permute-start | bytes 774152 | tf_op jit(solution)/shard_map/ppermute | solution.py:421
  47.1 4.8 %collective-permute-done.14.refs_3_ = f32[9,72,128]{2,1,0:T(8,128)S(1)} collective-permute-done((f32[9,72,128]{2,1,0:T(8,128)S(1)}, f32[9,72,128]{2,1,0:T(8,128)S(1)}, u32[]{:S(2)}, u32[]{:S(2)}) %collective-permute-start.14) | collective-permute-done | bytes 331808 | tf_op jit(solution)/shard_map/ppermute | solution.py:421
  51.9 1.3 %shard_map.77 = (f32[3,10,144,128]{3,2,1,0:T(8,128)S(1)}, f32[3,7,144,128]{3,2,1,0:T(8,128)S(1)}, f32[3,4,144,128]{3,2,1,0:T(8,128)S(1)}, f32[3,10,144,128]{3,2,...) custom-call(f32[3,10,144,128]{3,2,1,0:T(8,128)S(1)} %get-tuple-element.97., ...), custom_call_target="tpu_custom_call", output_to_operand_aliasing={{0}: (0, {})} | custom-call | flops 5000000000 | bytes 18000000 | tf_op jit(solution)/shard_map/pallas_call | solution.py:38
  53.1 4.0 %collective-permute-start.18 = (f32[9,64,128]{2,1,0:T(8,128)S(1)}, f32[9,64,128]{2,1,0:T(8,128)S(1)}, u32[]{:S(2)}, u32[]{:S(2)}) collective-permute-start(f32[9,64,128]{2,1,0:T(8,128)S(1)} %get-tuple-element.111), channel_id=1, source_target_pairs={{4,8},{12,16},{20,24},{8,4},{16,12},{24,20},{5,9},{13,17},{21,25},... | collective-permute-start | bytes 884744 | tf_op jit(solution)/shard_map/ppermute | solution.py:421
  57.3 1.2 %shard_map.78 = (f32[3,10,144,128]{3,2,1,0:T(8,128)S(1)}, f32[3,7,144,128]{3,2,1,0:T(8,128)S(1)}, f32[3,4,144,128]{3,2,1,0:T(8,128)S(1)}, f32[3,10,144,128]{3,2,...) custom-call(f32[3,10,144,128]{3,2,1,0:T(8,128)S(1)} %get-tuple-eleme, ...), custom_call_target="tpu_custom_call", output_to_operand_aliasing={{0}: (0, {}), {1}: (11, {}), {2}: (12, {}), {3}: (13, {})} | custom-call | flops 5000000000 | bytes 18000000 | tf_op jit(solution)/shard_map/pallas_call | solution.py:38
  58.5 3.6 %collective-permute-start.20 = (f32[9,64,128]{2,1,0:T(8,128)S(1)}, f32[9,64,128]{2,1,0:T(8,128)S(1)}, u32[]{:S(2)}, u32[]{:S(2)}) collective-permute-start(f32[9,64,128]{2,1,0:T(8,128)S(1)} %get-tuple-element.114), channel_id=1, source_target_pairs={{4,8},{12,16},{20,24},{8,4},{16,12},{24,20},{5,9},{13,17},{21,25},... | collective-permute-start | bytes 884744 | tf_op jit(solution)/shard_map/ppermute | solution.py:421
  62.2 2.5 %collective-permute-done.18.refs_3_ = f32[9,64,128]{2,1,0:T(8,128)S(1)} collective-permute-done((f32[9,64,128]{2,1,0:T(8,128)S(1)}, f32[9,64,128]{2,1,0:T(8,128)S(1)}, u32[]{:S(2)}, u32[]{:S(2)}) %collective-permute-start.18) | collective-permute-done | bytes 294944 | tf_op jit(solution)/shard_map/ppermute | solution.py:421
  64.7 1.1 %shard_map.79 = (f32[3,10,144,128]{3,2,1,0:T(8,128)S(1)}, f32[3,7,144,128]{3,2,1,0:T(8,128)S(1)}, f32[3,4,144,128]{3,2,1,0:T(8,128)S(1)}, f32[3,10,144,128]{3,2,...) custom-call(f32[3,10,144,128]{3,2,1,0:T(8,128)S(1)} %get-tuple-element.108, ...), custom_call_target="tpu_custom_call", output_to_operand_aliasing={{0}: (0, {})} | custom-call | flops 5000000000 | bytes 18000000 | tf_op jit(solution)/shard_map/pallas_call | solution.py:38
  65.8 1.9 %collective-permute-start.22 = (f32[5,56,128]{2,1,0:T(8,128)S(1)}, f32[5,56,128]{2,1,0:T(8,128)S(1)}, u32[]{:S(2)}, u32[]{:S(2)}) collective-permute-start(f32[5,56,128]{2,1,0:T(8,128)S(1)} %get-tuple-element.122), channel_id=1, source_target_pairs={{4,8},{12,16},{20,24},{8,4},{16,12},{24,20},{5,9},{13,17},{21,25},... | collective-permute-start | bytes 430088 | tf_op jit(solution)/shard_map/ppermute | solution.py:421
  67.8 3.2 %collective-permute-done.20.refs_3_ = f32[9,64,128]{2,1,0:T(8,128)S(1)} collective-permute-done((f32[9,64,128]{2,1,0:T(8,128)S(1)}, f32[9,64,128]{2,1,0:T(8,128)S(1)}, u32[]{:S(2)}, u32[]{:S(2)}) %collective-permute-start.20) | collective-permute-done | bytes 294944 | tf_op jit(solution)/shard_map/ppermute | solution.py:421
  71.0 1.3 %shard_map.80 = (f32[3,10,144,128]{3,2,1,0:T(8,128)S(1)}, f32[3,7,144,128]{3,2,1,0:T(8,128)S(1)}, f32[3,4,144,128]{3,2,1,0:T(8,128)S(1)}, f32[3,10,144,128]{3,2,...) custom-call(f32[3,10,144,128]{3,2,1,0:T(8,128)S(1)} %get-tuple-eleme, ...), custom_call_target="tpu_custom_call", output_to_operand_aliasing={{0}: (0, {}), {1}: (11, {}), {2}: (12, {}), {3}: (13, {})} | custom-call | flops 5000000000 | bytes 18000000 | tf_op jit(solution)/shard_map/pallas_call | solution.py:38
  72.2 3.2 %collective-permute-start.24 = (f32[5,72,128]{2,1,0:T(8,128)S(1)}, f32[5,72,128]{2,1,0:T(8,128)S(1)}, u32[]{:S(2)}, u32[]{:S(2)}) collective-permute-start(f32[5,72,128]{2,1,0:T(8,128)S(1)} %get-tuple-element.125), channel_id=1, source_target_pairs={{4,8},{12,16},{20,24},{8,4},{16,12},{24,20},{5,9},{13,17},{21,25},... | collective-permute-start | bytes 552968 | tf_op jit(solution)/shard_map/ppermute | solution.py:421
  75.6 1.4 %shard_map.81 = (f32[3,10,144,128]{3,2,1,0:T(8,128)S(1)}, f32[1,9,4,128,128]{4,3,2,1,0:T(8,128)}) custom-call(f32[3,10,144,128]{3,2,1,0:T(8,128)S(1)} %get-tuple-element.119.refs_0_, f32[3,7,144,128]{3,2,1,0:T(8,128)S(1)} %get-tuple-element.120.refs_1_, f32[3,4,144,128]{3,2,1,0:T(8,128)S(1)} %get-tuple-element.121.refs_2_, ...), custom_call_target="tpu_custom_call", output_to_operand_aliasing={{0}: (0, {})} | custom-call | flops 5000000000 | bytes 18000000 | tf_op jit(solution)/shard_map/pallas_call | solution.py:38
  77.0 3.0 %collective-permute-done.24.refs_3_ = f32[5,72,128]{2,1,0:T(8,128)S(1)} collective-permute-done((f32[5,72,128]{2,1,0:T(8,128)S(1)}, f32[5,72,128]{2,1,0:T(8,128)S(1)}, u32[]{:S(2)}, u32[]{:S(2)}) %collective-permute-start.24) | collective-permute-done | bytes 184352 | tf_op jit(solution)/shard_map/ppermute | solution.py:421
  80.0 1.5 %shard_map.82 = (f32[3,10,144,128]{3,2,1,0:T(8,128)S(1)}, f32[1,9,4,128,128]{4,3,2,1,0:T(8,128)}) custom-call(f32[3,10,144,128]{3,2,1,0:T(8,128)S(1)} %get-tuple-element.124.refs_0_, f32[3,7,144,128]{3,2,1,0:T(8,128)S(1)} %get-tuple-element.120.refs_1_, ...), custom_call_target="tpu_custom_call", output_to_operand_aliasing={{0}: (0, {}), {1}: (11, {})} | custom-call | flops 5000000000 | bytes 18000000 | tf_op jit(solution)/shard_map/pallas_call | solution.py:38
  (44 shorter events, 6.1 us)
Async XLA Ops:
  1.1 8.3 %collective-permute-start = (f32[6,32,128]{2,1,0:T(8,128)S(1)}, f32[6,32,128]{2,1,0:T(8,128)S(1)}, u32[]{:S(2)}, u32[]{:S(2)}) collective-permute-start(f32[6,32,128]{2,1,0:T(8,128)S(1)} %get-tuple-element.67), channel_id=1, source_target_pairs={{4,8},{12,16},{20,24},{8,4},{16,12},{24,20},{5,9},{13,17},{21,25},... | collective-permute-start | bytes 294920 | tf_op jit(solution)/shard_map/ppermute | solution.py:429
  4.7 9.2 %collective-permute-start.4 = (f32[8,32,128]{2,1,0:T(8,128)S(1)}, f32[8,32,128]{2,1,0:T(8,128)S(1)}, u32[]{:S(2)}, u32[]{:S(2)}) collective-permute-start(f32[8,32,128]{2,1,0:T(8,128)S(1)} %get-tuple-element.75.refs_7_), channel_id=1, source_target_pairs={{0,2},{1,3},{2,0},{3,1},{4,6},{5,7},{6,4},{7,5},{8,10},{9,11},{10,... | collective-permute-start | bytes 393224 | tf_op jit(solution)/shard_map/ppermute | solution.py:384
  7.1 6.9 %collective-permute-start.3 = (f32[8,32,128]{2,1,0:T(8,128)S(1)}, f32[8,32,128]{2,1,0:T(8,128)S(1)}, u32[]{:S(2)}, u32[]{:S(2)}) collective-permute-start(f32[8,32,128]{2,1,0:T(8,128)S(1)} %get-tuple-element.75.refs_7_), channel_id=1, source_target_pairs={{0,1},{1,0},{2,3},{3,2},{4,5},{5,4},{6,7},{7,6},{8,9},{9,8},{10,11... | collective-permute-start | bytes 393224 | tf_op jit(solution)/shard_map/ppermute | solution.py:383
  10.6 11.9 %collective-permute-start.1 = (f32[5,128,128]{2,1,0:T(8,128)S(1)}, f32[5,128,128]{2,1,0:T(8,128)S(1)}, u32[]{:S(2)}, u32[]{:S(2)}) collective-permute-start(f32[5,128,128]{2,1,0:T(8,128)S(1)} %get-tuple-element.68), channel_id=1, source_target_pairs={{4,8},{12,16},{20,24},{8,4},{16,12},{24,20},{5,9},{13,17},{21,25},... | collective-permute-start | bytes 983048 | tf_op jit(solution)/shard_map/ppermute | solution.py:421
  13.9 8.6 %collective-permute-start.2 = (f32[5,128,128]{2,1,0:T(8,128)S(1)}, f32[5,128,128]{2,1,0:T(8,128)S(1)}, u32[]{:S(2)}, u32[]{:S(2)}) collective-permute-start(f32[5,128,128]{2,1,0:T(8,128)S(1)} %get-tuple-element.69), channel_id=1, source_target_pairs={{0,4},{8,12},{16,20},{24,28},{4,0},{12,8},{20,16},{28,24},{1,5},{9... | collective-permute-start | bytes 983048 | tf_op jit(solution)/shard_map/ppermute | solution.py:421
  14.0 3.0 %copy-start = (f32[1,9,4,128,128]{4,3,2,1,0:T(8,128)S(1)}, f32[1,9,4,128,128]{4,3,2,1,0:T(8,128)}, u32[]{:S(2)}) copy-start(f32[1,9,4,128,128]{4,3,2,1,0:T(8,128)} %refs_0_.5) | copy-start | bytes 7077892
  14.1 6.0 %collective-permute-start.5 = (f32[8,32,128]{2,1,0:T(8,128)S(1)}, f32[8,32,128]{2,1,0:T(8,128)S(1)}, u32[]{:S(2)}, u32[]{:S(2)}) collective-permute-start(f32[8,32,128]{2,1,0:T(8,128)S(1)} %shard_map.67.refs_0_), channel_id=1, source_target_pairs={{0,1},{1,0},{2,3},{3,2},{4,5},{5,4},{6,7},{7,6},{8,9},{9,8},{10,11... | collective-permute-start | bytes 393224 | tf_op jit(solution)/shard_map/ppermute | solution.py:388
  14.9 12.8 %collective-permute-start.9 = (f32[14,32,128]{2,1,0:T(8,128)S(1)}, f32[14,32,128]{2,1,0:T(8,128)S(1)}, u32[]{:S(2)}, u32[]{:S(2)}) collective-permute-start(f32[14,32,128]{2,1,0:T(8,128)S(1)} %shard_map.72.refs_1_), channel_id=1, source_target_pairs={{0,2},{1,3},{2,0},{3,1},{4,6},{5,7},{6,4},{7,5},{8,10},{9,11},{10,... | collective-permute-start | bytes 688136 | tf_op jit(solution)/shard_map/ppermute | solution.py:384
  17.0 10.7 %collective-permute-start.8 = (f32[14,32,128]{2,1,0:T(8,128)S(1)}, f32[14,32,128]{2,1,0:T(8,128)S(1)}, u32[]{:S(2)}, u32[]{:S(2)}) collective-permute-start(f32[14,32,128]{2,1,0:T(8,128)S(1)} %shard_map.72.refs_1_), channel_id=1, source_target_pairs={{0,1},{1,0},{2,3},{3,2},{4,5},{5,4},{6,7},{7,6},{8,9},{9,8},{10,11... | collective-permute-start | bytes 688136 | tf_op jit(solution)/shard_map/ppermute | solution.py:383
  22.9 13.6 %collective-permute-start.6 = (f32[9,80,128]{2,1,0:T(8,128)S(1)}, f32[9,80,128]{2,1,0:T(8,128)S(1)}, u32[]{:S(2)}, u32[]{:S(2)}) collective-permute-start(f32[9,80,128]{2,1,0:T(8,128)S(1)} %get-tuple-element.81), channel_id=1, source_target_pairs={{4,8},{12,16},{20,24},{8,4},{16,12},{24,20},{5,9},{13,17},{21,25},... | collective-permute-start | bytes 1105928 | tf_op jit(solution)/shard_map/ppermute | solution.py:421
  26.6 9.8 %collective-permute-start.7 = (f32[9,80,128]{2,1,0:T(8,128)S(1)}, f32[9,80,128]{2,1,0:T(8,128)S(1)}, u32[]{:S(2)}, u32[]{:S(2)}) collective-permute-start(f32[9,80,128]{2,1,0:T(8,128)S(1)} %get-tuple-element.82), channel_id=1, source_target_pairs={{0,4},{8,12},{16,20},{24,28},{4,0},{12,8},{20,16},{28,24},{1,5},{9... | collective-permute-start | bytes 1105928 | tf_op jit(solution)/shard_map/ppermute | solution.py:421
  27.7 7.0 %collective-permute-start.10 = (f32[14,32,128]{2,1,0:T(8,128)S(1)}, f32[14,32,128]{2,1,0:T(8,128)S(1)}, u32[]{:S(2)}, u32[]{:S(2)}) collective-permute-start(f32[14,32,128]{2,1,0:T(8,128)S(1)} %shard_map.73), channel_id=1, source_target_pairs={{0,1},{1,0},{2,3},{3,2},{4,5},{5,4},{6,7},{7,6},{8,9},{9,8},{10,11... | collective-permute-start | bytes 688136 | tf_op jit(solution)/shard_map/ppermute | solution.py:388
  29.9 4.8 %collective-permute-start.11 = (f32[9,48,128]{2,1,0:T(8,128)S(1)}, f32[9,48,128]{2,1,0:T(8,128)S(1)}, u32[]{:S(2)}, u32[]{:S(2)}) collective-permute-start(f32[9,48,128]{2,1,0:T(8,128)S(1)} %get-tuple-element.84), channel_id=1, source_target_pairs={{0,4},{8,12},{16,20},{24,28},{4,0},{12,8},{20,16},{28,24},{1,5},{9... | collective-permute-start | bytes 663560 | tf_op jit(solution)/shard_map/ppermute | solution.py:421
  31.2 12.0 %collective-permute-start.13 = (f32[9,48,128]{2,1,0:T(8,128)S(1)}, f32[9,48,128]{2,1,0:T(8,128)S(1)}, u32[]{:S(2)}, u32[]{:S(2)}) collective-permute-start(f32[9,48,128]{2,1,0:T(8,128)S(1)} %get-tuple-element.90), channel_id=1, source_target_pairs={{4,8},{12,16},{20,24},{8,4},{16,12},{24,20},{5,9},{13,17},{21,25},... | collective-permute-start | bytes 663560 | tf_op jit(solution)/shard_map/ppermute | solution.py:421
  34.8 2.9 %collective-permute-start.12 = (f32[6,128,128]{2,1,0:T(8,128)S(1)}, f32[6,128,128]{2,1,0:T(8,128)S(1)}, u32[]{:S(2)}, u32[]{:S(2)}) collective-permute-start(f32[6,128,128]{2,1,0:T(8,128)S(1)} %get-tuple-element.88), channel_id=1, source_target_pairs={{0,4},{8,12},{16,20},{24,28},{4,0},{12,8},{20,16},{28,24},{1,5},{9... | collective-permute-start | bytes 1179656 | tf_op jit(solution)/shard_map/ppermute | solution.py:528
  39.0 12.9 %collective-permute-start.14 = (f32[9,72,128]{2,1,0:T(8,128)S(1)}, f32[9,72,128]{2,1,0:T(8,128)S(1)}, u32[]{:S(2)}, u32[]{:S(2)}) collective-permute-start(f32[9,72,128]{2,1,0:T(8,128)S(1)} %get-tuple-element.100), channel_id=1, source_target_pairs={{4,8},{12,16},{20,24},{8,4},{16,12},{24,20},{5,9},{13,17},{21,25},... | collective-permute-start | bytes 995336 | tf_op jit(solution)/shard_map/ppermute | solution.py:421
  43.1 8.7 %collective-permute-start.15 = (f32[9,72,128]{2,1,0:T(8,128)S(1)}, f32[9,72,128]{2,1,0:T(8,128)S(1)}, u32[]{:S(2)}, u32[]{:S(2)}) collective-permute-start(f32[9,72,128]{2,1,0:T(8,128)S(1)} %get-tuple-element.101), channel_id=1, source_target_pairs={{0,4},{8,12},{16,20},{24,28},{4,0},{12,8},{20,16},{28,24},{1,5},{9... | collective-permute-start | bytes 995336 | tf_op jit(solution)/shard_map/ppermute | solution.py:421
  44.3 13.0 %collective-permute-start.16 = (f32[9,56,128]{2,1,0:T(8,128)S(1)}, f32[9,56,128]{2,1,0:T(8,128)S(1)}, u32[]{:S(2)}, u32[]{:S(2)}) collective-permute-start(f32[9,56,128]{2,1,0:T(8,128)S(1)} %get-tuple-element.103), channel_id=1, source_target_pairs={{4,8},{12,16},{20,24},{8,4},{16,12},{24,20},{5,9},{13,17},{21,25},... | collective-permute-start | bytes 774152 | tf_op jit(solution)/shard_map/ppermute | solution.py:421
  47.0 10.3 %collective-permute-start.17 = (f32[9,56,128]{2,1,0:T(8,128)S(1)}, f32[9,56,128]{2,1,0:T(8,128)S(1)}, u32[]{:S(2)}, u32[]{:S(2)}) collective-permute-start(f32[9,56,128]{2,1,0:T(8,128)S(1)} %get-tuple-element.104), channel_id=1, source_target_pairs={{0,4},{8,12},{16,20},{24,28},{4,0},{12,8},{20,16},{28,24},{1,5},{9... | collective-permute-start | bytes 774152 | tf_op jit(solution)/shard_map/ppermute | solution.py:421
  53.1 11.5 %collective-permute-start.18 = (f32[9,64,128]{2,1,0:T(8,128)S(1)}, f32[9,64,128]{2,1,0:T(8,128)S(1)}, u32[]{:S(2)}, u32[]{:S(2)}) collective-permute-start(f32[9,64,128]{2,1,0:T(8,128)S(1)} %get-tuple-element.111), channel_id=1, source_target_pairs={{4,8},{12,16},{20,24},{8,4},{16,12},{24,20},{5,9},{13,17},{21,25},... | collective-permute-start | bytes 884744 | tf_op jit(solution)/shard_map/ppermute | solution.py:421
  57.2 7.5 %collective-permute-start.19 = (f32[9,64,128]{2,1,0:T(8,128)S(1)}, f32[9,64,128]{2,1,0:T(8,128)S(1)}, u32[]{:S(2)}, u32[]{:S(2)}) collective-permute-start(f32[9,64,128]{2,1,0:T(8,128)S(1)} %get-tuple-element.112), channel_id=1, source_target_pairs={{0,4},{8,12},{16,20},{24,28},{4,0},{12,8},{20,16},{28,24},{1,5},{9... | collective-permute-start | bytes 884744 | tf_op jit(solution)/shard_map/ppermute | solution.py:421
  58.5 12.5 %collective-permute-start.20 = (f32[9,64,128]{2,1,0:T(8,128)S(1)}, f32[9,64,128]{2,1,0:T(8,128)S(1)}, u32[]{:S(2)}, u32[]{:S(2)}) collective-permute-start(f32[9,64,128]{2,1,0:T(8,128)S(1)} %get-tuple-element.114), channel_id=1, source_target_pairs={{4,8},{12,16},{20,24},{8,4},{16,12},{24,20},{5,9},{13,17},{21,25},... | collective-permute-start | bytes 884744 | tf_op jit(solution)/shard_map/ppermute | solution.py:421
  62.1 8.9 %collective-permute-start.21 = (f32[9,64,128]{2,1,0:T(8,128)S(1)}, f32[9,64,128]{2,1,0:T(8,128)S(1)}, u32[]{:S(2)}, u32[]{:S(2)}) collective-permute-start(f32[9,64,128]{2,1,0:T(8,128)S(1)} %get-tuple-element.115), channel_id=1, source_target_pairs={{0,4},{8,12},{16,20},{24,28},{4,0},{12,8},{20,16},{28,24},{1,5},{9... | collective-permute-start | bytes 884744 | tf_op jit(solution)/shard_map/ppermute | solution.py:421
  65.8 9.8 %collective-permute-start.22 = (f32[5,56,128]{2,1,0:T(8,128)S(1)}, f32[5,56,128]{2,1,0:T(8,128)S(1)}, u32[]{:S(2)}, u32[]{:S(2)}) collective-permute-start(f32[5,56,128]{2,1,0:T(8,128)S(1)} %get-tuple-element.122), channel_id=1, source_target_pairs={{4,8},{12,16},{20,24},{8,4},{16,12},{24,20},{5,9},{13,17},{21,25},... | collective-permute-start | bytes 430088 | tf_op jit(solution)/shard_map/ppermute | solution.py:421
  67.7 7.9 %collective-permute-start.23 = (f32[5,56,128]{2,1,0:T(8,128)S(1)}, f32[5,56,128]{2,1,0:T(8,128)S(1)}, u32[]{:S(2)}, u32[]{:S(2)}) collective-permute-start(f32[5,56,128]{2,1,0:T(8,128)S(1)} %get-tuple-element.123), channel_id=1, source_target_pairs={{0,4},{8,12},{16,20},{24,28},{4,0},{12,8},{20,16},{28,24},{1,5},{9... | collective-permute-start | bytes 430088 | tf_op jit(solution)/shard_map/ppermute | solution.py:421
  72.2 7.8 %collective-permute-start.24 = (f32[5,72,128]{2,1,0:T(8,128)S(1)}, f32[5,72,128]{2,1,0:T(8,128)S(1)}, u32[]{:S(2)}, u32[]{:S(2)}) collective-permute-start(f32[5,72,128]{2,1,0:T(8,128)S(1)} %get-tuple-element.125), channel_id=1, source_target_pairs={{4,8},{12,16},{20,24},{8,4},{16,12},{24,20},{5,9},{13,17},{21,25},... | collective-permute-start | bytes 552968 | tf_op jit(solution)/shard_map/ppermute | solution.py:421
  75.5 4.5 %collective-permute-start.25 = (f32[5,72,128]{2,1,0:T(8,128)S(1)}, f32[5,72,128]{2,1,0:T(8,128)S(1)}, u32[]{:S(2)}, u32[]{:S(2)}) collective-permute-start(f32[5,72,128]{2,1,0:T(8,128)S(1)} %get-tuple-element.126), channel_id=1, source_target_pairs={{0,4},{8,12},{16,20},{24,28},{4,0},{12,8},{20,16},{28,24},{1,5},{9... | collective-permute-start | bytes 552968 | tf_op jit(solution)/shard_map/ppermute | solution.py:421
